TPU v7x, 32 devices: a whole 2x2x4 slice. The times are simulated.
32 devices in a mesh: groups: 1, expert: 16 (over z, y, x), dp: 2 (over core).
Axes of the slice: x: 2, y: 2, z: 4, core: 2. Of those that a mesh axis runs over, the one named last changes fastest.
Arguments:
- tokens: bfloat16 [4096, 2048], P(('groups', 'expert', 'dp')), may hold values from -6 to 6
- routes: int32 [4096, 8], P(('groups', 'expert', 'dp')), may hold values from 0 to 15, all different within a row; in each aligned block of 128 rows (0 to 127, 128 to 255, ...) at most 72 rows name the same one
- route_logits: float32 [4096, 8], P(('groups', 'expert', 'dp')), may hold values from -4 to 4
- cotangent: bfloat16 [4096, 2048], P(('groups', 'expert', 'dp')), may hold values from -6 to 6
- gate_weight: bfloat16 [16, 2048, 768], P('expert', 'dp'), may hold values from -0.125 to 0.125
- up_weight: bfloat16 [16, 2048, 768], P('expert', 'dp'), may hold values from -0.125 to 0.125
- down_weight: bfloat16 [16, 2048, 768], P('expert', 'dp'), may hold values from -0.21875 to 0.21875
Outputs:
- mixed: bfloat16 [4096, 2048], P(('groups', 'expert', 'dp'))
- grad_down: bfloat16 [16, 2048, 768], P(('groups', 'expert'), 'dp')
Inputs may be any that keep to these rules, and one draw needn't show every extreme that they name: `routes`: each token names 8 different experts. Within each device's 128 rows (aligned blocks of rows) no expert is named by more than 72 rows, and in some blocks some expert is named by exactly 72. Every expert is named somewhere.
All inputs are finite; a program needn't handle non-finite values.
Results may differ from a plain program's by a relative error of at most 0.0058.
Values may be sent and summed in bfloat16 or wider, within the bound.
No kernel may reach another device: no remote copies, remote signals or barrier semaphores. Data moves between devices by JAX's collectives and lax.ppermute only.
A program may use at most 128 MiB of HBM per device.

v0:
```python
import jax
import jax.numpy as jnp
from jax import lax
from jax.sharding import PartitionSpec as P


def shards(tokens, routes, route_logits, cotangent, gate_weight, up_weight, down_weight):
    tok_rows, top_count = routes.shape
    experts = lax.axis_size("expert")
    per_expert = tok_rows * top_count // experts
    slot_count = min(tok_rows, per_expert + max(2, per_expert // 8))
    model_width = tokens.shape[1]
    out_cols = cotangent.shape[1]
    pair_count = tok_rows * top_count
    gate_full, up_full, down_full = (
        lax.all_gather(gate_weight, "dp", axis=1, tiled=True),
        lax.all_gather(up_weight, "dp", axis=1, tiled=True),
        lax.all_gather(down_weight, "dp", axis=1, tiled=True),
    )
    gate_mat = gate_full[0]
    up_mat = up_full[0]
    down_mat = down_full[0]
    exp_logits = jnp.exp(route_logits)
    route_weight = exp_logits / jnp.sum(exp_logits, axis=1, keepdims=True)
    flat_routes = routes.reshape(-1)
    onehot = (flat_routes[:, None] == jnp.arange(experts, dtype=jnp.int32)[None, :]).astype(
        jnp.int32
    )
    earlier = jnp.cumsum(onehot, axis=0) - onehot
    position = jnp.sum(earlier * onehot, axis=1)
    slot_index = flat_routes * slot_count + position
    source = jnp.full((experts * slot_count,), pair_count, jnp.int32)
    source = source.at[slot_index].set(jnp.arange(pair_count, dtype=jnp.int32))
    padded_tokens = jnp.concatenate([tokens, jnp.zeros((1, model_width), tokens.dtype)], axis=0)
    send_rows = padded_tokens[source // top_count].reshape(experts, slot_count, model_width)
    scaled = (route_weight[:, :, None] * cotangent[:, None, :].astype(jnp.float32)).astype(
        jnp.bfloat16
    )
    padded_scaled = jnp.concatenate(
        [scaled.reshape(pair_count, out_cols), jnp.zeros((1, out_cols), jnp.bfloat16)], axis=0
    )
    send_grads = padded_scaled[source].reshape(experts, slot_count, out_cols)
    rows_in = lax.all_to_all(send_rows, "expert", split_axis=0, concat_axis=0, tiled=True)
    grads_in = lax.all_to_all(send_grads, "expert", split_axis=0, concat_axis=0, tiled=True)
    count_src = rows_in.shape[0]
    slot_span = rows_in.shape[1]
    flat_rows = rows_in.reshape(count_src * slot_span, model_width)
    gate_act = jnp.dot(flat_rows, gate_mat, preferred_element_type=jnp.float32)
    up_act = jnp.dot(flat_rows, up_mat, preferred_element_type=jnp.float32)
    hidden = (jax.nn.silu(gate_act) * up_act).astype(jnp.bfloat16)
    outputs = lax.dot_general(
        hidden, down_mat, (((1,), (1,)), ((), ())), preferred_element_type=jnp.float32
    ).astype(jnp.bfloat16)
    returned = lax.all_to_all(
        outputs.reshape(count_src, slot_span, out_cols),
        "expert",
        split_axis=0,
        concat_axis=0,
        tiled=True,
    )
    returned, hidden_all, grads_all = (
        returned,
        hidden.reshape(count_src, slot_span, hidden.shape[1]),
        grads_in,
    )
    back_flat = returned.reshape(experts * slot_count, out_cols)
    picked = back_flat[slot_index].reshape(tok_rows, top_count, out_cols)
    mixed_out = jnp.sum(picked.astype(jnp.float32) * route_weight[:, :, None], axis=1).astype(
        jnp.bfloat16
    )
    hidden_rows = hidden_all.reshape(-1, hidden_all.shape[2])
    grad_rows = grads_all.reshape(-1, out_cols)
    grad = lax.psum_scatter(
        lax.dot_general(
            grad_rows, hidden_rows, (((0,), (0,)), ((), ())), preferred_element_type=jnp.float32
        ),
        "dp",
        scatter_dimension=0,
        tiled=True,
    )
    return (mixed_out, grad[None].astype(jnp.bfloat16))


def solution(mesh):
    placed = (
        P(("groups", "expert", "dp"), None),
        P(("groups", "expert", "dp"), None),
        P(("groups", "expert", "dp"), None),
        P(("groups", "expert", "dp"), None),
        P("expert", "dp", None),
        P("expert", "dp", None),
        P("expert", "dp", None),
    )
    return jax.shard_map(
        shards,
        mesh=mesh,
        in_specs=placed,
        out_specs=(P(("groups", "expert", "dp"), None), P(("groups", "expert"), "dp", None)),
        check_vma=False,
    )
```

profile of v0, /device:TPU:9, one launch (start us, length us, event | category | flops | bytes accessed | tf_op | source)
XLA Modules:
  0.0 398.1 jit_solution(164110659538798952)
XLA Ops:
  7.2 0.8 copy.13
  8.0 0.1 eq.29
  8.0 0.1 eq.25
  8.1 0.7 broadcast_multiply_fusion
  8.8 4.5 %reduce-window.6 = s32[16,8,128]{2,1,0:T(8,128)S(1)} reduce-window(s32[16,8,128]{2,1,0:T(8,128)S(1)} %fusion.10, s32[]{:T(128)} %constant.30.clone.1), window={size=1x1x128 pad=0_0x0_0x127_0}, to_apply=%region_0.0 | reduce-window | flops 2080768 | bytes 131076 | tf_op jit(solution)/shard_map/reduce-window
  13.4 0.1 slice.14
  13.4 0.1 copy.15
  13.6 0.1 copy.16
  13.7 0.1 broadcast_add_fusion
  13.8 0.1 copy.12
  13.9 0.1 mul.54
  14.0 4.3 %scatter_custom_fusion = s32[1152]{0:T(1024)S(1)} fusion(s32[1024]{0:T(1024)S(1)} %bitcast.55, s32[1024]{0:T(1024)S(1)} %iota.11, s32[]{:T(128)} %constant.14.clone.1), kind=kCustom, calls=%fused_computation.36 | custom fusion | bytes 4612 | tf_op jit(solution)/shard_map/scatter | solution.py:33
  18.4 1.1 concatenate.6
  19.5 5.9 %gather_fusion = bf16[1152,2048]{1,0:T(8,128)(2,1)} fusion(bf16[129,2048]{1,0:T(8,128)(2,1)S(1)} %concatenate.6, s32[2048]{0:T(1024)S(1)} %get-tuple-element.5), kind=kCustom, calls=%fused_computation | custom fusion | bytes 9441792 | tf_op jit(solution)/shard_map/gather | solution.py:35
  25.4 0.0 copy-start.1
  25.4 0.0 copy-start
  25.4 6.8 %all-to-all-start = ((bf16[16,72,2048]{2,1,0:T(8,128)(2,1)}), bf16[16,72,2048]{2,1,0:T(8,128)(2,1)}, u32[]{:S(2)}, u32[]{:S(2)}) async-start(bf16[16,72,2048]{2,1,0:T(8,128)(2,1)} %bitcast.50), calls=%async_computation | async-start | bytes 9437184 | tf_op jit(solution)/shard_map/all_to_all | solution.py:43
  32.2 0.0 copy-done.1
  32.2 0.1 copy.17
  32.3 0.1 mul.60
  32.4 0.0 copy-done
  32.4 0.1 convert_element_type.43
  32.5 0.9 fusion.1
  33.4 2.3 concatenate.7
  35.7 13.4 %gather_fusion.2 = bf16[1152,2048]{1,0:T(8,128)(2,1)} fusion(bf16[1025,2048]{1,0:T(8,128)(2,1)} %concatenate.7, s32[2048]{0:T(1024)S(1)} %get-tuple-element.4), kind=kCustom, calls=%fused_computation.2 | custom fusion | bytes 9441792 | tf_op jit(solution)/shard_map/gather | solution.py:42
  49.1 84.5 %all-to-all-done = bf16[16,72,2048]{2,1,0:T(8,128)(2,1)} async-done(((bf16[16,72,2048]{2,1,0:T(8,128)(2,1)}), bf16[16,72,2048]{2,1,0:T(8,128)(2,1)}, u32[]{:S(2)}, u32[]{:S(2)}) %all-to-all-start) | async-done | bytes 4718624 | tf_op jit(solution)/shard_map/all_to_all | solution.py:43
  133.6 9.4 %all-to-all-start.2 = ((bf16[16,72,2048]{2,1,0:T(8,128)(2,1)}), bf16[16,72,2048]{2,1,0:T(8,128)(2,1)}, u32[]{:S(2)}, u32[]{:S(2)}) async-start(bf16[16,72,2048]{2,1,0:T(8,128)(2,1)} %bitcast.49), calls=%async_computation.2 | async-start | bytes 9437184 | tf_op jit(solution)/shard_map/all_to_all | solution.py:44
  143.1 0.0 all-gather.4.cloned.1.call-start
  143.1 0.7 all-gather.4.cloned.1.call-update
  143.8 0.0 all-gather.6.cloned.1.call-start
  143.8 0.7 all-gather.6.cloned.1.call-update
  144.5 0.0 all-gather.8.cloned.1.call-start
  144.6 0.7 all-gather.8.cloned.1.call-update
  145.3 0.2 reduce-scatter.2.cloned.1.call-start
  145.5 15.0 %all-gather.4.cloned.1.call-done = bf16[1,2048,768]{2,1,0:T(8,128)(2,1)} async-done(((bf16[1,1024,768]{2,1,0:T(8,128)(2,1)}), bf16[1,2048,768]{2,1,0:T(8,128)(2,1)}) %all-gather.4.cloned.1.call-update) | async-done | bytes 3145744 | tf_op jit(solution)/shard_map/all_gather | solution.py:16
  160.5 8.9 %fusion.5 = f32[1152,768]{1,0:T(8,128)} fusion(bf16[1152,2048]{1,0:T(8,128)(2,1)} %bitcast.5, bf16[1,2048,768]{2,1,0:T(8,128)(2,1)} %all-gather.4.cloned.1.call-done), kind=kOutput, calls=%fused_computation.13 | convolution fusion | flops 3623878656 | bytes 11403264 | tf_op jit(solution)/shard_map/dot_general | solution.py:48
  169.4 6.0 %all-gather.6.cloned.1.call-done = bf16[1,2048,768]{2,1,0:T(8,128)(2,1)} async-done(((bf16[1,1024,768]{2,1,0:T(8,128)(2,1)}), bf16[1,2048,768]{2,1,0:T(8,128)(2,1)}) %all-gather.6.cloned.1.call-update) | async-done | bytes 3145744 | tf_op jit(solution)/shard_map/all_gather | solution.py:17
  175.4 8.5 %fusion.2 = bf16[1152,768]{1,0:T(8,128)(2,1)S(1)} fusion(bf16[1152,2048]{1,0:T(8,128)(2,1)} %bitcast.5, f32[1152,768]{1,0:T(8,128)} %fusion.5, bf16[1,2048,768]{2,1,0:T(8,128)(2,1)} %all-gather.6.cloned.1.call-done), kind=kOutput, calls=%fused_computation.10 | convolution fusion | flops 3629187072 | bytes 13172736 | tf_op jit(solution)/shard_map/dot_general | solution.py:49
  183.9 59.9 %all-to-all-done.2 = bf16[16,72,2048]{2,1,0:T(8,128)(2,1)} async-done(((bf16[16,72,2048]{2,1,0:T(8,128)(2,1)}), bf16[16,72,2048]{2,1,0:T(8,128)(2,1)}, u32[]{:S(2)}, u32[]{:S(2)}) %all-to-all-start.2) | async-done | bytes 4718624 | tf_op jit(solution)/shard_map/all_to_all | solution.py:44
  243.7 8.4 %fusion.15 = f32[2048,768]{1,0:T(8,128)} fusion(bf16[1152,2048]{1,0:T(8,128)(2,1)} %bitcast.14, bf16[1152,768]{1,0:T(8,128)(2,1)S(1)} %fusion.2), kind=kOutput, calls=%fused_computation.42 | convolution fusion | flops 3623878656 | bytes 12779520 | tf_op jit(solution)/shard_map/dot_general | solution.py:74
  252.2 0.0 reduce-scatter.2.cloned.1.call-update
  252.2 0.0 all-gather.8.cloned.1.call-done
  252.2 7.4 %convolution_convert_fusion = bf16[1152,2048]{1,0:T(8,128)(2,1)} fusion(bf16[1152,768]{1,0:T(8,128)(2,1)S(1)} %fusion.2, bf16[1,2048,768]{2,1,0:T(8,128)(2,1)} %all-gather.8.cloned.1.call-done), kind=kOutput, calls=%fused_computation.8 | convolution fusion | flops 3626237952 | bytes 9633792 | tf_op jit(solution)/shard_map/dot_general | solution.py:51
  259.6 8.9 %all-to-all-start.1 = ((bf16[16,72,2048]{2,1,0:T(8,128)(2,1)}), bf16[16,72,2048]{2,1,0:T(8,128)(2,1)}, u32[]{:S(2)}, u32[]{:S(2)}) async-start(bf16[16,72,2048]{2,1,0:T(8,128)(2,1)} %bitcast.51), calls=%async_computation.1 | async-start | bytes 9437184 | tf_op jit(solution)/shard_map/all_to_all | solution.py:54
  268.5 100.8 %all-to-all-done.1 = bf16[16,72,2048]{2,1,0:T(8,128)(2,1)} async-done(((bf16[16,72,2048]{2,1,0:T(8,128)(2,1)}), bf16[16,72,2048]{2,1,0:T(8,128)(2,1)}, u32[]{:S(2)}, u32[]{:S(2)}) %all-to-all-start.1) | async-done | bytes 4718624 | tf_op jit(solution)/shard_map/all_to_all | solution.py:54
  369.3 11.8 %gather_fusion.1 = bf16[1024,2048]{1,0:T(8,128)(2,1)} fusion(bf16[1152,2048]{1,0:T(8,128)(2,1)} %bitcast.10, s32[1024]{0:T(1024)S(1)} %broadcast_clamp_fusion), kind=kCustom, calls=%fused_computation.1 | custom fusion | bytes 8392704 | tf_op jit(solution)/shard_map/gather | solution.py:67
  381.0 7.3 %fusion = bf16[128,2048]{1,0:T(8,128)(2,1)} fusion(bf16[1024,2048]{1,0:T(8,128)(2,1)} %gather_fusion.1, f32[128,8]{1,0:T(8,128)S(1)} %copy.17), kind=kLoop, calls=%fused_computation.5 | loop fusion | flops 6029312 | bytes 4722688 | tf_op jit(solution)/shard_map/reduce_sum | solution.py:68
  388.4 3.2 convert_bitcast_fusion
  (12 shorter events, 0.1 us)
Async XLA Ops:
  25.4 6.8 %copy-start.1 = (f32[128,8]{0,1:T(8,128)S(1)}, f32[128,8]{0,1:T(8,128)}, u32[]{:S(2)}) copy-start(f32[128,8]{0,1:T(8,128)} %param.9) | copy-start | bytes 12292
  25.4 7.0 %copy-start = (bf16[128,2048]{1,0:T(8,128)(2,1)S(1)}, bf16[128,2048]{1,0:T(8,128)(2,1)}, u32[]{:S(2)}) copy-start(bf16[128,2048]{1,0:T(8,128)(2,1)} %param.10) | copy-start | bytes 1572868
  25.4 108.3 %all-to-all-start = ((bf16[16,72,2048]{2,1,0:T(8,128)(2,1)}), bf16[16,72,2048]{2,1,0:T(8,128)(2,1)}, u32[]{:S(2)}, u32[]{:S(2)}) async-start(bf16[16,72,2048]{2,1,0:T(8,128)(2,1)} %bitcast.50), calls=%async_computation | async-start | bytes 9437184 | tf_op jit(solution)/shard_map/all_to_all | solution.py:43
  133.6 110.1 %all-to-all-start.2 = ((bf16[16,72,2048]{2,1,0:T(8,128)(2,1)}), bf16[16,72,2048]{2,1,0:T(8,128)(2,1)}, u32[]{:S(2)}, u32[]{:S(2)}) async-start(bf16[16,72,2048]{2,1,0:T(8,128)(2,1)} %bitcast.49), calls=%async_computation.2 | async-start | bytes 9437184 | tf_op jit(solution)/shard_map/all_to_all | solution.py:44
  143.1 17.5 %all-gather.4.cloned.1.call-start = ((), (), s32[]{:S(2)}) async-start(), calls=%async_computation.4 | async-start | bytes 4718592 | tf_op jit(solution)/shard_map/all_gather | solution.py:16
  143.8 31.6 %all-gather.6.cloned.1.call-start = ((), (), s32[]{:S(2)}) async-start(), calls=%async_computation.5 | async-start | bytes 4718592 | tf_op jit(solution)/shard_map/all_gather | solution.py:17
  144.5 107.7 %all-gather.8.cloned.1.call-start = ((), (), s32[]{:S(2)}) async-start(), calls=%async_computation.6 | async-start | bytes 4718592 | tf_op jit(solution)/shard_map/all_gather | solution.py:18
  145.3 243.1 %reduce-scatter.2.cloned.1.call-start = ((), (), s32[]{:S(2)}) async-start(), calls=%async_computation.7 | async-start | bytes 9437184 | tf_op jit(solution)/shard_map/reduce_scatter | solution.py:73
  259.6 109.7 %all-to-all-start.1 = ((bf16[16,72,2048]{2,1,0:T(8,128)(2,1)}), bf16[16,72,2048]{2,1,0:T(8,128)(2,1)}, u32[]{:S(2)}, u32[]{:S(2)}) async-start(bf16[16,72,2048]{2,1,0:T(8,128)(2,1)} %bitcast.51), calls=%async_computation.1 | async-start | bytes 9437184 | tf_op jit(solution)/shard_map/all_to_all | solution.py:54
Sparse Core Ops, SparseCore 0:
  145.4 15.0 all-gather.3
  162.0 13.2 all-gather.5
  176.9 13.2 all-gather.7
  252.3 19.2 reduce-scatter.1
where the time goes:
time: 404 us; the launch traced here: 398 us
  waiting for transfers between devices  268 us (66%)
  local copies, waits for them, and re-layouts  40.4 us (10%)
  matrix products  33.2 us (8%)
  starting transfers between devices  25.4 us (6%)
  other arithmetic  16.9 us (4%)
  between operations  13.9 us (3%)
    all_to_all x1, waiting for transfers between devices, shards(): lax.all_to_all(outputs.reshape(count_src, slot_span, out_cols), 'expert',...  101 us
    all_to_all x1, waiting for transfers between devices, shards(): lax.all_to_all(send_rows, 'expert', split_axis=0, concat_axis=0, tiled=True)  84.5 us
    all_to_all x1, waiting for transfers between devices, shards(): lax.all_to_all(send_grads, 'expert', split_axis=0, concat_axis=0, tiled=T...  59.9 us
    all_gather x1, waiting for transfers between devices, shards(): lax.all_gather(gate_weight, 'dp', axis=1, tiled=True)  15 us
    gather x1, local copies, waits for them, and re-layouts, shards(): send_grads = padded_scaled[source].reshape(experts, slot_count, out_cols)  13.4 us
    gather x1, local copies, waits for them, and re-layouts, shards(): picked = back_flat[slot_index].reshape(tok_rows, top_count, out_cols)  11.8 us
    all_to_all x1, starting transfers between devices, shards(): lax.all_to_all(send_grads, 'expert', split_axis=0, concat_axis=0, tiled=T...  9.42 us
    dot_general x1, matrix products, shards(): gate_act = jnp.dot(flat_rows, gate_mat, preferred_element_type=jnp.float32)  8.89 us
  transfers between devices with their start and end apart: 7, of which 5 were waited for; matrix products, arithmetic and copies ran while one was open for 17% of the time, Pallas kernels for 0%

commit v1 on v0

v1 whole, which is shorter than its diff:
```python
import functools

import jax
import jax.numpy as jnp
from jax import lax
from jax.experimental import pallas as pl
from jax.experimental.pallas import tpu as pltpu
from jax.sharding import PartitionSpec as P

F32 = jnp.float32
BF16 = jnp.bfloat16
VMEM_LIMIT = 48 * 1024 * 1024


def two_levels(experts):
    minor = 1
    while minor * minor * 4 <= experts:
        minor *= 2
    return experts // minor, minor


def column_tile(columns):
    return 512 if columns % 512 == 0 else columns


def select_kernel(peers, count, slots, scaled, pos_ref, weight_ref, *refs):
    sources, outs = refs[:count], refs[count:]
    toks = pos_ref.shape[1]
    slot = lax.broadcasted_iota(jnp.int32, (slots, toks), 0).astype(F32)
    for g in range(count):
        hits = [slot == pos_ref[k * count + g : k * count + g + 1, :] for k in range(peers)]
        onehot = jnp.concatenate([jnp.where(h, 1.0, 0.0) for h in hits], axis=0).astype(BF16)
        rows = jnp.dot(onehot, sources[g][...], preferred_element_type=F32)
        for k in range(peers):
            part = rows[k * slots : (k + 1) * slots]
            if scaled:
                weights = weight_ref[k * count + g : k * count + g + 1, :]
                part = part * jnp.sum(jnp.where(hits[k], weights, 0.0), axis=1, keepdims=True)
            outs[k][g] = part.astype(BF16)


def select(pos, weight, sources, slots, scaled):
    count = len(sources)
    peers = pos.shape[0] // count
    toks, cols = sources[0].shape
    tile = column_tile(cols)
    small = pl.BlockSpec(pos.shape, lambda j: (0, 0))
    return pl.pallas_call(
        functools.partial(select_kernel, peers, count, slots, scaled),
        grid=(cols // tile,),
        in_specs=[small, small] + [pl.BlockSpec((toks, tile), lambda j: (0, j))] * count,
        out_specs=[pl.BlockSpec((count, slots, tile), lambda j: (0, 0, j))] * peers,
        out_shape=[jax.ShapeDtypeStruct((count, slots, cols), BF16)] * peers,
        compiler_params=pltpu.CompilerParams(vmem_limit_bytes=VMEM_LIMIT),
        cost_estimate=pl.CostEstimate(
            flops=2 * peers * count * slots * toks * cols,
            bytes_accessed=2 * count * cols * (toks + peers * slots),
            transcendentals=0,
        ),
    )(pos, weight, *sources)


def combine_kernel(peers, count, extra, pos_ref, weight_ref, *refs):
    rows, extras, outs = refs[:peers], refs[peers : peers + extra], refs[peers + extra :]
    toks = pos_ref.shape[1]
    slots = rows[0].shape[1]
    slot = lax.broadcasted_iota(jnp.int32, (slots, toks), 0).astype(F32)
    across = (((0,), (0,)), ((), ()))
    for g in range(count):
        total = None
        for k in range(peers):
            at = slice(k * count + g, k * count + g + 1)
            spread = jnp.where(slot == pos_ref[at, :], weight_ref[at, :], 0.0)
            high = spread.astype(BF16)
            low = (spread - high.astype(F32)).astype(BF16)
            part = rows[k][g]
            part = lax.dot_general(
                high, part, across, preferred_element_type=F32
            ) + lax.dot_general(low, part, across, preferred_element_type=F32)
            total = part if total is None else total + part
        for e in extras:
            total = total + e[...].astype(F32)
        outs[g][...] = total.astype(BF16)


def combine(pos, weight, rows, extras=()):
    count, slots, cols = rows[0].shape
    peers, toks = len(rows), pos.shape[1]
    tile = column_tile(cols)
    small = pl.BlockSpec(pos.shape, lambda j: (0, 0))
    flat = pl.BlockSpec((toks, tile), lambda j: (0, j))
    return pl.pallas_call(
        functools.partial(combine_kernel, peers, count, len(extras)),
        grid=(cols // tile,),
        in_specs=[small, small]
        + [pl.BlockSpec((count, slots, tile), lambda j: (0, 0, j))] * peers
        + [flat] * len(extras),
        out_specs=[flat] * count,
        out_shape=[jax.ShapeDtypeStruct((toks, cols), BF16)] * count,
        compiler_params=pltpu.CompilerParams(vmem_limit_bytes=VMEM_LIMIT),
        cost_estimate=pl.CostEstimate(
            flops=4 * peers * count * slots * toks * cols,
            bytes_accessed=2 * cols * (count * (toks + peers * slots) + toks * len(extras)),
            transcendentals=0,
        ),
    )(pos, weight, *rows, *extras)


def shards(tokens, routes, route_logits, cotangent, gate_weight, up_weight, down_weight):
    toks, top = routes.shape
    experts = lax.axis_size("expert")
    major, minor = two_levels(experts)
    per_expert = toks * top // experts
    slots = min(toks, per_expert + max(2, per_expert // 8))
    slots = -(-slots // 8) * 8
    here = lax.axis_index("expert")
    core = lax.axis_index("dp")
    plane, place = here // minor, here % minor

    def to_plane(x, shift):
        return lax.ppermute(x, "expert", [(i, (i + shift * minor) % experts) for i in range(experts)])

    def to_peer(x, k):
        return lax.ppermute(x, "expert", [(i, i ^ k) for i in range(experts)])

    def other_core(x):
        return lax.ppermute(x, "dp", [(0, 1), (1, 0)])

    exp_logits = jnp.exp(route_logits)
    route_weight = (exp_logits / jnp.sum(exp_logits, axis=1, keepdims=True)).T
    names = routes.T[:, None, :] == jnp.arange(experts, dtype=jnp.int32)[None, :, None]
    chosen = jnp.sum(names.astype(F32), axis=0)
    dense_weight = jnp.sum(jnp.where(names, route_weight[:, None, :], 0.0), axis=0)
    before = jnp.arange(toks)[:, None] < jnp.arange(toks)[None, :]
    position = jnp.dot(chosen.astype(BF16), before.astype(BF16), preferred_element_type=F32)
    meta = jnp.stack([jnp.where(chosen > 0, position, -1.0), dense_weight])

    metas = [meta] + [to_plane(meta, s) for s in range(1, major)]
    token_rows = [tokens] + [to_plane(tokens, s) for s in range(1, major)]
    cot_rows = [cotangent] + [to_plane(cotangent, s) for s in range(1, major)]

    mine = plane * minor + (place ^ jnp.arange(minor))
    mine = (mine[:, None] == jnp.arange(experts)[None, :]).astype(F32)

    groups = []
    for near in range(major // 2 + 1):
        groups.append(sorted({near, (major - near) % major}))

    def full_of(w):
        w = w[0]
        got = other_core(w)
        return jnp.concatenate([jnp.where(core == 0, w, got), jnp.where(core == 0, got, w)], axis=0)

    gate_mat, up_mat, down_mat = full_of(gate_weight), full_of(up_weight), full_of(down_weight)

    tables, hiddens, grads, returns = [], [], [], []
    for shifts in groups:
        stacked = jnp.stack([metas[s] for s in shifts])
        picked = jnp.sum(stacked[:, :, None] * mine[None, None, :, :, None], axis=3)
        picked = picked.transpose(1, 2, 0, 3).reshape(2, minor * len(shifts), toks)
        pos, weight = picked[0], picked[1]
        tables.append((pos, weight))
        rows = select(pos, weight, [token_rows[s] for s in shifts], slots, False)
        rows = [rows[0]] + [to_peer(rows[k], k) for k in range(1, minor)]
        flat = jnp.concatenate(rows, axis=0).reshape(-1, tokens.shape[1])
        gate_act = jnp.dot(flat, gate_mat, preferred_element_type=F32)
        up_act = jnp.dot(flat, up_mat, preferred_element_type=F32)
        hidden = (jax.nn.silu(gate_act) * up_act).astype(BF16)
        hiddens.append(hidden)
    for shifts, (pos, weight) in zip(groups, tables):
        rows = select(pos, weight, [cot_rows[s] for s in shifts], slots, True)
        rows = [rows[0]] + [to_peer(rows[k], k) for k in range(1, minor)]
        grads.append(jnp.concatenate(rows, axis=0).reshape(-1, cotangent.shape[1]))

    partial = []
    for shifts, (pos, weight), hidden in reversed(list(zip(groups, tables, hiddens))):
        out = lax.dot_general(
            hidden, down_mat, (((1,), (1,)), ((), ())), preferred_element_type=F32
        ).astype(BF16)
        out = out.reshape(minor, len(shifts), slots, out.shape[1])
        rows = [out[0]] + [to_peer(out[k], k) for k in range(1, minor)]
        if shifts != [0]:
            sums = combine(pos, weight, rows)
            partial += [to_plane(x, major - s) for s, x in zip(shifts, sums)]
        else:
            (mixed,) = combine(pos, weight, rows, partial)

    hidden_all = jnp.concatenate(hiddens, axis=0)
    grad_all = jnp.concatenate(grads, axis=0)
    half = grad_all.shape[1] // 2
    over_rows = (((0,), (0,)), ((), ()))

    def grad_of(which):
        side = lax.dynamic_slice_in_dim(grad_all, which * half, half, axis=1)
        return lax.dot_general(side, hidden_all, over_rows, preferred_element_type=F32)

    theirs = other_core(grad_of(1 - core).astype(BF16))
    grad = (grad_of(core) + theirs.astype(F32)).astype(BF16)
    return mixed, grad[None]


def solution(mesh):
    placed = (
        P(("groups", "expert", "dp"), None),
        P(("groups", "expert", "dp"), None),
        P(("groups", "expert", "dp"), None),
        P(("groups", "expert", "dp"), None),
        P("expert", "dp", None),
        P("expert", "dp", None),
        P("expert", "dp", None),
    )
    return jax.shard_map(
        shards,
        mesh=mesh,
        in_specs=placed,
        out_specs=(P(("groups", "expert", "dp"), None), P(("groups", "expert"), "dp", None)),
        check_vma=False,
    )
```

time: 404 us -> 303 us (0.75); the launches traced: 398 us -> 303 us
  waiting for transfers between devices: 268 us -> 193 us
  local copies, waits for them, and re-layouts: 40.4 us -> 6.33 us
  Pallas kernels: 0 us -> 22 us
  starting transfers between devices: 25.4 us -> 46.4 us
  between operations: 13.9 us -> 1.07 us
  matrix products: 33.2 us -> 22.1 us
  other arithmetic: 16.9 us -> 11.8 us
    all_to_all x3 -> x0, waiting for transfers between devices: 245 us -> none  [the longest x1 101 us: shards(): lax.all_to_all(outputs.reshape(count_src, slot_span, out_cols), 'expert',...]
    ppermute x0 -> x43, waiting for transfers between devices: none -> 193 us  [the longest x12 102 us: to_plane(): lax.ppermute(x, 'expert', [(i, (i + shift * minor) % experts) for i in ra...]
    ppermute x0 -> x43, starting transfers between devices: none -> 46.4 us  [the longest x27 21.4 us: to_peer(): return lax.ppermute(x, 'expert', [(i, i ^ k) for i in range(experts)])]
    gather x3 -> x0, local copies, waits for them, and re-layouts: 31.1 us -> none  [the longest x1 13.4 us: shards(): send_grads = padded_scaled[source].reshape(experts, slot_count, out_cols)]
    all_to_all x3 -> x0, starting transfers between devices: 25.1 us -> none  [the longest x1 9.42 us: shards(): lax.all_to_all(send_grads, 'expert', split_axis=0, concat_axis=0, tiled=T...]
    pallas_call x0 -> x9, Pallas kernels: none -> 22 us  [the longest x6 13.1 us: select(): pl.pallas_call(functools.partial(select_kernel, peers, count, slots, scal...]
    all_gather x3 -> x0, waiting for transfers between devices: 21 us -> none  [the longest x1 15 us: shards(): lax.all_gather(gate_weight, 'dp', axis=1, tiled=True)]
    concatenate x0 -> x7, other arithmetic: none -> 8.75 us  [the longest x3 4.14 us: shards(): grads.append(jnp.concatenate(rows, axis=0).reshape(-1, cotangent.shape[1]))]
  transfers between devices with their start and end apart: 7 -> 43, of which waited for: 5 -> 18; matrix products, arithmetic and copies ran while one was open for 17% -> 7% of each run, Pallas kernels for 0% -> 6%
where the time goes in v1:
time: 303 us
  waiting for transfers between devices  193 us (64%)
  starting transfers between devices  46.4 us (15%)
  matrix products  22.1 us (7%)
  Pallas kernels  22 us (7%)
  other arithmetic  11.8 us (4%)
  local copies, waits for them, and re-layouts  6.33 us (2%)
    ppermute x12, waiting for transfers between devices, to_plane(): lax.ppermute(x, 'expert', [(i, (i + shift * minor) % experts) for i in ra...  102 us
    ppermute x27, waiting for transfers between devices, to_peer(): return lax.ppermute(x, 'expert', [(i, i ^ k) for i in range(experts)])  90.7 us
    ppermute x27, starting transfers between devices, to_peer(): return lax.ppermute(x, 'expert', [(i, i ^ k) for i in range(experts)])  21.4 us
    ppermute x12, starting transfers between devices, to_plane(): lax.ppermute(x, 'expert', [(i, (i + shift * minor) % experts) for i in ra...  17.9 us
    pallas_call x6, Pallas kernels, select(): pl.pallas_call(functools.partial(select_kernel, peers, count, slots, scal...  13.1 us
    dot_general x2, matrix products, grad_of(): lax.dot_general(side, hidden_all, over_rows, preferred_element_type=F32)  9.05 us
    pallas_call x3, Pallas kernels, combine(): pl.pallas_call(functools.partial(combine_kernel, peers, count, len(extras...  8.89 us
    ppermute x4, starting transfers between devices, other_core(): return lax.ppermute(x, 'dp', [(0, 1), (1, 0)])  7.16 us
  transfers between devices with their start and end apart: 43, of which 18 were waited for; matrix products, arithmetic and copies ran while one was open for 7% of the time, Pallas kernels for 6%

profile of v1, /device:TPU:9, one launch (start us, length us, event | category | flops | bytes accessed | tf_op | source)
XLA Modules:
  0.0 302.7 jit_solution(4431593162983407898)
XLA Ops:
  2.9 2.3 collective-permute-start.9
  6.5 2.6 shard_map.92
  9.1 1.3 collective-permute-start.30
  11.6 2.4 collective-permute-start.38
  14.2 23.4 %collective-permute-done.18 = f32[2,16,128]{2,1,0:T(8,128)S(1)} collective-permute-done((f32[2,16,128]{2,1,0:T(8,128)S(1)}, f32[2,16,128]{2,1,0:T(8,128)S(1)}, u32[]{:S(2)}, u32[]{:S(2)}) %collective-permute-start.18) | collective-permute-done | bytes 16416 | tf_op jit(solution)/shard_map/ppermute | solution.py:121
  37.6 2.6 shard_map.86
  41.4 2.2 collective-permute-start.2
  43.6 1.5 collective-permute-start.33
  45.1 2.9 collective-permute-done
  48.1 1.5 collective-permute-start.20
  49.6 4.8 %collective-permute-done.2 = bf16[1,72,2048]{2,1,0:T(8,128)(2,1)S(1)} collective-permute-done((bf16[1,72,2048]{2,1,0:T(8,128)(2,1)S(1)}, bf16[1,72,2048]{2,1,0:T(8,128)(2,1)S(1)}, u32[]{:S(2)}, u32[]{:S(2)}) %collective-permute-start.2) | collective-permute-done | bytes 294944 | tf_op jit(solution)/shard_map/ppermute | solution.py:124
  54.4 3.4 %collective-permute-start.10 = (bf16[128,2048]{1,0:T(8,128)(2,1)}, bf16[128,2048]{1,0:T(8,128)(2,1)S(1)}, u32[]{:S(2)}, u32[]{:S(2)}) collective-permute-start(bf16[128,2048]{1,0:T(8,128)(2,1)} %refs_0_.2), channel_id=1, source_target_pairs={{0,16},{2,18},{4,20},{6,22},{8,24},{10,26},{12,28},{14,30},{16,0},... | collective-permute-start | bytes 1572872 | tf_op jit(solution)/shard_map/ppermute | solution.py:121
  57.8 2.0 shard_map.94
  60.2 11.7 %collective-permute-done.34.refs_1_ = bf16[128,2048]{1,0:T(8,128)(2,1)S(1)} collective-permute-done((bf16[128,2048]{1,0:T(8,128)(2,1)}, bf16[128,2048]{1,0:T(8,128)(2,1)S(1)}, u32[]{:S(2)}, u32[]{:S(2)}) %collective-permute-start.34) | collective-permute-done | bytes 524320 | tf_op jit(solution)/shard_map/ppermute | solution.py:121
  72.1 5.6 %collective-permute-done.20.refs_0_ = bf16[128,2048]{1,0:T(8,128)(2,1)S(1)} collective-permute-done((bf16[128,2048]{1,0:T(8,128)(2,1)}, bf16[128,2048]{1,0:T(8,128)(2,1)S(1)}, u32[]{:S(2)}, u32[]{:S(2)}) %collective-permute-start.20) | collective-permute-done | bytes 524320 | tf_op jit(solution)/shard_map/ppermute | solution.py:121
  78.7 2.4 shard_map.93
  81.1 13.2 %collective-permute-done.21.refs_1_ = bf16[128,2048]{1,0:T(8,128)(2,1)S(1)} collective-permute-done((bf16[128,2048]{1,0:T(8,128)(2,1)}, bf16[128,2048]{1,0:T(8,128)(2,1)S(1)}, u32[]{:S(2)}, u32[]{:S(2)}) %collective-permute-start.21) | collective-permute-done | bytes 524320 | tf_op jit(solution)/shard_map/ppermute | solution.py:121
  95.3 15.1 %collective-permute-done.10.refs_0_ = bf16[128,2048]{1,0:T(8,128)(2,1)S(1)} collective-permute-done((bf16[128,2048]{1,0:T(8,128)(2,1)}, bf16[128,2048]{1,0:T(8,128)(2,1)S(1)}, u32[]{:S(2)}, u32[]{:S(2)}) %collective-permute-start.10) | collective-permute-done | bytes 524320 | tf_op jit(solution)/shard_map/ppermute | solution.py:121
  110.7 2.0 shard_map.87
  115.1 1.2 collective-permute-start.12
  117.5 1.3 pad_maximum_fusion.9
  118.8 5.1 %collective-permute-done.11 = bf16[1,72,2048]{2,1,0:T(8,128)(2,1)} collective-permute-done((bf16[1,72,2048]{2,1,0:T(8,128)(2,1)}, bf16[1,72,2048]{2,1,0:T(8,128)(2,1)}, u32[]{:S(2)}, u32[]{:S(2)}) %collective-permute-start.11) | collective-permute-done | bytes 294944 | tf_op jit(solution)/shard_map/ppermute | solution.py:124
  123.9 1.5 collective-permute-start.37
  125.4 2.1 pad_maximum_fusion.7
  127.5 1.5 shard_map.89
  129.0 19.0 %collective-permute-done.12 = bf16[1,72,2048]{2,1,0:T(8,128)(2,1)S(1)} collective-permute-done((bf16[1,72,2048]{2,1,0:T(8,128)(2,1)}, bf16[1,72,2048]{2,1,0:T(8,128)(2,1)S(1)}, u32[]{:S(2)}, u32[]{:S(2)}) %collective-permute-start.12) | collective-permute-done | bytes 294944 | tf_op jit(solution)/shard_map/ppermute | solution.py:124
  148.0 3.8 %collective-permute-start.3 = (bf16[1024,768]{1,0:T(8,128)(2,1)S(1)}, bf16[1024,768]{1,0:T(8,128)(2,1)S(1)}, u32[]{:S(2)}, u32[]{:S(2)}) collective-permute-start(bf16[1024,768]{1,0:T(8,128)(2,1)S(1)} %bitcast.79), channel_id=1, source_target_pairs={{0,1},{1,0},{2,3},{3,2},{4,5},{5,4},{6,7},{7,6},{8,9},{9,8},{10,11... | collective-permute-start | bytes 4718600 | tf_op jit(solution)/shard_map/ppermute | solution.py:127
  152.3 2.2 collective-permute-start.24
  158.1 1.7 pad_maximum_fusion.5
  159.8 6.9 %collective-permute-done.22 = bf16[2,72,2048]{2,1,0:T(8,128)(2,1)S(1)} collective-permute-done((bf16[2,72,2048]{2,1,0:T(8,128)(2,1)S(1)}, bf16[2,72,2048]{2,1,0:T(8,128)(2,1)S(1)}, u32[]{:S(2)}, u32[]{:S(2)}) %collective-permute-start.22) | collective-permute-done | bytes 589856 | tf_op jit(solution)/shard_map/ppermute | solution.py:124
  166.7 1.3 collective-permute-start.5
  168.0 11.3 %collective-permute-done.24 = bf16[2,72,2048]{2,1,0:T(8,128)(2,1)S(1)} collective-permute-done((bf16[2,72,2048]{2,1,0:T(8,128)(2,1)S(1)}, bf16[2,72,2048]{2,1,0:T(8,128)(2,1)S(1)}, u32[]{:S(2)}, u32[]{:S(2)}) %collective-permute-start.24) | collective-permute-done | bytes 589856 | tf_op jit(solution)/shard_map/ppermute | solution.py:124
  186.7 2.0 fusion.14
  188.7 2.1 multiply_convert_fusion
  191.1 2.0 convolution_convert_fusion
  194.3 3.5 %fusion.4 = bf16[1024,768]{1,0:T(8,128)(2,1)} fusion(bf16[1152,2048]{1,0:T(8,128)(2,1)S(1)} %pad_maximum_fusion, s32[]{:T(128)S(6)} %select_n.65, bf16[288,768]{1,0:T(8,128)(2,1)S(1)} %multiply_convert_fusion.1, bf16[576,768]{1,0:T(8,128)(2,1)S(1)} %multiply_convert_fusion, bf16[288,768]{1,0:T(8,128)(2,1)S(1)} %multiply_convert_fusion.2), kind=kOutput, calls=%fused_computation.16 | convolution fusion | flops 1818034176 | bytes 5701636 | tf_op jit(solution)/shard_map/dot_general | solution.py:195
  199.2 1.3 collective-permute-start.25
  203.5 17.0 %collective-permute-done.14.refs_1_ = bf16[1,72,2048]{2,1,0:T(8,128)(2,1)S(1)} collective-permute-done((bf16[1,72,2048]{2,1,0:T(8,128)(2,1)S(1)}, bf16[1,72,2048]{2,1,0:T(8,128)(2,1)S(1)}, u32[]{:S(2)}, u32[]{:S(2)}) %collective-permute-start.14) | collective-permute-done | bytes 294944 | tf_op jit(solution)/shard_map/ppermute | solution.py:124
  223.7 18.1 %collective-permute-done.16.refs_3_ = bf16[1,72,2048]{2,1,0:T(8,128)(2,1)S(1)} collective-permute-done((bf16[1,72,2048]{2,1,0:T(8,128)(2,1)S(1)}, bf16[1,72,2048]{2,1,0:T(8,128)(2,1)S(1)}, u32[]{:S(2)}, u32[]{:S(2)}) %collective-permute-start.16) | collective-permute-done | bytes 294944 | tf_op jit(solution)/shard_map/ppermute | solution.py:124
  243.3 2.0 shard_map.88
  245.3 2.7 collective-permute-start.17
  248.1 3.9 %shard_map.90 = (bf16[128,2048]{1,0:T(8,128)(2,1)}, bf16[128,2048]{1,0:T(8,128)(2,1)}) custom-call(f32[8,128]{1,0:T(8,128)S(1)} %bitcast.70, f32[8,128]{1,0:T(8,128)S(1)} %bitcast.73, bf16[2,72,2048]{2,1,0:T(8,128)(2,1)S(1)} %bitcast.67, bf16[2,72,2048]{2,1,0:T(8,128)(2,1)S(1)} %collective-permute-done.25.refs_1_, ...), custom_call_target="tpu_custom_call" | custom-call | flops 603979776 | bytes 3407872 | tf_op jit(solution)/shard_map/pallas_call | solution.py:92
  251.9 2.9 collective-permute-start.28
  257.2 5.5 %collective-permute-done.8.refs_3_ = bf16[1,72,2048]{2,1,0:T(8,128)(2,1)S(1)} collective-permute-done((bf16[1,72,2048]{2,1,0:T(8,128)(2,1)}, bf16[1,72,2048]{2,1,0:T(8,128)(2,1)S(1)}, u32[]{:S(2)}, u32[]{:S(2)}) %collective-permute-start.8) | collective-permute-done | bytes 294944 | tf_op jit(solution)/shard_map/ppermute | solution.py:124
  262.7 16.9 %collective-permute-done.17.refs_4_ = bf16[128,2048]{1,0:T(8,128)(2,1)S(1)} collective-permute-done((bf16[128,2048]{1,0:T(8,128)(2,1)S(1)}, bf16[128,2048]{1,0:T(8,128)(2,1)S(1)}, u32[]{:S(2)}, u32[]{:S(2)}) %collective-permute-start.17) | collective-permute-done | bytes 524320 | tf_op jit(solution)/shard_map/ppermute | solution.py:121
  279.6 14.6 %collective-permute-done.28.refs_5_ = bf16[128,2048]{1,0:T(8,128)(2,1)S(1)} collective-permute-done((bf16[128,2048]{1,0:T(8,128)(2,1)}, bf16[128,2048]{1,0:T(8,128)(2,1)S(1)}, u32[]{:S(2)}, u32[]{:S(2)}) %collective-permute-start.28) | collective-permute-done | bytes 524320 | tf_op jit(solution)/shard_map/ppermute | solution.py:121
  294.2 3.0 shard_map.91
  297.2 5.5 %fusion.7 = bf16[1,1024,768]{2,1,0:T(8,128)(2,1)} fusion(bf16[1024,768]{1,0:T(8,128)(2,1)} %collective-permute-done.42, bf16[1152,2048]{1,0:T(8,128)(2,1)} %copy-done.6, s32[]{:T(128)S(6)} %select_n.64, bf16[288,768]{1,0:T(8,128)(2,1)S(1)} %copy-done.24, bf16[576,768]{1,0:T(8,128)(2,1)S(1)} %copy-done.22, bf16[288,768]{1,0:T(8,128)(2,1)S(1)} %copy-done.26), kind=kOutput, calls=%fused_computation.17 | convolution fusion | flops 1819607040 | bytes 7274500 | tf_op jit(solution)/shard_map/dot_general | solution.py:195
  (140 shorter events, 36.8 us)
Async XLA Ops:
  2.9 3.5 %collective-permute-start.9 = (f32[2,16,128]{2,1,0:T(8,128)S(1)}, f32[2,16,128]{2,1,0:T(8,128)S(1)}, u32[]{:S(2)}, u32[]{:S(2)}) collective-permute-start(f32[2,16,128]{2,1,0:T(8,128)S(1)} %pad_maximum_fusion.25), channel_id=1, source_target_pairs={{0,16},{2,18},{4,20},{6,22},{8,24},{10,26},{12,28},{14,30},{16,0},... | collective-permute-start | bytes 49160 | tf_op jit(solution)/shard_map/ppermute | solution.py:121
  9.1 32.1 %collective-permute-start.30 = (bf16[1,72,2048]{2,1,0:T(8,128)(2,1)S(1)}, bf16[1,72,2048]{2,1,0:T(8,128)(2,1)S(1)}, u32[]{:S(2)}, u32[]{:S(2)}) collective-permute-start(bf16[1,72,2048]{2,1,0:T(8,128)(2,1)S(1)} %get-tuple-element.43), channel_id=1, source_target_pairs={{0,2},{2,0},{4,6},{6,4},{8,10},{10,8},{12,14},{14,12},{16,18},{18,... | collective-permute-start | bytes 884744 | tf_op jit(solution)/shard_map/ppermute | solution.py:124
  10.4 31.0 %collective-permute-start.31 = (bf16[1,72,2048]{2,1,0:T(8,128)(2,1)S(1)}, bf16[1,72,2048]{2,1,0:T(8,128)(2,1)S(1)}, u32[]{:S(2)}, u32[]{:S(2)}) collective-permute-start(bf16[1,72,2048]{2,1,0:T(8,128)(2,1)S(1)} %get-tuple-element.44), channel_id=1, source_target_pairs={{0,4},{2,6},{4,0},{6,2},{8,12},{10,14},{12,8},{14,10},{16,20},{18,... | collective-permute-start | bytes 884744 | tf_op jit(solution)/shard_map/ppermute | solution.py:124
  11.6 42.8 %collective-permute-start.38 = (bf16[128,2048]{1,0:T(8,128)(2,1)}, bf16[128,2048]{1,0:T(8,128)(2,1)S(1)}, u32[]{:S(2)}, u32[]{:S(2)}) collective-permute-start(bf16[128,2048]{1,0:T(8,128)(2,1)} %refs_0_.3), channel_id=1, source_target_pairs={{0,16},{2,18},{4,20},{6,22},{8,24},{10,26},{12,28},{14,30},{16,0},... | collective-permute-start | bytes 1572872 | tf_op jit(solution)/shard_map/ppermute | solution.py:121
  14.0 29.6 %collective-permute-start.32 = (bf16[1,72,2048]{2,1,0:T(8,128)(2,1)S(1)}, bf16[1,72,2048]{2,1,0:T(8,128)(2,1)S(1)}, u32[]{:S(2)}, u32[]{:S(2)}) collective-permute-start(bf16[1,72,2048]{2,1,0:T(8,128)(2,1)S(1)} %get-tuple-element.45), channel_id=1, source_target_pairs={{0,6},{2,4},{4,2},{6,0},{8,14},{10,12},{12,10},{14,8},{16,22},{18,... | collective-permute-start | bytes 884744 | tf_op jit(solution)/shard_map/ppermute | solution.py:124
  14.2 23.4 %collective-permute-start.18 = (f32[2,16,128]{2,1,0:T(8,128)S(1)}, f32[2,16,128]{2,1,0:T(8,128)S(1)}, u32[]{:S(2)}, u32[]{:S(2)}) collective-permute-start(f32[2,16,128]{2,1,0:T(8,128)S(1)} %pad_maximum_fusion.25), channel_id=1, source_target_pairs={{0,8},{2,10},{4,12},{6,14},{8,16},{10,18},{12,20},{14,22},{16,24},... | collective-permute-start | bytes 49160 | tf_op jit(solution)/shard_map/ppermute | solution.py:121
  37.6 3.3 %collective-permute-start.19 = (f32[2,16,128]{2,1,0:T(8,128)S(1)}, f32[2,16,128]{2,1,0:T(8,128)S(1)}, u32[]{:S(2)}, u32[]{:S(2)}) collective-permute-start(f32[2,16,128]{2,1,0:T(8,128)S(1)} %pad_maximum_fusion.25), channel_id=1, source_target_pairs={{0,24},{2,26},{4,28},{6,30},{8,0},{10,2},{12,4},{14,6},{16,8},{18,... | collective-permute-start | bytes 49160 | tf_op jit(solution)/shard_map/ppermute | solution.py:121
  40.9 7.1 %collective-permute-start = (bf16[1,72,2048]{2,1,0:T(8,128)(2,1)S(1)}, bf16[1,72,2048]{2,1,0:T(8,128)(2,1)S(1)}, u32[]{:S(2)}, u32[]{:S(2)}) collective-permute-start(bf16[1,72,2048]{2,1,0:T(8,128)(2,1)S(1)} %get-tuple-element.29), channel_id=1, source_target_pairs={{0,2},{2,0},{4,6},{6,4},{8,10},{10,8},{12,14},{14,12},{16,18},{18,... | collective-permute-start | bytes 884744 | tf_op jit(solution)/shard_map/ppermute | solution.py:124
  41.2 6.9 %collective-permute-start.1 = (bf16[1,72,2048]{2,1,0:T(8,128)(2,1)S(1)}, bf16[1,72,2048]{2,1,0:T(8,128)(2,1)S(1)}, u32[]{:S(2)}, u32[]{:S(2)}) collective-permute-start(bf16[1,72,2048]{2,1,0:T(8,128)(2,1)S(1)} %get-tuple-element.30), channel_id=1, source_target_pairs={{0,4},{2,6},{4,0},{6,2},{8,12},{10,14},{12,8},{14,10},{16,20},{18,... | collective-permute-start | bytes 884744 | tf_op jit(solution)/shard_map/ppermute | solution.py:124
  41.4 13.0 %collective-permute-start.2 = (bf16[1,72,2048]{2,1,0:T(8,128)(2,1)S(1)}, bf16[1,72,2048]{2,1,0:T(8,128)(2,1)S(1)}, u32[]{:S(2)}, u32[]{:S(2)}) collective-permute-start(bf16[1,72,2048]{2,1,0:T(8,128)(2,1)S(1)} %get-tuple-element.31), channel_id=1, source_target_pairs={{0,6},{2,4},{4,2},{6,0},{8,14},{10,12},{12,10},{14,8},{16,22},{18,... | collective-permute-start | bytes 884744 | tf_op jit(solution)/shard_map/ppermute | solution.py:124
  43.6 70.5 %copy-start.13 = (bf16[1,72,2048]{2,1,0:T(8,128)(2,1)}, bf16[1,72,2048]{2,1,0:T(8,128)(2,1)S(1)}, u32[]{:S(2)}) copy-start(bf16[1,72,2048]{2,1,0:T(8,128)(2,1)S(1)} %collective-permute-done.32) | copy-start | bytes 884740
  43.6 16.2 %collective-permute-start.33 = (bf16[128,2048]{1,0:T(8,128)(2,1)}, bf16[128,2048]{1,0:T(8,128)(2,1)S(1)}, u32[]{:S(2)}, u32[]{:S(2)}) collective-permute-start(bf16[128,2048]{1,0:T(8,128)(2,1)} %refs_0_.3), channel_id=1, source_target_pairs={{0,8},{2,10},{4,12},{6,14},{8,16},{10,18},{12,20},{14,22},{16,24},... | collective-permute-start | bytes 1572872 | tf_op jit(solution)/shard_map/ppermute | solution.py:121
  48.1 23.8 %collective-permute-start.34 = (bf16[128,2048]{1,0:T(8,128)(2,1)}, bf16[128,2048]{1,0:T(8,128)(2,1)S(1)}, u32[]{:S(2)}, u32[]{:S(2)}) collective-permute-start(bf16[128,2048]{1,0:T(8,128)(2,1)} %refs_0_.3), channel_id=1, source_target_pairs={{0,24},{2,26},{4,28},{6,30},{8,0},{10,2},{12,4},{14,6},{16,8},{18,... | collective-permute-start | bytes 1572872 | tf_op jit(solution)/shard_map/ppermute | solution.py:121
  48.1 66.0 %copy-start.15 = (bf16[1,72,2048]{2,1,0:T(8,128)(2,1)}, bf16[1,72,2048]{2,1,0:T(8,128)(2,1)S(1)}, u32[]{:S(2)}) copy-start(bf16[1,72,2048]{2,1,0:T(8,128)(2,1)S(1)} %collective-permute-done.1) | copy-start | bytes 884740
  48.1 29.6 %collective-permute-start.20 = (bf16[128,2048]{1,0:T(8,128)(2,1)}, bf16[128,2048]{1,0:T(8,128)(2,1)S(1)}, u32[]{:S(2)}, u32[]{:S(2)}) collective-permute-start(bf16[128,2048]{1,0:T(8,128)(2,1)} %refs_0_.2), channel_id=1, source_target_pairs={{0,8},{2,10},{4,12},{6,14},{8,16},{10,18},{12,20},{14,22},{16,24},... | collective-permute-start | bytes 1572872 | tf_op jit(solution)/shard_map/ppermute | solution.py:121
  54.4 59.8 %copy-start.17 = (bf16[1,72,2048]{2,1,0:T(8,128)(2,1)}, bf16[1,72,2048]{2,1,0:T(8,128)(2,1)S(1)}, u32[]{:S(2)}) copy-start(bf16[1,72,2048]{2,1,0:T(8,128)(2,1)S(1)} %collective-permute-done.2) | copy-start | bytes 884740
  54.4 39.9 %collective-permute-start.21 = (bf16[128,2048]{1,0:T(8,128)(2,1)}, bf16[128,2048]{1,0:T(8,128)(2,1)S(1)}, u32[]{:S(2)}, u32[]{:S(2)}) collective-permute-start(bf16[128,2048]{1,0:T(8,128)(2,1)} %refs_0_.2), channel_id=1, source_target_pairs={{0,24},{2,26},{4,28},{6,30},{8,0},{10,2},{12,4},{14,6},{16,8},{18,... | collective-permute-start | bytes 1572872 | tf_op jit(solution)/shard_map/ppermute | solution.py:121
  54.4 56.1 %collective-permute-start.10 = (bf16[128,2048]{1,0:T(8,128)(2,1)}, bf16[128,2048]{1,0:T(8,128)(2,1)S(1)}, u32[]{:S(2)}, u32[]{:S(2)}) collective-permute-start(bf16[128,2048]{1,0:T(8,128)(2,1)} %refs_0_.2), channel_id=1, source_target_pairs={{0,16},{2,18},{4,20},{6,22},{8,24},{10,26},{12,28},{14,30},{16,0},... | collective-permute-start | bytes 1572872 | tf_op jit(solution)/shard_map/ppermute | solution.py:121
  59.8 54.3 %collective-permute-start.39 = (bf16[1,72,2048]{2,1,0:T(8,128)(2,1)S(1)}, bf16[1,72,2048]{2,1,0:T(8,128)(2,1)S(1)}, u32[]{:S(2)}, u32[]{:S(2)}) collective-permute-start(bf16[1,72,2048]{2,1,0:T(8,128)(2,1)S(1)} %get-tuple-element.51), channel_id=1, source_target_pairs={{0,2},{2,0},{4,6},{6,4},{8,10},{10,8},{12,14},{14,12},{16,18},{18,... | collective-permute-start | bytes 884744 | tf_op jit(solution)/shard_map/ppermute | solution.py:124
  71.9 43.2 %collective-permute-start.40 = (bf16[1,72,2048]{2,1,0:T(8,128)(2,1)}, bf16[1,72,2048]{2,1,0:T(8,128)(2,1)}, u32[]{:S(2)}, u32[]{:S(2)}) collective-permute-start(bf16[1,72,2048]{2,1,0:T(8,128)(2,1)} %get-tuple-element.52), channel_id=1, source_target_pairs={{0,4},{2,6},{4,0},{6,2},{8,12},{10,14},{12,8},{14,10},{16,20},{18,... | collective-permute-start | bytes 884744 | tf_op jit(solution)/shard_map/ppermute | solution.py:124
  78.5 37.9 %collective-permute-start.41 = (bf16[1,72,2048]{2,1,0:T(8,128)(2,1)S(1)}, bf16[1,72,2048]{2,1,0:T(8,128)(2,1)}, u32[]{:S(2)}, u32[]{:S(2)}) collective-permute-start(bf16[1,72,2048]{2,1,0:T(8,128)(2,1)S(1)} %get-tuple-element.53), channel_id=1, source_target_pairs={{0,6},{2,4},{4,2},{6,0},{8,14},{10,12},{12,10},{14,8},{16,22},{18,... | collective-permute-start | bytes 884744 | tf_op jit(solution)/shard_map/ppermute | solution.py:124
  95.1 57.0 %collective-permute-start.35 = (bf16[2,72,2048]{2,1,0:T(8,128)(2,1)}, bf16[2,72,2048]{2,1,0:T(8,128)(2,1)}, u32[]{:S(2)}, u32[]{:S(2)}) collective-permute-start(bf16[2,72,2048]{2,1,0:T(8,128)(2,1)} %get-tuple-element.47), channel_id=1, source_target_pairs={{0,2},{2,0},{4,6},{6,4},{8,10},{10,8},{12,14},{14,12},{16,18},{18,... | collective-permute-start | bytes 1769480 | tf_op jit(solution)/shard_map/ppermute | solution.py:124
  110.4 41.9 %collective-permute-start.36 = (bf16[2,72,2048]{2,1,0:T(8,128)(2,1)S(1)}, bf16[2,72,2048]{2,1,0:T(8,128)(2,1)}, u32[]{:S(2)}, u32[]{:S(2)}) collective-permute-start(bf16[2,72,2048]{2,1,0:T(8,128)(2,1)S(1)} %get-tuple-element.48), channel_id=1, source_target_pairs={{0,4},{2,6},{4,0},{6,2},{8,12},{10,14},{12,8},{14,10},{16,20},{18,... | collective-permute-start | bytes 1769480 | tf_op jit(solution)/shard_map/ppermute | solution.py:124
  114.8 9.1 %collective-permute-start.11 = (bf16[1,72,2048]{2,1,0:T(8,128)(2,1)}, bf16[1,72,2048]{2,1,0:T(8,128)(2,1)}, u32[]{:S(2)}, u32[]{:S(2)}) collective-permute-start(bf16[1,72,2048]{2,1,0:T(8,128)(2,1)} %get-tuple-element.33), channel_id=1, source_target_pairs={{0,2},{2,0},{4,6},{6,4},{8,10},{10,8},{12,14},{14,12},{16,18},{18,... | collective-permute-start | bytes 884744 | tf_op jit(solution)/shard_map/ppermute | solution.py:124
  115.1 33.0 %collective-permute-start.12 = (bf16[1,72,2048]{2,1,0:T(8,128)(2,1)}, bf16[1,72,2048]{2,1,0:T(8,128)(2,1)S(1)}, u32[]{:S(2)}, u32[]{:S(2)}) collective-permute-start(bf16[1,72,2048]{2,1,0:T(8,128)(2,1)} %copy-done.5), channel_id=1, source_target_pairs={{0,4},{2,6},{4,0},{6,2},{8,12},{10,14},{12,8},{14,10},{16,20},{18,... | collective-permute-start | bytes 884744 | tf_op jit(solution)/shard_map/ppermute | solution.py:124
  116.3 35.5 %collective-permute-start.13 = (bf16[1,72,2048]{2,1,0:T(8,128)(2,1)}, bf16[1,72,2048]{2,1,0:T(8,128)(2,1)S(1)}, u32[]{:S(2)}, u32[]{:S(2)}) collective-permute-start(bf16[1,72,2048]{2,1,0:T(8,128)(2,1)} %copy-done.4), channel_id=1, source_target_pairs={{0,6},{2,4},{4,2},{6,0},{8,14},{10,12},{12,10},{14,8},{16,22},{18,... | collective-permute-start | bytes 884744 | tf_op jit(solution)/shard_map/ppermute | solution.py:124
  123.9 33.0 %collective-permute-start.37 = (bf16[2,72,2048]{2,1,0:T(8,128)(2,1)S(1)}, bf16[2,72,2048]{2,1,0:T(8,128)(2,1)S(1)}, u32[]{:S(2)}, u32[]{:S(2)}) collective-permute-start(bf16[2,72,2048]{2,1,0:T(8,128)(2,1)S(1)} %get-tuple-element.49), channel_id=1, source_target_pairs={{0,6},{2,4},{4,2},{6,0},{8,14},{10,12},{12,10},{14,8},{16,22},{18,... | collective-permute-start | bytes 1769480 | tf_op jit(solution)/shard_map/ppermute | solution.py:124
  148.0 32.6 %collective-permute-start.3 = (bf16[1024,768]{1,0:T(8,128)(2,1)S(1)}, bf16[1024,768]{1,0:T(8,128)(2,1)S(1)}, u32[]{:S(2)}, u32[]{:S(2)}) collective-permute-start(bf16[1024,768]{1,0:T(8,128)(2,1)S(1)} %bitcast.79), channel_id=1, source_target_pairs={{0,1},{1,0},{2,3},{3,2},{4,5},{5,4},{6,7},{7,6},{8,9},{9,8},{10,11... | collective-permute-start | bytes 4718600 | tf_op jit(solution)/shard_map/ppermute | solution.py:127
  151.8 14.9 %collective-permute-start.22 = (bf16[2,72,2048]{2,1,0:T(8,128)(2,1)S(1)}, bf16[2,72,2048]{2,1,0:T(8,128)(2,1)S(1)}, u32[]{:S(2)}, u32[]{:S(2)}) collective-permute-start(bf16[2,72,2048]{2,1,0:T(8,128)(2,1)S(1)} %get-tuple-element.37), channel_id=1, source_target_pairs={{0,2},{2,0},{4,6},{6,4},{8,10},{10,8},{12,14},{14,12},{16,18},{18,... | collective-permute-start | bytes 1769480 | tf_op jit(solution)/shard_map/ppermute | solution.py:124
  152.1 16.0 %collective-permute-start.23 = (bf16[2,72,2048]{2,1,0:T(8,128)(2,1)S(1)}, bf16[2,72,2048]{2,1,0:T(8,128)(2,1)S(1)}, u32[]{:S(2)}, u32[]{:S(2)}) collective-permute-start(bf16[2,72,2048]{2,1,0:T(8,128)(2,1)S(1)} %get-tuple-element.38), channel_id=1, source_target_pairs={{0,4},{2,6},{4,0},{6,2},{8,12},{10,14},{12,8},{14,10},{16,20},{18,... | collective-permute-start | bytes 1769480 | tf_op jit(solution)/shard_map/ppermute | solution.py:124
  152.3 27.0 %collective-permute-start.24 = (bf16[2,72,2048]{2,1,0:T(8,128)(2,1)S(1)}, bf16[2,72,2048]{2,1,0:T(8,128)(2,1)S(1)}, u32[]{:S(2)}, u32[]{:S(2)}) collective-permute-start(bf16[2,72,2048]{2,1,0:T(8,128)(2,1)S(1)} %get-tuple-element.39), channel_id=1, source_target_pairs={{0,6},{2,4},{4,2},{6,0},{8,14},{10,12},{12,10},{14,8},{16,22},{18,... | collective-permute-start | bytes 1769480 | tf_op jit(solution)/shard_map/ppermute | solution.py:124
  157.2 26.9 %collective-permute-start.4 = (bf16[1024,768]{1,0:T(8,128)(2,1)S(1)}, bf16[1024,768]{1,0:T(8,128)(2,1)S(1)}, u32[]{:S(2)}, u32[]{:S(2)}) collective-permute-start(bf16[1024,768]{1,0:T(8,128)(2,1)S(1)} %bitcast.80), channel_id=1, source_target_pairs={{0,1},{1,0},{2,3},{3,2},{4,5},{5,4},{6,7},{7,6},{8,9},{9,8},{10,11... | collective-permute-start | bytes 4718600 | tf_op jit(solution)/shard_map/ppermute | solution.py:127
  166.7 24.1 %collective-permute-start.5 = (bf16[1024,768]{1,0:T(8,128)(2,1)S(1)}, bf16[1024,768]{1,0:T(8,128)(2,1)S(1)}, u32[]{:S(2)}, u32[]{:S(2)}) collective-permute-start(bf16[1024,768]{1,0:T(8,128)(2,1)S(1)} %bitcast.81), channel_id=1, source_target_pairs={{0,1},{1,0},{2,3},{3,2},{4,5},{5,4},{6,7},{7,6},{8,9},{9,8},{10,11... | collective-permute-start | bytes 4718600 | tf_op jit(solution)/shard_map/ppermute | solution.py:127
  197.8 99.4 %collective-permute-start.42 = (bf16[1024,768]{1,0:T(8,128)(2,1)}, bf16[1024,768]{1,0:T(8,128)(2,1)}, u32[]{:S(2)}, u32[]{:S(2)}) collective-permute-start(bf16[1024,768]{1,0:T(8,128)(2,1)} %fusion.4), channel_id=1, source_target_pairs={{0,1},{1,0},{2,3},{3,2},{4,5},{5,4},{6,7},{7,6},{8,9},{9,8},{10,11... | collective-permute-start | bytes 4718600 | tf_op jit(solution)/shard_map/ppermute | solution.py:127
  199.2 43.9 %collective-permute-start.25 = (bf16[2,72,2048]{2,1,0:T(8,128)(2,1)S(1)}, bf16[2,72,2048]{2,1,0:T(8,128)(2,1)S(1)}, u32[]{:S(2)}, u32[]{:S(2)}) collective-permute-start(bf16[2,72,2048]{2,1,0:T(8,128)(2,1)S(1)} %bitcast.88), channel_id=1, source_target_pairs={{0,2},{2,0},{4,6},{6,4},{8,10},{10,8},{12,14},{14,12},{16,18},{18,... | collective-permute-start | bytes 1769480 | tf_op jit(solution)/shard_map/ppermute | solution.py:124
  200.5 44.9 %collective-permute-start.26 = (bf16[2,72,2048]{2,1,0:T(8,128)(2,1)S(1)}, bf16[2,72,2048]{2,1,0:T(8,128)(2,1)S(1)}, u32[]{:S(2)}, u32[]{:S(2)}) collective-permute-start(bf16[2,72,2048]{2,1,0:T(8,128)(2,1)S(1)} %bitcast.87), channel_id=1, source_target_pairs={{0,4},{2,6},{4,0},{6,2},{8,12},{10,14},{12,8},{14,10},{16,20},{18,... | collective-permute-start | bytes 1769480 | tf_op jit(solution)/shard_map/ppermute | solution.py:124
  200.8 19.7 %collective-permute-start.14 = (bf16[1,72,2048]{2,1,0:T(8,128)(2,1)S(1)}, bf16[1,72,2048]{2,1,0:T(8,128)(2,1)S(1)}, u32[]{:S(2)}, u32[]{:S(2)}) collective-permute-start(bf16[1,72,2048]{2,1,0:T(8,128)(2,1)S(1)} %get-tuple-element.70), channel_id=1, source_target_pairs={{0,2},{2,0},{4,6},{6,4},{8,10},{10,8},{12,14},{14,12},{16,18},{18,... | collective-permute-start | bytes 884744 | tf_op jit(solution)/shard_map/ppermute | solution.py:124
  201.8 19.9 %collective-permute-start.15 = (bf16[1,72,2048]{2,1,0:T(8,128)(2,1)S(1)}, bf16[1,72,2048]{2,1,0:T(8,128)(2,1)S(1)}, u32[]{:S(2)}, u32[]{:S(2)}) collective-permute-start(bf16[1,72,2048]{2,1,0:T(8,128)(2,1)S(1)} %get-tuple-element.69), channel_id=1, source_target_pairs={{0,4},{2,6},{4,0},{6,2},{8,12},{10,14},{12,8},{14,10},{16,20},{18,... | collective-permute-start | bytes 884744 | tf_op jit(solution)/shard_map/ppermute | solution.py:124
  220.5 27.5 %collective-permute-start.27 = (bf16[2,72,2048]{2,1,0:T(8,128)(2,1)S(1)}, bf16[2,72,2048]{2,1,0:T(8,128)(2,1)S(1)}, u32[]{:S(2)}, u32[]{:S(2)}) collective-permute-start(bf16[2,72,2048]{2,1,0:T(8,128)(2,1)S(1)} %bitcast.86), channel_id=1, source_target_pairs={{0,6},{2,4},{4,2},{6,0},{8,14},{10,12},{12,10},{14,8},{16,22},{18,... | collective-permute-start | bytes 1769480 | tf_op jit(solution)/shard_map/ppermute | solution.py:124
  221.7 20.1 %collective-permute-start.16 = (bf16[1,72,2048]{2,1,0:T(8,128)(2,1)S(1)}, bf16[1,72,2048]{2,1,0:T(8,128)(2,1)S(1)}, u32[]{:S(2)}, u32[]{:S(2)}) collective-permute-start(bf16[1,72,2048]{2,1,0:T(8,128)(2,1)S(1)} %get-tuple-element.68), channel_id=1, source_target_pairs={{0,6},{2,4},{4,2},{6,0},{8,14},{10,12},{12,10},{14,8},{16,22},{18,... | collective-permute-start | bytes 884744 | tf_op jit(solution)/shard_map/ppermute | solution.py:124
  241.8 13.0 %collective-permute-start.6 = (bf16[1,72,2048]{2,1,0:T(8,128)(2,1)S(1)}, bf16[1,72,2048]{2,1,0:T(8,128)(2,1)S(1)}, u32[]{:S(2)}, u32[]{:S(2)}) collective-permute-start(bf16[1,72,2048]{2,1,0:T(8,128)(2,1)S(1)} %get-tuple-element.74), channel_id=1, source_target_pairs={{0,2},{2,0},{4,6},{6,4},{8,10},{10,8},{12,14},{14,12},{16,18},{18,... | collective-permute-start | bytes 884744 | tf_op jit(solution)/shard_map/ppermute | solution.py:124
  243.0 12.9 %collective-permute-start.7 = (bf16[1,72,2048]{2,1,0:T(8,128)(2,1)S(1)}, bf16[1,72,2048]{2,1,0:T(8,128)(2,1)S(1)}, u32[]{:S(2)}, u32[]{:S(2)}) collective-permute-start(bf16[1,72,2048]{2,1,0:T(8,128)(2,1)S(1)} %get-tuple-element.73), channel_id=1, source_target_pairs={{0,4},{2,6},{4,0},{6,2},{8,12},{10,14},{12,8},{14,10},{16,20},{18,... | collective-permute-start | bytes 884744 | tf_op jit(solution)/shard_map/ppermute | solution.py:124
  245.3 34.3 %collective-permute-start.17 = (bf16[128,2048]{1,0:T(8,128)(2,1)S(1)}, bf16[128,2048]{1,0:T(8,128)(2,1)S(1)}, u32[]{:S(2)}, u32[]{:S(2)}) collective-permute-start(bf16[128,2048]{1,0:T(8,128)(2,1)S(1)} %shard_map.88), channel_id=1, source_target_pairs={{0,16},{2,18},{4,20},{6,22},{8,24},{10,26},{12,28},{14,30},{16,0},... | collective-permute-start | bytes 1572872 | tf_op jit(solution)/shard_map/ppermute | solution.py:121
  251.9 42.3 %collective-permute-start.28 = (bf16[128,2048]{1,0:T(8,128)(2,1)}, bf16[128,2048]{1,0:T(8,128)(2,1)S(1)}, u32[]{:S(2)}, u32[]{:S(2)}) collective-permute-start(bf16[128,2048]{1,0:T(8,128)(2,1)} %get-tuple-element.40), channel_id=1, source_target_pairs={{0,24},{2,26},{4,28},{6,30},{8,0},{10,2},{12,4},{14,6},{16,8},{18,... | collective-permute-start | bytes 1572872 | tf_op jit(solution)/shard_map/ppermute | solution.py:121
  254.8 39.4 %collective-permute-start.29 = (bf16[128,2048]{1,0:T(8,128)(2,1)}, bf16[128,2048]{1,0:T(8,128)(2,1)S(1)}, u32[]{:S(2)}, u32[]{:S(2)}) collective-permute-start(bf16[128,2048]{1,0:T(8,128)(2,1)} %get-tuple-element.41), channel_id=1, source_target_pairs={{0,8},{2,10},{4,12},{6,14},{8,16},{10,18},{12,20},{14,22},{16,24},... | collective-permute-start | bytes 1572872 | tf_op jit(solution)/shard_map/ppermute | solution.py:121
  256.0 6.7 %collective-permute-start.8 = (bf16[1,72,2048]{2,1,0:T(8,128)(2,1)}, bf16[1,72,2048]{2,1,0:T(8,128)(2,1)S(1)}, u32[]{:S(2)}, u32[]{:S(2)}) collective-permute-start(bf16[1,72,2048]{2,1,0:T(8,128)(2,1)} %get-tuple-element.72), channel_id=1, source_target_pairs={{0,6},{2,4},{4,2},{6,0},{8,14},{10,12},{12,10},{14,8},{16,22},{18,... | collective-permute-start | bytes 884744 | tf_op jit(solution)/shard_map/ppermute | solution.py:124
  257.2 40.0 %copy-start.24 = (bf16[288,768]{1,0:T(8,128)(2,1)S(1)}, bf16[288,768]{1,0:T(8,128)(2,1)}, u32[]{:S(2)}) copy-start(bf16[288,768]{1,0:T(8,128)(2,1)} %copy-done.23) | copy-start | bytes 1327108
  257.2 40.0 %copy-start.26 = (bf16[288,768]{1,0:T(8,128)(2,1)S(1)}, bf16[288,768]{1,0:T(8,128)(2,1)}, u32[]{:S(2)}) copy-start(bf16[288,768]{1,0:T(8,128)(2,1)} %copy-done.25) | copy-start | bytes 1327108
  (22 other events, 276.7 us)

commit v2 on v1

v2 whole, which is shorter than its diff:
```python
import functools

import jax
import jax.numpy as jnp
from jax import lax
from jax.experimental import pallas as pl
from jax.experimental.pallas import tpu as pltpu
from jax.sharding import PartitionSpec as P

F32 = jnp.float32
BF16 = jnp.bfloat16
VMEM_LIMIT = 48 * 1024 * 1024
DEPTH = 1


def two_levels(experts):
    minor = 1
    while minor * minor * 4 <= experts:
        minor *= 2
    return experts // minor, minor


def column_tile(columns):
    return 512 if columns % 512 == 0 else columns


def select_kernel(peers, count, slots, scaled, _, pos_ref, weight_ref, *refs):
    sources, outs = refs[:count], refs[count:]
    toks = pos_ref.shape[1]
    slot = lax.broadcasted_iota(jnp.int32, (slots, toks), 0).astype(F32)
    for g in range(count):
        hits = [slot == pos_ref[k * count + g : k * count + g + 1, :] for k in range(peers)]
        onehot = jnp.concatenate([jnp.where(h, 1.0, 0.0) for h in hits], axis=0).astype(BF16)
        rows = jnp.dot(onehot, sources[g][0], preferred_element_type=F32)
        for k in range(peers):
            part = rows[k * slots : (k + 1) * slots]
            if scaled:
                weights = weight_ref[k * count + g : k * count + g + 1, :]
                part = part * jnp.sum(jnp.where(hits[k], weights, 0.0), axis=1, keepdims=True)
            outs[k][g] = part.astype(BF16)


def select(plane, shifts, pos, weight, blocks, slots, scaled):
    count = len(shifts)
    peers = pos.shape[0] // count
    major, toks, cols = blocks.shape
    tile = column_tile(cols)
    small = pl.BlockSpec(pos.shape, lambda j, ref: (0, 0))

    def source(shift):
        return pl.BlockSpec(
            (1, toks, tile), lambda j, ref: (lax.rem(ref[0] + (major - shift), major), 0, j)
        )

    return pl.pallas_call(
        functools.partial(select_kernel, peers, count, slots, scaled),
        grid_spec=pltpu.PrefetchScalarGridSpec(
            num_scalar_prefetch=1,
            grid=(cols // tile,),
            in_specs=[small, small] + [source(shift) for shift in shifts],
            out_specs=[pl.BlockSpec((count, slots, tile), lambda j, ref: (0, 0, j))] * peers,
        ),
        out_shape=[jax.ShapeDtypeStruct((count, slots, cols), BF16)] * peers,
        compiler_params=pltpu.CompilerParams(vmem_limit_bytes=VMEM_LIMIT),
        cost_estimate=pl.CostEstimate(
            flops=2 * peers * count * slots * toks * cols,
            bytes_accessed=2 * count * cols * (toks + peers * slots),
            transcendentals=0,
        ),
    )(plane.reshape(1), pos, weight, *[blocks] * count)


def combine_kernel(peers, _, pos_ref, weight_ref, *refs):
    rows, out = refs[:peers], refs[peers]
    g, count = pl.program_id(0), pl.num_programs(0)
    toks, slots = pos_ref.shape[1], rows[0].shape[1]
    slot = lax.broadcasted_iota(jnp.int32, (slots, toks), 0).astype(F32)
    across = (((0,), (0,)), ((), ()))
    total = None
    for k in range(peers):
        at = pl.ds(k * count + g, 1)
        spread = jnp.where(slot == pos_ref[at, :], weight_ref[at, :], 0.0)
        high = spread.astype(BF16)
        low = (spread - high.astype(F32)).astype(BF16)
        part = rows[k][0]
        part = lax.dot_general(
            high, part, across, preferred_element_type=F32
        ) + lax.dot_general(low, part, across, preferred_element_type=F32)
        total = part if total is None else total + part
    out[0] = total.astype(BF16)


def combine(plane, pos, weight, rows):
    count, slots, cols = rows[0].shape
    peers, toks = len(rows), pos.shape[1]
    small = pl.BlockSpec(pos.shape, lambda g, ref: (0, 0))
    return pl.pallas_call(
        functools.partial(combine_kernel, peers),
        grid_spec=pltpu.PrefetchScalarGridSpec(
            num_scalar_prefetch=1,
            grid=(count,),
            in_specs=[small, small]
            + [pl.BlockSpec((1, slots, cols), lambda g, ref: (g, 0, 0))] * peers,
            out_specs=pl.BlockSpec(
                (1, toks, cols), lambda g, ref: (lax.rem(ref[0] + count - g, count), 0, 0)
            ),
        ),
        out_shape=jax.ShapeDtypeStruct((count, toks, cols), BF16),
        compiler_params=pltpu.CompilerParams(vmem_limit_bytes=VMEM_LIMIT),
        cost_estimate=pl.CostEstimate(
            flops=4 * peers * count * slots * toks * cols,
            bytes_accessed=2 * cols * count * (toks + peers * slots),
            transcendentals=0,
        ),
    )(plane.reshape(1), pos, weight, *rows)


def shards(tokens, routes, route_logits, cotangent, gate_weight, up_weight, down_weight):
    toks, top = routes.shape
    experts = lax.axis_size("expert")
    major, minor = two_levels(experts)
    per_expert = toks * top // experts
    slots = min(toks, per_expert + max(2, per_expert // 8))
    slots = -(-slots // 8) * 8
    here = lax.axis_index("expert")
    core = lax.axis_index("dp")
    plane, place = here // minor, here % minor

    def to_plane(x, shift):
        return lax.ppermute(x, "expert", [(i, (i + shift * minor) % experts) for i in range(experts)])

    def to_peer(x, k):
        return lax.ppermute(x, "expert", [(i, i ^ k) for i in range(experts)])

    def other_core(x):
        return lax.ppermute(x, "dp", [(0, 1), (1, 0)])

    def after(x, earlier):
        return lax.optimization_barrier((x, *earlier))[0] if earlier else x

    exp_logits = jnp.exp(route_logits)
    route_weight = (exp_logits / jnp.sum(exp_logits, axis=1, keepdims=True)).T
    names = routes.T[:, None, :] == jnp.arange(experts, dtype=jnp.int32)[None, :, None]
    chosen = jnp.sum(names.astype(F32), axis=0)
    dense_weight = jnp.sum(jnp.where(names, route_weight[:, None, :], 0.0), axis=0)
    before = jnp.arange(toks)[:, None] < jnp.arange(toks)[None, :]
    position = jnp.dot(chosen.astype(BF16), before.astype(BF16), preferred_element_type=F32)
    meta = jnp.stack([jnp.where(chosen > 0, position, -1.0), dense_weight])

    mine = plane * minor + (place ^ jnp.arange(minor))
    mine = (mine[:, None] == jnp.arange(experts)[None, :]).astype(F32)

    same_place = [[i * minor + j for i in range(major)] for j in range(minor)]

    def spread(x):
        return lax.all_gather(x, "expert", axis=0, axis_index_groups=same_place)

    model_width, out_cols = tokens.shape[1], cotangent.shape[1]
    piece = out_cols // 4
    cot_parts = [
        jnp.concatenate([cotangent[:, h * piece : (h + 1) * piece], cotangent[:, (2 + h) * piece : (3 + h) * piece]], axis=1)
        for h in range(2)
    ]
    token_parts = [tokens[:, : model_width // 2], tokens[:, model_width // 2 :]]
    token_all = [spread(x) for x in token_parts]
    cot_all = [spread(x) for x in cot_parts]

    metas = [meta] + [to_plane(meta, s) for s in range(1, major)]

    def table_of(shifts):
        stacked = jnp.stack([metas[s] for s in shifts])
        picked = jnp.sum(stacked[:, :, None] * mine[None, None, :, :, None], axis=3)
        picked = picked.transpose(1, 2, 0, 3).reshape(2, minor * len(shifts), toks)
        return picked[0], picked[1]

    all_table = table_of(list(range(major)))
    by_peer = [t.reshape(minor, major, toks) for t in all_table]
    own_table = [t[:, 0] for t in by_peer]
    rest_table = [t[:, 1:].reshape(-1, toks) for t in by_peer]
    others = list(range(1, major))

    def full_of(w, *earlier):
        w = w[0]
        got = other_core(after(w, earlier))
        return jnp.concatenate([jnp.where(core == 0, w, got), jnp.where(core == 0, got, w)], axis=0)

    gate_mat, up_mat = full_of(gate_weight, *metas[1:]), full_of(up_weight, *metas[1:])
    down_mat = full_of(down_weight, gate_mat)

    queues = [[] for _ in range(minor)]

    def exchange(rows):
        got = [rows[0]]
        for k in range(1, minor):
            queue = queues[k]
            got.append(to_peer(after(rows[k], queue[-DEPTH:][:1] if len(queue) >= DEPTH else []), k))
            queue.append(got[k])
        return got

    def send_own(x, scaled, *earlier):
        blocks = after(x, earlier)[None]
        here_only = jnp.zeros((), jnp.int32)
        return exchange(select(here_only, [0], *own_table, blocks, slots, scaled))

    def send_rest(blocks, scaled):
        return exchange(select(plane, others, *rest_table, blocks, slots, scaled))

    def joined(parts):
        return jnp.concatenate(parts, axis=0).reshape(-1, parts[0].shape[-1])

    def hidden_of(pieces):
        def against(w):
            total, at = None, 0
            for x in pieces:
                part = jnp.dot(x, w[at : at + x.shape[1]], preferred_element_type=F32)
                total, at = part if total is None else total + part, at + x.shape[1]
            return total

        return (jax.nn.silu(against(gate_mat)) * against(up_mat)).astype(BF16)

    own_rows = joined(send_own(tokens, False))
    own_hidden = hidden_of([own_rows])
    blocks = after(token_all[0], (gate_mat, up_mat, down_mat))
    first = send_rest(blocks, False)
    second = send_rest(after(token_all[1], first[1:]), False)
    rest_rows = [joined(first), joined(second)]
    own_cots = joined(send_own(jnp.concatenate(cot_parts, axis=1), True))
    rest_hidden = hidden_of(rest_rows)

    hidden = jnp.concatenate(
        [own_hidden.reshape(minor, 1, slots, -1), rest_hidden.reshape(minor, major - 1, slots, -1)],
        axis=1,
    ).reshape(minor * major * slots, -1)
    wide = out_cols // 2
    outs = [
        lax.dot_general(
            hidden,
            down_mat[h * wide : (h + 1) * wide],
            (((1,), (1,)), ((), ())),
            preferred_element_type=F32,
        ).astype(BF16).reshape(minor, major, slots, wide)
        for h in range(2)
    ]
    mixed = []
    for h in range(2):
        back = exchange([outs[h][k] for k in range(minor)])
        sums = combine(plane, *all_table, [after(x, [outs[1]]) for x in back])
        mixed.append(
            lax.psum_scatter(sums, "expert", scatter_dimension=0, axis_index_groups=same_place)
        )
    mixed = jnp.concatenate(mixed, axis=1)
    rest_cots = [joined(send_rest(x, True)) for x in cot_all]

    over_rows = (((0,), (0,)), ((), ()))
    done = []
    for h in range(2):
        own_half = own_cots[:, h * 2 * piece : (h + 1) * 2 * piece]

        def grad_of(which):
            def part(rows, hidden):
                side = lax.dynamic_slice_in_dim(rows, which * piece, piece, axis=1)
                return lax.dot_general(side, hidden, over_rows, preferred_element_type=F32)

            return part(own_half, own_hidden) + part(rest_cots[h], rest_hidden)

        theirs = other_core(grad_of(1 - core).astype(BF16))
        done.append((grad_of(core) + theirs.astype(F32)).astype(BF16))
    return mixed, jnp.concatenate(done, axis=0)[None]


def solution(mesh):
    placed = (
        P(("groups", "expert", "dp"), None),
        P(("groups", "expert", "dp"), None),
        P(("groups", "expert", "dp"), None),
        P(("groups", "expert", "dp"), None),
        P("expert", "dp", None),
        P("expert", "dp", None),
        P("expert", "dp", None),
    )
    return jax.shard_map(
        shards,
        mesh=mesh,
        in_specs=placed,
        out_specs=(P(("groups", "expert", "dp"), None), P(("groups", "expert"), "dp", None)),
        check_vma=False,
    )
```

time: 303 us -> 233 us (0.77)
  waiting for transfers between devices: 193 us -> 108 us
  starting transfers between devices: 46.4 us -> 32.1 us
  between operations: 1.07 us -> 14.7 us
  local copies, waits for them, and re-layouts: 6.33 us -> 16.7 us
  Pallas kernels: 22 us -> 14.5 us
  matrix products: 22.1 us -> 28.4 us
  other arithmetic: 11.8 us -> 17.3 us
    ppermute x12 -> x3, waiting for transfers between devices: 102 us -> 1.18 us  [to_plane(): lax.ppermute(x, 'expert', [(i, (i + shift * minor) % experts) for i in ra...]
    ppermute x12 -> x3, starting transfers between devices: 17.9 us -> 3.77 us  [to_plane(): lax.ppermute(x, 'expert', [(i, (i + shift * minor) % experts) for i in ra...]
    all_gather x0 -> x4, waiting for transfers between devices: none -> 12.6 us  [spread(): return lax.all_gather(x, 'expert', axis=0, axis_index_groups=same_place)]
    unnamed x54 -> x68, local copies, waits for them, and re-layouts: 5.11 us -> 14.2 us
    dot_general x11 -> x16, matrix products: 22 us -> 28.2 us  [the longest x8 11.3 us: part(): return lax.dot_general(side, hidden, over_rows, preferred_element_type=F32)]
    pallas_call x6, Pallas kernels: 13.1 us -> 7.13 us  [select(): pl.pallas_call(functools.partial(select_kernel, peers, count, slots, scal...]
    select_n x3 -> x2, other arithmetic: 0.63 us -> 5.44 us  [full_of(): jnp.where(core == 0, w, got)]
    ppermute x27 -> x24, waiting for transfers between devices: 90.7 us -> 93 us  [to_peer(): return lax.ppermute(x, 'expert', [(i, i ^ k) for i in range(experts)])]
  transfers between devices with their start and end apart: 43 -> 38, of which waited for: 18 -> 17; matrix products, arithmetic and copies ran while one was open for 7% -> 19% of each run, Pallas kernels for 6% -> 6%
where the time goes in v2:
time: 233 us; the launch traced here: 231 us
  waiting for transfers between devices  108 us (46%)
  starting transfers between devices  32.1 us (14%)
  matrix products  28.4 us (12%)
  other arithmetic  17.3 us (7%)
  local copies, waits for them, and re-layouts  16.7 us (7%)
  between operations  14.7 us (6%)
  Pallas kernels  14.5 us (6%)
    ppermute x24, waiting for transfers between devices, to_peer(): return lax.ppermute(x, 'expert', [(i, i ^ k) for i in range(experts)])  93 us
    ppermute x24, starting transfers between devices, to_peer(): return lax.ppermute(x, 'expert', [(i, i ^ k) for i in range(experts)])  21.5 us
    unnamed x68, local copies, waits for them, and re-layouts  14.2 us
    all_gather x4, waiting for transfers between devices, spread(): return lax.all_gather(x, 'expert', axis=0, axis_index_groups=same_place)  12.6 us
    dot_general x8, matrix products, part(): return lax.dot_general(side, hidden, over_rows, preferred_element_type=F32)  11.3 us
    dot_general x6, matrix products, against(): part = jnp.dot(x, w[at:at + x.shape[1]], preferred_element_type=F32)  10.1 us
    pallas_call x2, Pallas kernels, combine(): pl.pallas_call(functools.partial(combine_kernel, peers), grid_spec=pltpu....  7.37 us
    pallas_call x6, Pallas kernels, select(): pl.pallas_call(functools.partial(select_kernel, peers, count, slots, scal...  7.13 us
  transfers between devices with their start and end apart: 38, of which 17 were waited for; matrix products, arithmetic and copies ran while one was open for 19% of the time, Pallas kernels for 6%

profile of v2, /device:TPU:9, one launch (start us, length us, event | category | flops | bytes accessed | tf_op | source)
XLA Modules:
  0.0 231.2 jit_solution(4684717483596665498)
XLA Ops:
  7.2 1.9 fusion.38
  11.0 1.3 collective-permute-start
  13.4 1.4 collective-permute-start.2
  16.0 2.1 collective-permute-start.6
  19.4 1.4 collective-permute-start.3
  25.0 3.1 %collective-permute-done.3 = bf16[1,72,2048]{2,1,0:T(8,128)(2,1)S(1)} collective-permute-done((bf16[1,72,2048]{2,1,0:T(8,128)(2,1)S(1)}, bf16[1,72,2048]{2,1,0:T(8,128)(2,1)S(1)}, u32[]{:S(2)}, u32[]{:S(2)}) %collective-permute-start.3) | collective-permute-done | bytes 294944 | tf_op jit(solution)/shard_map/ppermute | solution.py:133
  28.1 6.3 %collective-permute-done.4 = bf16[1,72,2048]{2,1,0:T(8,128)(2,1)S(1)} collective-permute-done((bf16[1,72,2048]{2,1,0:T(8,128)(2,1)S(1)}, bf16[1,72,2048]{2,1,0:T(8,128)(2,1)S(1)}, u32[]{:S(2)}, u32[]{:S(2)}) %collective-permute-start.4) | collective-permute-done | bytes 294944 | tf_op jit(solution)/shard_map/ppermute | solution.py:133
  34.4 1.3 collective-permute-done.5
  35.7 2.2 pad_maximum_fusion.7
  37.9 3.7 %broadcast_select_fusion.3 = (bf16[1024,768]{1,0:T(8,128)(2,1)}, bf16[1024,768]{1,0:T(8,128)(2,1)}) fusion(bf16[1024,768]{1,0:T(8,128)(2,1)} %collective-permute-done.6, pred[]{:T(512)S(6)} %eq.46, bf16[1,1024,768]{2,1,0:T(8,128)(2,1)} %param.11), kind=kLoop, calls=%fused_computation.22 | loop fusion | flops 1572864 | bytes 6291457 | tf_op jit(solution)/shard_map/jit(_where)/select_n | solution.py:185
  43.9 1.3 collective-permute-start.10
  46.6 1.8 collective-permute-start.14
  48.4 2.5 %fusion.33 = f32[288,768]{1,0:T(8,128)S(1)} fusion(bf16[288,2048]{1,0:T(8,128)(2,1)} %bitcast.124, bf16[1024,768]{1,0:T(8,128)(2,1)S(1)} %copy-done.13, bf16[1024,768]{1,0:T(8,128)(2,1)S(1)} %copy-done.17), kind=kOutput, calls=%fused_computation.76 | convolution fusion | flops 912261120 | bytes 5210112 | tf_op jit(solution)/shard_map/dot_general | solution.py:215
  51.0 1.7 broadcast_select_fusion.1
  55.5 12.6 %all-gather.11.cloned.1.call-done = bf16[512,1024]{1,0:T(8,128)(2,1)} async-done(((bf16[128,1024]{1,0:T(8,128)(2,1)}), bf16[512,1024]{1,0:T(8,128)(2,1)}) %all-gather.11.cloned.1.call-update) | async-done | bytes 1048592 | tf_op jit(solution)/shard_map/all_gather | solution.py:156
  70.5 1.3 collective-permute-start.11
  73.2 1.6 pad_maximum_fusion.2
  75.0 1.5 fusion.39
  76.6 4.9 %collective-permute-done.11 = bf16[3,72,1024]{2,1,0:T(8,128)(2,1)S(1)} collective-permute-done((bf16[3,72,1024]{2,1,0:T(8,128)(2,1)S(1)}, bf16[3,72,1024]{2,1,0:T(8,128)(2,1)S(1)}, u32[]{:S(2)}, u32[]{:S(2)}) %collective-permute-start.11) | collective-permute-done | bytes 442400 | tf_op jit(solution)/shard_map/ppermute | solution.py:133
  82.3 9.5 %collective-permute-done.13 = bf16[3,72,1024]{2,1,0:T(8,128)(2,1)S(1)} collective-permute-done((bf16[3,72,1024]{2,1,0:T(8,128)(2,1)S(1)}, bf16[3,72,1024]{2,1,0:T(8,128)(2,1)S(1)}, u32[]{:S(2)}, u32[]{:S(2)}) %collective-permute-start.13) | collective-permute-done | bytes 442400 | tf_op jit(solution)/shard_map/ppermute | solution.py:133
  93.2 1.5 fusion.40
  94.7 1.2 collective-permute-start.19
  97.5 1.5 fusion.41
  99.0 1.8 multiply_convert_fusion
  102.7 3.4 %convolution_convert_fusion.1 = bf16[1152,1024]{1,0:T(8,128)(2,1)S(1)} fusion(bf16[1152,768]{1,0:T(8,128)(2,1)S(1)} %bitcast.114, bf16[1024,768]{1,0:T(8,128)(2,1)} %collective-permute-done.14, pred[]{:T(512)S(6)} %eq.46, bf16[1,1024,768]{2,1,0:T(8,128)(2,1)S(1)} %copy-done.33), kind=kOutput, calls=%fused_computation.1 | convolution fusion | flops 1813905408 | bytes 7274497 | tf_op jit(solution)/shard_map/dot_general | solution.py:236
  107.7 4.1 %collective-permute-done.17 = bf16[1,72,2048]{2,1,0:T(8,128)(2,1)S(1)} collective-permute-done((bf16[1,72,2048]{2,1,0:T(8,128)(2,1)S(1)}, bf16[1,72,2048]{2,1,0:T(8,128)(2,1)S(1)}, u32[]{:S(2)}, u32[]{:S(2)}) %collective-permute-start.17) | collective-permute-done | bytes 294944 | tf_op jit(solution)/shard_map/ppermute | solution.py:133
  111.8 1.5 collective-permute-start.16
  113.3 3.4 %convolution_convert_fusion = bf16[1152,1024]{1,0:T(8,128)(2,1)} fusion(bf16[1152,768]{1,0:T(8,128)(2,1)S(1)} %bitcast.115, bf16[1024,768]{1,0:T(8,128)(2,1)} %collective-permute-done.14, pred[]{:T(512)S(6)} %eq.46, bf16[1,1024,768]{2,1,0:T(8,128)(2,1)S(1)} %copy-done.33), kind=kOutput, calls=%fused_computation | convolution fusion | flops 1813905408 | bytes 7274497 | tf_op jit(solution)/shard_map/dot_general | solution.py:236
  116.7 6.1 %collective-permute-done.20.refs_3_ = bf16[4,72,1024]{2,1,0:T(8,128)(2,1)S(1)} collective-permute-done((bf16[4,72,1024]{2,1,0:T(8,128)(2,1)S(1)}, bf16[4,72,1024]{2,1,0:T(8,128)(2,1)S(1)}, u32[]{:S(2)}, u32[]{:S(2)}) %collective-permute-start.20) | collective-permute-done | bytes 589856 | tf_op jit(solution)/shard_map/ppermute | solution.py:133
  122.8 13.4 %collective-permute-done.18.refs_2_ = bf16[4,72,1024]{2,1,0:T(8,128)(2,1)S(1)} collective-permute-done((bf16[4,72,1024]{2,1,0:T(8,128)(2,1)S(1)}, bf16[4,72,1024]{2,1,0:T(8,128)(2,1)S(1)}, u32[]{:S(2)}, u32[]{:S(2)}) %collective-permute-start.18) | collective-permute-done | bytes 589856 | tf_op jit(solution)/shard_map/ppermute | solution.py:133
  136.3 3.7 %shard_map.90 = bf16[4,128,1024]{2,1,0:T(8,128)(2,1)} custom-call(s32[1]{0:T(128)} %bitcast._, f32[16,128]{1,0:T(8,128)S(1)} %bitcast.106, f32[16,128]{1,0:T(8,128)S(1)} %bitcast.108, bf16[4,72,1024]{2,1,0:T(8,128)(2,1)S(1)} %bitcast.104, bf16[4,72,1024]{2,1,0:T(8,128)(2,1)S(1)} %collective-permute-done.16.refs_1_, ...), custom_call_target="tpu_custom_call" | custom-call | flops 603979776 | bytes 3407872 | tf_op jit(solution)/shard_map/pallas_call | solution.py:97
  141.3 1.7 shard_map.92
  145.5 1.6 copy-done.9
  148.5 1.3 collective-permute-start.22
  150.2 1.8 fusion.17
  151.9 1.8 fusion.15
  153.7 9.0 %collective-permute-done.23.refs_3_ = bf16[4,72,1024]{2,1,0:T(8,128)(2,1)S(1)} collective-permute-done((bf16[4,72,1024]{2,1,0:T(8,128)(2,1)S(1)}, bf16[4,72,1024]{2,1,0:T(8,128)(2,1)S(1)}, u32[]{:S(2)}, u32[]{:S(2)}) %collective-permute-start.23) | collective-permute-done | bytes 589856 | tf_op jit(solution)/shard_map/ppermute | solution.py:133
  163.8 13.3 %collective-permute-done.22.refs_2_ = bf16[4,72,1024]{2,1,0:T(8,128)(2,1)S(1)} collective-permute-done((bf16[4,72,1024]{2,1,0:T(8,128)(2,1)S(1)}, bf16[4,72,1024]{2,1,0:T(8,128)(2,1)S(1)}, u32[]{:S(2)}, u32[]{:S(2)}) %collective-permute-start.22) | collective-permute-done | bytes 589856 | tf_op jit(solution)/shard_map/ppermute | solution.py:133
  178.4 1.8 fusion.13
  180.3 1.7 fusion.11
  182.0 3.7 %shard_map.91 = bf16[4,128,1024]{2,1,0:T(8,128)(2,1)} custom-call(s32[1]{0:T(128)} %bitcast._, f32[16,128]{1,0:T(8,128)S(1)} %bitcast.107, f32[16,128]{1,0:T(8,128)S(1)} %bitcast.109, bf16[4,72,1024]{2,1,0:T(8,128)(2,1)S(1)} %bitcast.103, bf16[4,72,1024]{2,1,0:T(8,128)(2,1)S(1)} %collective-permute-done.21.refs_1_, ...), custom_call_target="tpu_custom_call" | custom-call | flops 603979776 | bytes 3407872 | tf_op jit(solution)/shard_map/pallas_call | solution.py:97
  185.7 1.3 collective-permute-start.30
  187.1 9.1 %collective-permute-done.25 = bf16[3,72,1024]{2,1,0:T(8,128)(2,1)} collective-permute-done((bf16[3,72,1024]{2,1,0:T(8,128)(2,1)S(1)}, bf16[3,72,1024]{2,1,0:T(8,128)(2,1)}, u32[]{:S(2)}, u32[]{:S(2)}) %collective-permute-start.25) | collective-permute-done | bytes 442400 | tf_op jit(solution)/shard_map/ppermute | solution.py:133
  197.6 1.7 pad_maximum_fusion.5
  200.8 1.3 collective-permute-start.27
  202.1 1.8 collective-permute-done.30
  203.9 10.4 %collective-permute-done.29 = bf16[3,72,1024]{2,1,0:T(8,128)(2,1)S(1)} collective-permute-done((bf16[3,72,1024]{2,1,0:T(8,128)(2,1)S(1)}, bf16[3,72,1024]{2,1,0:T(8,128)(2,1)S(1)}, u32[]{:S(2)}, u32[]{:S(2)}) %collective-permute-start.29) | collective-permute-done | bytes 442400 | tf_op jit(solution)/shard_map/ppermute | solution.py:133
  222.5 1.9 pad_maximum_fusion.9
  (167 shorter events, 46.4 us)
Async XLA Ops:
  7.2 3.7 %copy-start.31 = (f32[128,8]{0,1:T(8,128)S(1)}, f32[128,8]{0,1:T(8,128)}, u32[]{:S(2)}) copy-start(f32[128,8]{0,1:T(8,128)} %param.9) | copy-start | bytes 12292
  7.2 3.7 %copy-start.32 = (s32[128,8]{0,1:T(8,128)S(1)}, s32[128,8]{0,1:T(8,128)}, u32[]{:S(2)}) copy-start(s32[128,8]{0,1:T(8,128)} %param.8) | copy-start | bytes 12292
  7.2 34.5 %all-gather.9.cloned.1.call-start = ((), (), s32[]{:S(2)}) async-start(), calls=%async_computation.4 | async-start | bytes 1310720 | tf_op jit(solution)/shard_map/all_gather | solution.py:156
  9.1 9.2 %copy-start.4 = (bf16[128,2048]{1,0:T(8,128)(2,1)S(1)}, bf16[128,2048]{1,0:T(8,128)(2,1)}, u32[]{:S(2)}) copy-start(bf16[128,2048]{1,0:T(8,128)(2,1)} %param.7) | copy-start | bytes 1572868
  9.1 58.9 %all-gather.11.cloned.1.call-start = ((), (), s32[]{:S(2)}) async-start(), calls=%async_computation.5 | async-start | bytes 1310720 | tf_op jit(solution)/shard_map/all_gather | solution.py:156
  9.9 130.2 %all-gather.13.cloned.1.call-start = ((), (), s32[]{:S(2)}) async-start(), calls=%async_computation.6 | async-start | bytes 1310720 | tf_op jit(solution)/shard_map/all_gather | solution.py:156
  10.8 132.2 %all-gather.15.cloned.1.call-start = ((), (), s32[]{:S(2)}) async-start(), calls=%async_computation.7 | async-start | bytes 1310720 | tf_op jit(solution)/shard_map/all_gather | solution.py:156
  11.0 3.8 %collective-permute-start = (f32[2,16,128]{2,1,0:T(8,128)S(1)}, f32[2,16,128]{2,1,0:T(8,128)S(1)}, u32[]{:S(2)}, u32[]{:S(2)}) collective-permute-start(f32[2,16,128]{2,1,0:T(8,128)S(1)} %get-tuple-element.145), channel_id=1, source_target_pairs={{0,8},{2,10},{4,12},{6,14},{8,16},{10,18},{12,20},{14,22},{16,24},... | collective-permute-start | bytes 49160 | tf_op jit(solution)/shard_map/ppermute | solution.py:130
  12.3 3.5 %collective-permute-start.1 = (f32[2,16,128]{2,1,0:T(8,128)S(1)}, f32[2,16,128]{2,1,0:T(8,128)S(1)}, u32[]{:S(2)}, u32[]{:S(2)}) collective-permute-start(f32[2,16,128]{2,1,0:T(8,128)S(1)} %get-tuple-element.145), channel_id=1, source_target_pairs={{0,16},{2,18},{4,20},{6,22},{8,24},{10,26},{12,28},{14,30},{16,0},... | collective-permute-start | bytes 49160 | tf_op jit(solution)/shard_map/ppermute | solution.py:130
  13.4 2.6 %collective-permute-start.2 = (f32[2,16,128]{2,1,0:T(8,128)S(1)}, f32[2,16,128]{2,1,0:T(8,128)S(1)}, u32[]{:S(2)}, u32[]{:S(2)}) collective-permute-start(f32[2,16,128]{2,1,0:T(8,128)S(1)} %get-tuple-element.145), channel_id=1, source_target_pairs={{0,24},{2,26},{4,28},{6,30},{8,0},{10,2},{12,4},{14,6},{16,8},{18,... | collective-permute-start | bytes 49160 | tf_op jit(solution)/shard_map/ppermute | solution.py:130
  16.0 21.9 %collective-permute-start.6 = (bf16[1024,768]{1,0:T(8,128)(2,1)}, bf16[1024,768]{1,0:T(8,128)(2,1)}, u32[]{:S(2)}, u32[]{:S(2)}) collective-permute-start(bf16[1024,768]{1,0:T(8,128)(2,1)} %bitcast.18), channel_id=1, source_target_pairs={{0,1},{1,0},{2,3},{3,2},{4,5},{5,4},{6,7},{7,6},{8,9},{9,8},{10,11... | collective-permute-start | bytes 4718600 | tf_op jit(solution)/shard_map/ppermute | solution.py:136
  19.4 8.7 %collective-permute-start.3 = (bf16[1,72,2048]{2,1,0:T(8,128)(2,1)S(1)}, bf16[1,72,2048]{2,1,0:T(8,128)(2,1)S(1)}, u32[]{:S(2)}, u32[]{:S(2)}) collective-permute-start(bf16[1,72,2048]{2,1,0:T(8,128)(2,1)S(1)} %get-tuple-element.61), channel_id=1, source_target_pairs={{0,2},{2,0},{4,6},{6,4},{8,10},{10,8},{12,14},{14,12},{16,18},{18,... | collective-permute-start | bytes 884744 | tf_op jit(solution)/shard_map/ppermute | solution.py:133
  20.9 13.5 %collective-permute-start.4 = (bf16[1,72,2048]{2,1,0:T(8,128)(2,1)S(1)}, bf16[1,72,2048]{2,1,0:T(8,128)(2,1)S(1)}, u32[]{:S(2)}, u32[]{:S(2)}) collective-permute-start(bf16[1,72,2048]{2,1,0:T(8,128)(2,1)S(1)} %get-tuple-element.62), channel_id=1, source_target_pairs={{0,4},{2,6},{4,0},{6,2},{8,12},{10,14},{12,8},{14,10},{16,20},{18,... | collective-permute-start | bytes 884744 | tf_op jit(solution)/shard_map/ppermute | solution.py:133
  22.1 13.6 %collective-permute-start.5 = (bf16[1,72,2048]{2,1,0:T(8,128)(2,1)S(1)}, bf16[1,72,2048]{2,1,0:T(8,128)(2,1)}, u32[]{:S(2)}, u32[]{:S(2)}) collective-permute-start(bf16[1,72,2048]{2,1,0:T(8,128)(2,1)S(1)} %get-tuple-element.63), channel_id=1, source_target_pairs={{0,6},{2,4},{4,2},{6,0},{8,14},{10,12},{12,10},{14,8},{16,22},{18,... | collective-permute-start | bytes 884744 | tf_op jit(solution)/shard_map/ppermute | solution.py:133
  22.1 28.8 %collective-permute-start.7 = (bf16[1024,768]{1,0:T(8,128)(2,1)}, bf16[1024,768]{1,0:T(8,128)(2,1)}, u32[]{:S(2)}, u32[]{:S(2)}) collective-permute-start(bf16[1024,768]{1,0:T(8,128)(2,1)} %bitcast.122), channel_id=1, source_target_pairs={{0,1},{1,0},{2,3},{3,2},{4,5},{5,4},{6,7},{7,6},{8,9},{9,8},{10,11... | collective-permute-start | bytes 4718600 | tf_op jit(solution)/shard_map/ppermute | solution.py:136
  23.8 198.8 %reduce-scatter.3.cloned.1.call-start = ((), (), s32[]{:S(2)}) async-start(), calls=%async_computation.2 | async-start | bytes 1310720 | tf_op jit(solution)/shard_map/reduce_scatter | solution.py:249
  42.9 5.5 %copy-start.13 = (bf16[1024,768]{1,0:T(8,128)(2,1)S(1)}, bf16[1024,768]{1,0:T(8,128)(2,1)}, u32[]{:S(2)}) copy-start(bf16[1024,768]{1,0:T(8,128)(2,1)} %get-tuple-element.123) | copy-start | bytes 4718596
  42.9 5.5 %copy-start.17 = (bf16[1024,768]{1,0:T(8,128)(2,1)S(1)}, bf16[1024,768]{1,0:T(8,128)(2,1)}, u32[]{:S(2)}) copy-start(bf16[1024,768]{1,0:T(8,128)(2,1)} %get-tuple-element.122) | copy-start | bytes 4718596
  43.9 24.2 %collective-permute-start.10 = (bf16[3,72,1024]{2,1,0:T(8,128)(2,1)S(1)}, bf16[3,72,1024]{2,1,0:T(8,128)(2,1)}, u32[]{:S(2)}, u32[]{:S(2)}) collective-permute-start(bf16[3,72,1024]{2,1,0:T(8,128)(2,1)S(1)} %get-tuple-element.73), channel_id=1, source_target_pairs={{0,6},{2,4},{4,2},{6,0},{8,14},{10,12},{12,10},{14,8},{16,22},{18,... | collective-permute-start | bytes 1327112 | tf_op jit(solution)/shard_map/ppermute | solution.py:133
  45.2 22.9 %collective-permute-start.9 = (bf16[3,72,1024]{2,1,0:T(8,128)(2,1)S(1)}, bf16[3,72,1024]{2,1,0:T(8,128)(2,1)}, u32[]{:S(2)}, u32[]{:S(2)}) collective-permute-start(bf16[3,72,1024]{2,1,0:T(8,128)(2,1)S(1)} %get-tuple-element.71), channel_id=1, source_target_pairs={{0,4},{2,6},{4,0},{6,2},{8,12},{10,14},{12,8},{14,10},{16,20},{18,... | collective-permute-start | bytes 1327112 | tf_op jit(solution)/shard_map/ppermute | solution.py:133
  46.4 21.7 %collective-permute-start.8 = (bf16[3,72,1024]{2,1,0:T(8,128)(2,1)S(1)}, bf16[3,72,1024]{2,1,0:T(8,128)(2,1)}, u32[]{:S(2)}, u32[]{:S(2)}) collective-permute-start(bf16[3,72,1024]{2,1,0:T(8,128)(2,1)S(1)} %get-tuple-element.69), channel_id=1, source_target_pairs={{0,2},{2,0},{4,6},{6,4},{8,10},{10,8},{12,14},{14,12},{16,18},{18,... | collective-permute-start | bytes 1327112 | tf_op jit(solution)/shard_map/ppermute | solution.py:133
  46.6 55.3 %collective-permute-start.14 = (bf16[1024,768]{1,0:T(8,128)(2,1)}, bf16[1024,768]{1,0:T(8,128)(2,1)}, u32[]{:S(2)}, u32[]{:S(2)}) collective-permute-start(bf16[1024,768]{1,0:T(8,128)(2,1)} %bitcast.140), channel_id=1, source_target_pairs={{0,1},{1,0},{2,3},{3,2},{4,5},{5,4},{6,7},{7,6},{8,9},{9,8},{10,11... | collective-permute-start | bytes 4718600 | tf_op jit(solution)/shard_map/ppermute | solution.py:136
  55.5 45.3 %copy-start.5 = (bf16[288,768]{1,0:T(8,128)(2,1)}, bf16[288,768]{1,0:T(8,128)(2,1)S(1)}, u32[]{:S(2)}) copy-start(bf16[288,768]{1,0:T(8,128)(2,1)S(1)} %multiply_convert_fusion.1) | copy-start | bytes 1327108
  70.5 10.9 %collective-permute-start.11 = (bf16[3,72,1024]{2,1,0:T(8,128)(2,1)S(1)}, bf16[3,72,1024]{2,1,0:T(8,128)(2,1)S(1)}, u32[]{:S(2)}, u32[]{:S(2)}) collective-permute-start(bf16[3,72,1024]{2,1,0:T(8,128)(2,1)S(1)} %get-tuple-element.77), channel_id=1, source_target_pairs={{0,2},{2,0},{4,6},{6,4},{8,10},{10,8},{12,14},{14,12},{16,18},{18,... | collective-permute-start | bytes 1327112 | tf_op jit(solution)/shard_map/ppermute | solution.py:133
  71.8 10.5 %collective-permute-start.12 = (bf16[3,72,1024]{2,1,0:T(8,128)(2,1)S(1)}, bf16[3,72,1024]{2,1,0:T(8,128)(2,1)S(1)}, u32[]{:S(2)}, u32[]{:S(2)}) collective-permute-start(bf16[3,72,1024]{2,1,0:T(8,128)(2,1)S(1)} %get-tuple-element.79), channel_id=1, source_target_pairs={{0,4},{2,6},{4,0},{6,2},{8,12},{10,14},{12,8},{14,10},{16,20},{18,... | collective-permute-start | bytes 1327112 | tf_op jit(solution)/shard_map/ppermute | solution.py:133
  73.0 18.8 %collective-permute-start.13 = (bf16[3,72,1024]{2,1,0:T(8,128)(2,1)S(1)}, bf16[3,72,1024]{2,1,0:T(8,128)(2,1)S(1)}, u32[]{:S(2)}, u32[]{:S(2)}) collective-permute-start(bf16[3,72,1024]{2,1,0:T(8,128)(2,1)S(1)} %get-tuple-element.81), channel_id=1, source_target_pairs={{0,6},{2,4},{4,2},{6,0},{8,14},{10,12},{12,10},{14,8},{16,22},{18,... | collective-permute-start | bytes 1327112 | tf_op jit(solution)/shard_map/ppermute | solution.py:133
  93.2 4.3 %copy-start.20 = (bf16[1024,768]{1,0:T(8,128)(2,1)S(1)}, bf16[1024,768]{1,0:T(8,128)(2,1)}, u32[]{:S(2)}) copy-start(bf16[1024,768]{1,0:T(8,128)(2,1)} %copy-done.19) | copy-start | bytes 4718596
  94.7 11.7 %collective-permute-start.19 = (bf16[1,72,2048]{2,1,0:T(8,128)(2,1)S(1)}, bf16[1,72,2048]{2,1,0:T(8,128)(2,1)S(1)}, u32[]{:S(2)}, u32[]{:S(2)}) collective-permute-start(bf16[1,72,2048]{2,1,0:T(8,128)(2,1)S(1)} %get-tuple-element.93), channel_id=1, source_target_pairs={{0,6},{2,4},{4,2},{6,0},{8,14},{10,12},{12,10},{14,8},{16,22},{18,... | collective-permute-start | bytes 884744 | tf_op jit(solution)/shard_map/ppermute | solution.py:133
  96.0 15.8 %collective-permute-start.17 = (bf16[1,72,2048]{2,1,0:T(8,128)(2,1)S(1)}, bf16[1,72,2048]{2,1,0:T(8,128)(2,1)S(1)}, u32[]{:S(2)}, u32[]{:S(2)}) collective-permute-start(bf16[1,72,2048]{2,1,0:T(8,128)(2,1)S(1)} %get-tuple-element.89), channel_id=1, source_target_pairs={{0,4},{2,6},{4,0},{6,2},{8,12},{10,14},{12,8},{14,10},{16,20},{18,... | collective-permute-start | bytes 884744 | tf_op jit(solution)/shard_map/ppermute | solution.py:133
  97.2 14.6 %collective-permute-start.15 = (bf16[1,72,2048]{2,1,0:T(8,128)(2,1)S(1)}, bf16[1,72,2048]{2,1,0:T(8,128)(2,1)S(1)}, u32[]{:S(2)}, u32[]{:S(2)}) collective-permute-start(bf16[1,72,2048]{2,1,0:T(8,128)(2,1)S(1)} %get-tuple-element.85), channel_id=1, source_target_pairs={{0,2},{2,0},{4,6},{6,4},{8,10},{10,8},{12,14},{14,12},{16,18},{18,... | collective-permute-start | bytes 884744 | tf_op jit(solution)/shard_map/ppermute | solution.py:133
  106.5 10.3 %copy-start.25 = (bf16[1,72,2048]{2,1,0:T(8,128)(2,1)}, bf16[1,72,2048]{2,1,0:T(8,128)(2,1)S(1)}, u32[]{:S(2)}) copy-start(bf16[1,72,2048]{2,1,0:T(8,128)(2,1)S(1)} %collective-permute-done.19) | copy-start | bytes 884740
  106.5 16.4 %collective-permute-start.20 = (bf16[4,72,1024]{2,1,0:T(8,128)(2,1)S(1)}, bf16[4,72,1024]{2,1,0:T(8,128)(2,1)S(1)}, u32[]{:S(2)}, u32[]{:S(2)}) collective-permute-start(bf16[4,72,1024]{2,1,0:T(8,128)(2,1)S(1)} %bitcast.128), channel_id=1, source_target_pairs={{0,6},{2,4},{4,2},{6,0},{8,14},{10,12},{12,10},{14,8},{16,22},{18,... | collective-permute-start | bytes 1769480 | tf_op jit(solution)/shard_map/ppermute | solution.py:133
  111.8 4.9 %copy-start.27 = (bf16[1,72,2048]{2,1,0:T(8,128)(2,1)}, bf16[1,72,2048]{2,1,0:T(8,128)(2,1)S(1)}, u32[]{:S(2)}) copy-start(bf16[1,72,2048]{2,1,0:T(8,128)(2,1)S(1)} %collective-permute-done.17) | copy-start | bytes 884740
  111.8 24.5 %collective-permute-start.18 = (bf16[4,72,1024]{2,1,0:T(8,128)(2,1)S(1)}, bf16[4,72,1024]{2,1,0:T(8,128)(2,1)S(1)}, u32[]{:S(2)}, u32[]{:S(2)}) collective-permute-start(bf16[4,72,1024]{2,1,0:T(8,128)(2,1)S(1)} %bitcast.127), channel_id=1, source_target_pairs={{0,4},{2,6},{4,0},{6,2},{8,12},{10,14},{12,8},{14,10},{16,20},{18,... | collective-permute-start | bytes 1769480 | tf_op jit(solution)/shard_map/ppermute | solution.py:133
  111.8 4.9 %copy-start.29 = (bf16[1,72,2048]{2,1,0:T(8,128)(2,1)}, bf16[1,72,2048]{2,1,0:T(8,128)(2,1)S(1)}, u32[]{:S(2)}) copy-start(bf16[1,72,2048]{2,1,0:T(8,128)(2,1)S(1)} %collective-permute-done.15) | copy-start | bytes 884740
  111.8 24.5 %collective-permute-start.16 = (bf16[4,72,1024]{2,1,0:T(8,128)(2,1)S(1)}, bf16[4,72,1024]{2,1,0:T(8,128)(2,1)S(1)}, u32[]{:S(2)}, u32[]{:S(2)}) collective-permute-start(bf16[4,72,1024]{2,1,0:T(8,128)(2,1)S(1)} %bitcast.126), channel_id=1, source_target_pairs={{0,2},{2,0},{4,6},{6,4},{8,10},{10,8},{12,14},{14,12},{16,18},{18,... | collective-permute-start | bytes 1769480 | tf_op jit(solution)/shard_map/ppermute | solution.py:133
  140.0 82.5 %reduce-scatter.5.cloned.1.call-start = ((), (), s32[]{:S(2)}) async-start(), calls=%async_computation.3 | async-start | bytes 1310720 | tf_op jit(solution)/shard_map/reduce_scatter | solution.py:249
  147.4 15.3 %collective-permute-start.23 = (bf16[4,72,1024]{2,1,0:T(8,128)(2,1)S(1)}, bf16[4,72,1024]{2,1,0:T(8,128)(2,1)S(1)}, u32[]{:S(2)}, u32[]{:S(2)}) collective-permute-start(bf16[4,72,1024]{2,1,0:T(8,128)(2,1)S(1)} %bitcast.131), channel_id=1, source_target_pairs={{0,6},{2,4},{4,2},{6,0},{8,14},{10,12},{12,10},{14,8},{16,22},{18,... | collective-permute-start | bytes 1769480 | tf_op jit(solution)/shard_map/ppermute | solution.py:133
  148.5 28.6 %collective-permute-start.22 = (bf16[4,72,1024]{2,1,0:T(8,128)(2,1)S(1)}, bf16[4,72,1024]{2,1,0:T(8,128)(2,1)S(1)}, u32[]{:S(2)}, u32[]{:S(2)}) collective-permute-start(bf16[4,72,1024]{2,1,0:T(8,128)(2,1)S(1)} %bitcast.130), channel_id=1, source_target_pairs={{0,4},{2,6},{4,0},{6,2},{8,12},{10,14},{12,8},{14,10},{16,20},{18,... | collective-permute-start | bytes 1769480 | tf_op jit(solution)/shard_map/ppermute | solution.py:133
  149.8 27.4 %collective-permute-start.21 = (bf16[4,72,1024]{2,1,0:T(8,128)(2,1)S(1)}, bf16[4,72,1024]{2,1,0:T(8,128)(2,1)S(1)}, u32[]{:S(2)}, u32[]{:S(2)}) collective-permute-start(bf16[4,72,1024]{2,1,0:T(8,128)(2,1)S(1)} %bitcast.129), channel_id=1, source_target_pairs={{0,2},{2,0},{4,6},{6,4},{8,10},{10,8},{12,14},{14,12},{16,18},{18,... | collective-permute-start | bytes 1769480 | tf_op jit(solution)/shard_map/ppermute | solution.py:133
  162.7 23.0 %collective-permute-start.26 = (bf16[3,72,1024]{2,1,0:T(8,128)(2,1)}, bf16[3,72,1024]{2,1,0:T(8,128)(2,1)}, u32[]{:S(2)}, u32[]{:S(2)}) collective-permute-start(bf16[3,72,1024]{2,1,0:T(8,128)(2,1)} %get-tuple-element.110), channel_id=1, source_target_pairs={{0,6},{2,4},{4,2},{6,0},{8,14},{10,12},{12,10},{14,8},{16,22},{18,... | collective-permute-start | bytes 1327112 | tf_op jit(solution)/shard_map/ppermute | solution.py:133
  177.1 19.1 %collective-permute-start.25 = (bf16[3,72,1024]{2,1,0:T(8,128)(2,1)S(1)}, bf16[3,72,1024]{2,1,0:T(8,128)(2,1)}, u32[]{:S(2)}, u32[]{:S(2)}) collective-permute-start(bf16[3,72,1024]{2,1,0:T(8,128)(2,1)S(1)} %get-tuple-element.108), channel_id=1, source_target_pairs={{0,4},{2,6},{4,0},{6,2},{8,12},{10,14},{12,8},{14,10},{16,20},{18,... | collective-permute-start | bytes 1327112 | tf_op jit(solution)/shard_map/ppermute | solution.py:133
  177.2 19.1 %collective-permute-start.24 = (bf16[3,72,1024]{2,1,0:T(8,128)(2,1)S(1)}, bf16[3,72,1024]{2,1,0:T(8,128)(2,1)}, u32[]{:S(2)}, u32[]{:S(2)}) collective-permute-start(bf16[3,72,1024]{2,1,0:T(8,128)(2,1)S(1)} %get-tuple-element.106), channel_id=1, source_target_pairs={{0,2},{2,0},{4,6},{6,4},{8,10},{10,8},{12,14},{14,12},{16,18},{18,... | collective-permute-start | bytes 1327112 | tf_op jit(solution)/shard_map/ppermute | solution.py:133
  185.7 18.1 %collective-permute-start.30 = (bf16[3,72,1024]{2,1,0:T(8,128)(2,1)S(1)}, bf16[3,72,1024]{2,1,0:T(8,128)(2,1)S(1)}, u32[]{:S(2)}, u32[]{:S(2)}) collective-permute-start(bf16[3,72,1024]{2,1,0:T(8,128)(2,1)S(1)} %get-tuple-element.117), channel_id=1, source_target_pairs={{0,6},{2,4},{4,2},{6,0},{8,14},{10,12},{12,10},{14,8},{16,22},{18,... | collective-permute-start | bytes 1327112 | tf_op jit(solution)/shard_map/ppermute | solution.py:133
  196.2 18.0 %collective-permute-start.29 = (bf16[3,72,1024]{2,1,0:T(8,128)(2,1)S(1)}, bf16[3,72,1024]{2,1,0:T(8,128)(2,1)S(1)}, u32[]{:S(2)}, u32[]{:S(2)}) collective-permute-start(bf16[3,72,1024]{2,1,0:T(8,128)(2,1)S(1)} %get-tuple-element.115), channel_id=1, source_target_pairs={{0,4},{2,6},{4,0},{6,2},{8,12},{10,14},{12,8},{14,10},{16,20},{18,... | collective-permute-start | bytes 1327112 | tf_op jit(solution)/shard_map/ppermute | solution.py:133
  196.4 17.9 %collective-permute-start.28 = (bf16[3,72,1024]{2,1,0:T(8,128)(2,1)S(1)}, bf16[3,72,1024]{2,1,0:T(8,128)(2,1)S(1)}, u32[]{:S(2)}, u32[]{:S(2)}) collective-permute-start(bf16[3,72,1024]{2,1,0:T(8,128)(2,1)S(1)} %get-tuple-element.113), channel_id=1, source_target_pairs={{0,2},{2,0},{4,6},{6,4},{8,10},{10,8},{12,14},{14,12},{16,18},{18,... | collective-permute-start | bytes 1327112 | tf_op jit(solution)/shard_map/ppermute | solution.py:133
  200.8 18.6 %collective-permute-start.27 = (bf16[512,768]{1,0:T(8,128)(2,1)S(1)}, bf16[512,768]{1,0:T(8,128)(2,1)S(1)}, u32[]{:S(2)}, u32[]{:S(2)}) collective-permute-start(bf16[512,768]{1,0:T(8,128)(2,1)S(1)} %add_convert_fusion.3), channel_id=1, source_target_pairs={{0,1},{1,0},{2,3},{3,2},{4,5},{5,4},{6,7},{7,6},{8,9},{9,8},{10,11... | collective-permute-start | bytes 2359304 | tf_op jit(solution)/shard_map/ppermute | solution.py:136
  216.7 3.4 %collective-permute-start.31 = (bf16[512,768]{1,0:T(8,128)(2,1)S(1)}, bf16[512,768]{1,0:T(8,128)(2,1)S(1)}, u32[]{:S(2)}, u32[]{:S(2)}) collective-permute-start(bf16[512,768]{1,0:T(8,128)(2,1)S(1)} %add_convert_fusion.1), channel_id=1, source_target_pairs={{0,1},{1,0},{2,3},{3,2},{4,5},{5,4},{6,7},{7,6},{8,9},{9,8},{10,11... | collective-permute-start | bytes 2359304 | tf_op jit(solution)/shard_map/ppermute | solution.py:136
  (24 other events, 40.8 us)
Sparse Core Ops, SparseCore 0:
  10.2 28.8 all-gather.8
  40.7 27.3 all-gather.10
  69.6 27.4 all-gather.12
  98.5 27.4 all-gather.14
  140.1 25.0 reduce-scatter.2
  185.8 25.7 reduce-scatter.4

commit v3 on v2

v3 whole, which is shorter than its diff:
```python
import functools

import jax
import jax.numpy as jnp
from jax import lax
from jax.experimental import pallas as pl
from jax.experimental.pallas import tpu as pltpu
from jax.sharding import PartitionSpec as P

F32 = jnp.float32
BF16 = jnp.bfloat16
VMEM_LIMIT = 48 * 1024 * 1024


def two_levels(experts):
    minor = 1
    while minor * minor * 4 <= experts:
        minor *= 2
    return experts // minor, minor


def column_tile(columns):
    return 512 if columns % 512 == 0 else columns


def select_kernel(peers, count, slots, scaled, _, pos_ref, weight_ref, *refs):
    sources, outs = refs[:count], refs[count:]
    toks = pos_ref.shape[1]
    slot = lax.broadcasted_iota(jnp.int32, (slots, toks), 0).astype(F32)
    for g in range(count):
        hits = [slot == pos_ref[k * count + g : k * count + g + 1, :] for k in range(peers)]
        onehot = jnp.concatenate([jnp.where(h, 1.0, 0.0) for h in hits], axis=0).astype(BF16)
        rows = jnp.dot(onehot, sources[g][0], preferred_element_type=F32)
        for k in range(peers):
            part = rows[k * slots : (k + 1) * slots]
            if scaled:
                weights = weight_ref[k * count + g : k * count + g + 1, :]
                part = part * jnp.sum(jnp.where(hits[k], weights, 0.0), axis=1, keepdims=True)
            outs[k][g] = part.astype(BF16)


def select(blocks, which, table, slots, scaled, tiles, tile):
    pos, weight = table
    count = len(blocks)
    peers = pos.shape[0] // count
    toks = blocks[0].shape[1]
    cols = tile * len(tiles)
    small = pl.BlockSpec(pos.shape, lambda j, ref: (0, 0))
    step = tiles[1] - tiles[0] if len(tiles) > 1 else 1
    inner = next((i for i in range(1, len(tiles)) if tiles[i] - tiles[i - 1] != step), len(tiles))
    hop = tiles[inner] - tiles[0] if inner < len(tiles) else 0

    def column(j):
        return tiles[0] + lax.rem(j, inner) * step + (j // inner) * hop

    def source(g):
        return pl.BlockSpec((1, toks, tile), lambda j, ref: (ref[g], 0, column(j)))

    return pl.pallas_call(
        functools.partial(select_kernel, peers, count, slots, scaled),
        grid_spec=pltpu.PrefetchScalarGridSpec(
            num_scalar_prefetch=1,
            grid=(len(tiles),),
            in_specs=[small, small] + [source(g) for g in range(count)],
            out_specs=[pl.BlockSpec((count, slots, tile), lambda j, ref: (0, 0, j))] * peers,
        ),
        out_shape=[jax.ShapeDtypeStruct((count, slots, cols), BF16)] * peers,
        compiler_params=pltpu.CompilerParams(vmem_limit_bytes=VMEM_LIMIT),
        cost_estimate=pl.CostEstimate(
            flops=2 * peers * count * slots * toks * cols,
            bytes_accessed=2 * count * cols * (toks + peers * slots),
            transcendentals=0,
        ),
    )(which, pos, weight, *blocks)


def combine_kernel(peers, _, pos_ref, weight_ref, *refs):
    own, rest, out = refs[:peers], refs[peers : 2 * peers], refs[2 * peers]
    g, count = pl.program_id(0), pl.num_programs(0)
    toks, slots = pos_ref.shape[1], own[0].shape[1]

    def add_up(rows):
        slot = lax.broadcasted_iota(jnp.int32, (slots, toks), 0).astype(F32)
        spread = []
        for k in range(peers):
            at = pl.ds(k * count + g, 1)
            spread.append(jnp.where(slot == pos_ref[at, :], weight_ref[at, :], 0.0))
        spread = jnp.concatenate(spread, axis=0)
        high = spread.astype(BF16).astype(F32)
        both = jnp.concatenate([high, spread - high], axis=1).astype(BF16)
        held = jnp.concatenate([r[0] for r in rows], axis=0)
        total = lax.dot_general(both, held, (((0,), (0,)), ((), ())), preferred_element_type=F32)
        out[0] = (total[:toks] + total[toks:]).astype(BF16)

    pl.when(g == 0)(lambda: add_up(own))
    pl.when(g > 0)(lambda: add_up(rest))


def combine(which, table, own, rest, half):
    pos, weight = table
    count, slots, cols = rest[0].shape
    count += 1
    peers, toks = len(rest), pos.shape[1]
    small = pl.BlockSpec(pos.shape, lambda g, ref: (0, 0))
    return pl.pallas_call(
        functools.partial(combine_kernel, peers),
        grid_spec=pltpu.PrefetchScalarGridSpec(
            num_scalar_prefetch=1,
            grid=(count,),
            in_specs=[small, small]
            + [pl.BlockSpec((1, slots, cols), lambda g, ref: (0, 0, half))] * peers
            + [pl.BlockSpec((1, slots, cols), lambda g, ref: (jnp.maximum(g - 1, 0), 0, 0))] * peers,
            out_specs=pl.BlockSpec((1, toks, cols), lambda g, ref: (ref[g], 0, 0)),
        ),
        out_shape=jax.ShapeDtypeStruct((count, toks, cols), BF16),
        compiler_params=pltpu.CompilerParams(vmem_limit_bytes=VMEM_LIMIT),
        cost_estimate=pl.CostEstimate(
            flops=4 * peers * count * slots * toks * cols,
            bytes_accessed=2 * cols * count * (toks + peers * slots),
            transcendentals=0,
        ),
    )(which, pos, weight, *own, *rest)


def shards(tokens, routes, route_logits, cotangent, gate_weight, up_weight, down_weight):
    toks, top = routes.shape
    experts = lax.axis_size("expert")
    major, minor = two_levels(experts)
    per_expert = toks * top // experts
    slots = min(toks, per_expert + max(2, per_expert // 8))
    slots = -(-slots // 8) * 8
    here = lax.axis_index("expert")
    core = lax.axis_index("dp")
    plane, place = here // minor, here % minor

    def to_plane(x, shift):
        return lax.ppermute(x, "expert", [(i, (i + shift * minor) % experts) for i in range(experts)])

    def to_peer(x, k):
        return lax.ppermute(x, "expert", [(i, i ^ k) for i in range(experts)])

    def other_core(x):
        return lax.ppermute(x, "dp", [(0, 1), (1, 0)])

    def after(x, earlier):
        return lax.optimization_barrier((x, *earlier))[0] if earlier else x

    def after_all(xs, earlier):
        return list(lax.optimization_barrier((*xs, *earlier))[: len(xs)])

    exp_logits = jnp.exp(route_logits)
    route_weight = (exp_logits / jnp.sum(exp_logits, axis=1, keepdims=True)).T
    names = routes.T[:, None, :] == jnp.arange(experts, dtype=jnp.int32)[None, :, None]
    chosen = jnp.sum(names.astype(F32), axis=0)
    dense_weight = jnp.sum(jnp.where(names, route_weight[:, None, :], 0.0), axis=0)
    before = jnp.arange(toks)[:, None] < jnp.arange(toks)[None, :]
    position = jnp.dot(chosen.astype(BF16), before.astype(BF16), preferred_element_type=F32)
    meta = jnp.stack([jnp.where(chosen > 0, position, -1.0), dense_weight])

    mine = plane * minor + (place ^ jnp.arange(minor))
    mine = (mine[:, None] == jnp.arange(experts)[None, :]).astype(F32)

    sender = (plane + major - jnp.arange(major, dtype=jnp.int32)) % major
    zero = jnp.zeros((1,), jnp.int32)
    same_place = [[i * minor + j for i in range(major)] for j in range(minor)]
    model_width, out_cols = tokens.shape[1], cotangent.shape[1]
    piece, wide, deep = out_cols // 4, out_cols // 2, model_width // 2

    def spread(x):
        return lax.all_gather(x, "expert", axis=0, axis_index_groups=same_place)

    token_all = [spread(tokens[:, h * deep : (h + 1) * deep]) for h in range(2)]
    cot_all = [
        spread(
            jnp.concatenate(
                [cotangent[:, i * piece : (i + 1) * piece] for i in (h, 2 + h)], axis=1
            )
        )
        for h in range(2)
    ]
    metas = [meta] + [to_plane(meta, s) for s in range(1, major)]

    def table_of(shifts):
        stacked = jnp.stack([metas[s] for s in shifts])
        picked = jnp.sum(stacked[:, :, None] * mine[None, None, :, :, None], axis=3)
        picked = picked.transpose(1, 2, 0, 3).reshape(2, minor * len(shifts), toks)
        return picked[0], picked[1]

    own_table, all_table = table_of([0]), table_of(list(range(major)))
    rest_table = [t.reshape(minor, major, toks)[:, 1:].reshape(-1, toks) for t in all_table]

    queue = [[] for _ in range(minor)]

    def exchange(rows):
        back = [rows[0]]
        for k in range(1, minor):
            back.append(to_peer(after(rows[k], queue[k]), k))
            queue[k] = [back[k]]
        return back

    def joined(parts):
        return jnp.concatenate(parts, axis=0).reshape(-1, parts[0].shape[-1])

    def pick_rest(x, scaled):
        tile = column_tile(x.shape[2])
        tiles = list(range(x.shape[2] // tile))
        return select([x] * (major - 1), sender[1:], rest_table, slots, scaled, tiles, tile)

    def hidden_of(pieces):
        def against(w):
            total, at = None, 0
            for x in pieces:
                part = jnp.dot(x, w[at : at + x.shape[1]], preferred_element_type=F32)
                total, at = part if total is None else total + part, at + x.shape[1]
            return total

        return (jax.nn.silu(against(gate_mat)) * against(up_mat)).astype(BF16)

    def out_of(hidden, w):
        out = lax.dot_general(hidden, w, (((1,), (1,)), ((), ())), preferred_element_type=F32)
        out = out.astype(BF16).reshape(minor, -1, slots, w.shape[0])
        return [out[k] for k in range(minor)]

    tile = column_tile(model_width)
    got = [other_core(w[0]) for w in (gate_weight, up_weight, down_weight)]
    gate_mat, up_mat, down_mat = (
        jnp.concatenate([jnp.where(core == 0, w[0], g), jnp.where(core == 0, g, w[0])], axis=0)
        for w, g in zip((gate_weight, up_weight, down_weight), got)
    )
    every = list(range(model_width // tile))
    own_tokens = after(tokens, metas[1:])[None]
    own_rows = exchange(select([own_tokens], zero, own_table, slots, False, every, tile))
    own_cots = joined(
        exchange(select([cotangent[None]], zero, own_table, slots, True, [0, 2, 1, 3], piece))
    )
    own_hidden = hidden_of([joined(own_rows)])
    own_out = out_of(own_hidden, down_mat)
    first = exchange(pick_rest(after(token_all[0], got), False))
    second = exchange(pick_rest(after(token_all[1], [*first[1:], *own_out]), False))
    own_back = exchange(own_out)
    rest_hidden = hidden_of([joined(first), joined(second)])

    outs = [out_of(rest_hidden, down_mat[h * wide : (h + 1) * wide]) for h in range(2)]
    cots = [pick_rest(after(cot_all[0], second[1:]), True), None]
    mixed = []
    for h in range(2):
        back = exchange(outs[h] if h else after_all(outs[h], cots[0]))
        sums = combine(sender, all_table, own_back, after_all(back, outs[1]), h)
        mixed.append(
            lax.psum_scatter(sums, "expert", scatter_dimension=0, axis_index_groups=same_place)
        )
    mixed = jnp.concatenate(mixed, axis=1)
    cots[1] = pick_rest(cot_all[1], True)
    rest_cots = [joined(exchange(x)) for x in cots]

    over_rows = (((0,), (0,)), ((), ()))
    done = []
    for h in range(2):
        own_half = own_cots[:, h * 2 * piece : (h + 1) * 2 * piece]

        def grad_of(which):
            def part(rows, hidden):
                side = lax.dynamic_slice_in_dim(rows, which * piece, piece, axis=1)
                return lax.dot_general(side, hidden, over_rows, preferred_element_type=F32)

            return part(own_half, own_hidden) + part(rest_cots[h], rest_hidden)

        theirs = other_core(grad_of(1 - core).astype(BF16))
        done.append((grad_of(core) + theirs.astype(F32)).astype(BF16))
    return mixed, jnp.concatenate(done, axis=0)[None]


def solution(mesh):
    placed = (
        P(("groups", "expert", "dp"), None),
        P(("groups", "expert", "dp"), None),
        P(("groups", "expert", "dp"), None),
        P(("groups", "expert", "dp"), None),
        P("expert", "dp", None),
        P("expert", "dp", None),
        P("expert", "dp", None),
    )
    return jax.shard_map(
        shards,
        mesh=mesh,
        in_specs=placed,
        out_specs=(P(("groups", "expert", "dp"), None), P(("groups", "expert"), "dp", None)),
        check_vma=False,
    )
```

time: 233 us -> 222 us (0.953)
  waiting for transfers between devices: 108 us -> 89.7 us
  starting transfers between devices: 32.1 us -> 37 us
  matrix products: 28.4 us -> 26 us
    all_gather x4, waiting for transfers between devices: 12.6 us -> 0.04 us  [spread(): return lax.all_gather(x, 'expert', axis=0, axis_index_groups=same_place)]
    ppermute x24 -> x27, starting transfers between devices: 21.5 us -> 28.9 us  [to_peer(): return lax.ppermute(x, 'expert', [(i, i ^ k) for i in range(experts)])]
    ppermute x24 -> x27, waiting for transfers between devices: 93 us -> 88 us  [to_peer(): return lax.ppermute(x, 'expert', [(i, i ^ k) for i in range(experts)])]
    ppermute x5, starting transfers between devices: 6.6 us -> 2.96 us  [other_core(): return lax.ppermute(x, 'dp', [(0, 1), (1, 0)])]
    pallas_call x6, Pallas kernels: 7.13 us -> 9.6 us  [select(): pl.pallas_call(functools.partial(select_kernel, peers, count, slots, scal...]
    dot_general x2 -> x3, matrix products: 6.88 us -> 5.83 us  [out_of(): lax.dot_general(hidden, w, (((1,), (1,)), ((), ())), preferred_element_ty...]
    unnamed x68 -> x86, local copies, waits for them, and re-layouts: 14.2 us -> 13.6 us
    select_n x2 -> x4, other arithmetic: 5.44 us -> 5.99 us  [the longest x3 5.98 us: shards(): jnp.where(core == 0, w[0], g)]
  transfers between devices with their start and end apart: 38 -> 41, of which waited for: 17 -> 13; matrix products, arithmetic and copies ran while one was open for 19% -> 20% of each run, Pallas kernels for 6% -> 8%
where the time goes in v3:
time: 222 us; the launch traced here: 221 us
  waiting for transfers between devices  89.7 us (40%)
  starting transfers between devices  37 us (17%)
  matrix products  26 us (12%)
  other arithmetic  18.7 us (8%)
  local copies, waits for them, and re-layouts  18 us (8%)
  Pallas kernels  16.6 us (7%)
  between operations  14.8 us (7%)
    ppermute x27, waiting for transfers between devices, to_peer(): return lax.ppermute(x, 'expert', [(i, i ^ k) for i in range(experts)])  88 us
    ppermute x27, starting transfers between devices, to_peer(): return lax.ppermute(x, 'expert', [(i, i ^ k) for i in range(experts)])  28.9 us
    unnamed x86, local copies, waits for them, and re-layouts  13.6 us
    dot_general x8, matrix products, part(): return lax.dot_general(side, hidden, over_rows, preferred_element_type=F32)  11.2 us
    pallas_call x6, Pallas kernels, select(): pl.pallas_call(functools.partial(select_kernel, peers, count, slots, scal...  9.6 us
    dot_general x6, matrix products, against(): part = jnp.dot(x, w[at:at + x.shape[1]], preferred_element_type=F32)  8.76 us
    concatenate x6, other arithmetic, joined(): return jnp.concatenate(parts, axis=0).reshape(-1, parts[0].shape[-1])  7.11 us
    pallas_call x2, Pallas kernels, combine(): pl.pallas_call(functools.partial(combine_kernel, peers), grid_spec=pltpu....  6.96 us
  transfers between devices with their start and end apart: 41, of which 13 were waited for; matrix products, arithmetic and copies ran while one was open for 20% of the time, Pallas kernels for 8%

profile of v3, /device:TPU:9, one launch (start us, length us, event | category | flops | bytes accessed | tf_op | source)
XLA Modules:
  0.0 220.7 jit_solution(9252602188951046980)
XLA Ops:
  7.3 1.9 fusion.51
  11.8 2.5 %collective-permute-start.1 = (f32[2,16,128]{2,1,0:T(8,128)S(1)}, f32[2,16,128]{2,1,0:T(8,128)S(1)}, u32[]{:S(2)}, u32[]{:S(2)}) collective-permute-start(f32[2,16,128]{2,1,0:T(8,128)S(1)} %get-tuple-element.163), channel_id=1, source_target_pairs={{0,16},{2,18},{4,20},{6,22},{8,24},{10,26},{12,28},{14,30},{16,0},... | collective-permute-start | bytes 49160 | tf_op jit(solution)/shard_map/ppermute | solution.py:137
  15.1 2.2 %collective-permute-start = (f32[2,16,128]{2,1,0:T(8,128)S(1)}, f32[2,16,128]{2,1,0:T(8,128)S(1)}, u32[]{:S(2)}, u32[]{:S(2)}) collective-permute-start(f32[2,16,128]{2,1,0:T(8,128)S(1)} %get-tuple-element.163), channel_id=1, source_target_pairs={{0,8},{2,10},{4,12},{6,14},{8,16},{10,18},{12,20},{14,22},{16,24},... | collective-permute-start | bytes 49160 | tf_op jit(solution)/shard_map/ppermute | solution.py:137
  19.3 1.3 collective-permute-start.3
  21.4 1.3 collective-permute-start.5
  22.7 3.9 %collective-permute-done.3 = bf16[1,72,2048]{2,1,0:T(8,128)(2,1)S(1)} collective-permute-done((bf16[1,72,2048]{2,1,0:T(8,128)(2,1)S(1)}, bf16[1,72,2048]{2,1,0:T(8,128)(2,1)S(1)}, u32[]{:S(2)}, u32[]{:S(2)}) %collective-permute-start.3) | collective-permute-done | bytes 294944 | tf_op jit(solution)/shard_map/ppermute | solution.py:140
  29.1 10.8 %collective-permute-done.4 = bf16[1,72,2048]{2,1,0:T(8,128)(2,1)} collective-permute-done((bf16[1,72,2048]{2,1,0:T(8,128)(2,1)S(1)}, bf16[1,72,2048]{2,1,0:T(8,128)(2,1)}, u32[]{:S(2)}, u32[]{:S(2)}) %collective-permute-start.4) | collective-permute-done | bytes 294944 | tf_op jit(solution)/shard_map/ppermute | solution.py:140
  42.7 2.3 %pad_maximum_fusion.4 = bf16[4,72,2048]{2,1,0:T(8,128)(2,1)} fusion(bf16[1,72,2048]{2,1,0:T(8,128)(2,1)} %collective-permute-done.5, bf16[1,72,2048]{2,1,0:T(8,128)(2,1)} %collective-permute-done.4, bf16[1,72,2048]{2,1,0:T(8,128)(2,1)} %copy-done.37, bf16[1,72,2048]{2,1,0:T(8,128)(2,1)S(1)} %get-tuple-element.67), kind=kLoop, calls=%fused_computation.31 | loop fusion | flops 1769472 | bytes 2359296 | tf_op jit(solution)/shard_map/concatenate | solution.py:202
  46.3 1.6 shard_map.87
  51.0 3.8 %collective-permute-done.13 = bf16[1,72,2048]{2,1,0:T(8,128)(2,1)} collective-permute-done((bf16[1,72,2048]{2,1,0:T(8,128)(2,1)S(1)}, bf16[1,72,2048]{2,1,0:T(8,128)(2,1)}, u32[]{:S(2)}, u32[]{:S(2)}) %collective-permute-start.13) | collective-permute-done | bytes 294944 | tf_op jit(solution)/shard_map/ppermute | solution.py:140
  55.4 1.6 broadcast_select_fusion.5
  59.3 2.1 broadcast_select_fusion.3
  63.7 2.3 %broadcast_select_fusion.1 = (bf16[1024,768]{1,0:T(8,128)(2,1)S(1)}, bf16[1024,768]{1,0:T(8,128)(2,1)S(1)}) fusion(bf16[1024,768]{1,0:T(8,128)(2,1)} %collective-permute-done.8, pred[]{:T(512)S(6)} %eq.46, bf16[1,1024,768]{2,1,0:T(8,128)(2,1)} %param.13), kind=kLoop, calls=%fused_computation.26 | loop fusion | flops 1572864 | bytes 6291457 | tf_op jit(solution)/shard_map/jit(_where)/select_n | solution.py:227
  68.7 5.2 %collective-permute-done.14 = bf16[3,72,1024]{2,1,0:T(8,128)(2,1)} collective-permute-done((bf16[3,72,1024]{2,1,0:T(8,128)(2,1)S(1)}, bf16[3,72,1024]{2,1,0:T(8,128)(2,1)}, u32[]{:S(2)}, u32[]{:S(2)}) %collective-permute-start.14) | collective-permute-done | bytes 442400 | tf_op jit(solution)/shard_map/ppermute | solution.py:140
  75.1 1.8 shard_map.89
  78.0 1.6 collective-permute-start.19
  79.6 1.5 pad_maximum_fusion
  81.2 1.5 fusion.52
  82.8 3.8 %collective-permute-done.15 = bf16[3,72,1024]{2,1,0:T(8,128)(2,1)S(1)} collective-permute-done((bf16[3,72,1024]{2,1,0:T(8,128)(2,1)S(1)}, bf16[3,72,1024]{2,1,0:T(8,128)(2,1)S(1)}, u32[]{:S(2)}, u32[]{:S(2)}) %collective-permute-start.15) | collective-permute-done | bytes 442400 | tf_op jit(solution)/shard_map/ppermute | solution.py:140
  86.5 3.7 %collective-permute-done.17 = bf16[3,72,1024]{2,1,0:T(8,128)(2,1)S(1)} collective-permute-done((bf16[3,72,1024]{2,1,0:T(8,128)(2,1)S(1)}, bf16[3,72,1024]{2,1,0:T(8,128)(2,1)S(1)}, u32[]{:S(2)}, u32[]{:S(2)}) %collective-permute-start.17) | collective-permute-done | bytes 442400 | tf_op jit(solution)/shard_map/ppermute | solution.py:140
  90.2 4.7 %collective-permute-done.19 = bf16[3,72,1024]{2,1,0:T(8,128)(2,1)S(1)} collective-permute-done((bf16[3,72,1024]{2,1,0:T(8,128)(2,1)S(1)}, bf16[3,72,1024]{2,1,0:T(8,128)(2,1)S(1)}, u32[]{:S(2)}, u32[]{:S(2)}) %collective-permute-start.19) | collective-permute-done | bytes 442400 | tf_op jit(solution)/shard_map/ppermute | solution.py:140
  96.3 1.5 fusion.54
  97.9 1.5 fusion.53
  100.5 2.3 %collective-permute-start.18 = (bf16[1,72,2048]{2,1,0:T(8,128)(2,1)}, bf16[1,72,2048]{2,1,0:T(8,128)(2,1)S(1)}, u32[]{:S(2)}, u32[]{:S(2)}) collective-permute-start(bf16[1,72,2048]{2,1,0:T(8,128)(2,1)} %get-tuple-element.90), channel_id=1, source_target_pairs={{0,4},{2,6},{4,0},{6,2},{8,12},{10,14},{12,8},{14,10},{16,20},{18,... | collective-permute-start | bytes 884744 | tf_op jit(solution)/shard_map/ppermute | solution.py:140
  102.9 1.9 multiply_convert_fusion
  105.9 3.1 %convolution_convert_fusion.1 = bf16[864,1024]{1,0:T(8,128)(2,1)S(1)} fusion(bf16[864,768]{1,0:T(8,128)(2,1)S(1)} %multiply_convert_fusion, bf16[1024,768]{1,0:T(8,128)(2,1)} %copy-done.23), kind=kOutput, calls=%fused_computation.19 | convolution fusion | flops 1359839232 | bytes 4669440 | tf_op jit(solution)/shard_map/dot_general | solution.py:220
  109.1 2.4 %shard_map.90 = (bf16[3,72,1024]{2,1,0:T(8,128)(2,1)S(1)}, bf16[3,72,1024]{2,1,0:T(8,128)(2,1)}, bf16[3,72,1024]{2,1,0:T(8,128)(2,1)}, bf16[3,72,1024]{2,1,0:T(8,128)(2,1)}) custom-call(s32[3]{0:T(128)S(1)} %slice.106._, f32[12,128]{1,0:T(8,128)S(1)} %reshape.98.pos_ref, f32[12,128]{1,0:T(8,128)S(1)} %reshape.99.weight_ref, ...), custom_call_target="tpu_custom_call" | custom-call | flops 226492416 | bytes 2555904 | tf_op jit(solution)/shard_map/pallas_call | solution.py:59
  111.7 1.2 collective-permute-start.21
  112.9 2.0 collective-permute-done.18.refs_2_
  115.0 2.4 %collective-permute-start.22 = (bf16[3,72,1024]{2,1,0:T(8,128)(2,1)S(1)}, bf16[3,72,1024]{2,1,0:T(8,128)(2,1)S(1)}, u32[]{:S(2)}, u32[]{:S(2)}) collective-permute-start(bf16[3,72,1024]{2,1,0:T(8,128)(2,1)S(1)} %bitcast.121), channel_id=1, source_target_pairs={{0,4},{2,6},{4,0},{6,2},{8,12},{10,14},{12,8},{14,10},{16,20},{18,... | collective-permute-start | bytes 1327112 | tf_op jit(solution)/shard_map/ppermute | solution.py:140
  117.4 1.6 convolution_convert_fusion
  120.1 15.4 %collective-permute-done.22.refs_6_ = bf16[3,72,1024]{2,1,0:T(8,128)(2,1)S(1)} collective-permute-done((bf16[3,72,1024]{2,1,0:T(8,128)(2,1)S(1)}, bf16[3,72,1024]{2,1,0:T(8,128)(2,1)S(1)}, u32[]{:S(2)}, u32[]{:S(2)}) %collective-permute-start.22) | collective-permute-done | bytes 442400 | tf_op jit(solution)/shard_map/ppermute | solution.py:140
  135.4 3.5 %shard_map.91 = bf16[4,128,1024]{2,1,0:T(8,128)(2,1)} custom-call(s32[4]{0:T(128)S(1)} %and_select_fusion._, f32[16,128]{1,0:T(8,128)S(1)} %bitcast.103, f32[16,128]{1,0:T(8,128)S(1)} %bitcast.105, bf16[1,72,2048]{2,1,0:T(8,128)(2,1)S(1)} %get-tuple-element.151.refs_0_, bf16[1,72,2048]{2,1,0:T(8,128)(2,1)S(1)} %collective-permute-done.16.refs_1_, ...), custom_call_target="tpu_custom_call" | custom-call | flops 603979776 | bytes 3407872 | tf_op jit(solution)/shard_map/pallas_call | solution.py:105
  140.6 2.3 %collective-permute-start.25 = (bf16[3,72,1024]{2,1,0:T(8,128)(2,1)}, bf16[3,72,1024]{2,1,0:T(8,128)(2,1)S(1)}, u32[]{:S(2)}, u32[]{:S(2)}) collective-permute-start(bf16[3,72,1024]{2,1,0:T(8,128)(2,1)} %bitcast.37), channel_id=1, source_target_pairs={{0,4},{2,6},{4,0},{6,2},{8,12},{10,14},{12,8},{14,10},{16,20},{18,... | collective-permute-start | bytes 1327112 | tf_op jit(solution)/shard_map/ppermute | solution.py:140
  144.0 1.7 fusion.22
  145.8 1.8 fusion.24
  147.5 14.6 %collective-permute-done.26.refs_7_ = bf16[3,72,1024]{2,1,0:T(8,128)(2,1)S(1)} collective-permute-done((bf16[3,72,1024]{2,1,0:T(8,128)(2,1)S(1)}, bf16[3,72,1024]{2,1,0:T(8,128)(2,1)S(1)}, u32[]{:S(2)}, u32[]{:S(2)}) %collective-permute-start.26) | collective-permute-done | bytes 442400 | tf_op jit(solution)/shard_map/ppermute | solution.py:140
  162.1 1.5 collective-permute-start.28
  164.8 1.7 fusion.26
  167.7 1.6 shard_map.93
  170.9 1.8 fusion.28
  172.7 3.5 %shard_map.92 = bf16[4,128,1024]{2,1,0:T(8,128)(2,1)} custom-call(s32[4]{0:T(128)S(1)} %and_select_fusion._, f32[16,128]{1,0:T(8,128)S(1)} %bitcast.104, f32[16,128]{1,0:T(8,128)S(1)} %bitcast.106, bf16[1,72,2048]{2,1,0:T(8,128)(2,1)S(1)} %get-tuple-element.151.refs_0_, bf16[1,72,2048]{2,1,0:T(8,128)(2,1)S(1)} %collective-permute-done.16.refs_1_, ...), custom_call_target="tpu_custom_call" | custom-call | flops 603979776 | bytes 3407872 | tf_op jit(solution)/shard_map/pallas_call | solution.py:105
  176.4 8.2 %collective-permute-done.28 = bf16[3,72,1024]{2,1,0:T(8,128)(2,1)} collective-permute-done((bf16[3,72,1024]{2,1,0:T(8,128)(2,1)}, bf16[3,72,1024]{2,1,0:T(8,128)(2,1)}, u32[]{:S(2)}, u32[]{:S(2)}) %collective-permute-start.28) | collective-permute-done | bytes 442400 | tf_op jit(solution)/shard_map/ppermute | solution.py:140
  184.6 2.7 %collective-permute-start.32 = (bf16[3,72,1024]{2,1,0:T(8,128)(2,1)}, bf16[3,72,1024]{2,1,0:T(8,128)(2,1)S(1)}, u32[]{:S(2)}, u32[]{:S(2)}) collective-permute-start(bf16[3,72,1024]{2,1,0:T(8,128)(2,1)} %copy-done.9), channel_id=1, source_target_pairs={{0,4},{2,6},{4,0},{6,2},{8,12},{10,14},{12,8},{14,10},{16,20},{18,... | collective-permute-start | bytes 1327112 | tf_op jit(solution)/shard_map/ppermute | solution.py:140
  188.0 1.7 pad_maximum_fusion.2
  191.8 12.0 %collective-permute-done.32 = bf16[3,72,1024]{2,1,0:T(8,128)(2,1)S(1)} collective-permute-done((bf16[3,72,1024]{2,1,0:T(8,128)(2,1)}, bf16[3,72,1024]{2,1,0:T(8,128)(2,1)S(1)}, u32[]{:S(2)}, u32[]{:S(2)}) %collective-permute-start.32) | collective-permute-done | bytes 442400 | tf_op jit(solution)/shard_map/ppermute | solution.py:140
  210.7 1.2 maximum_bitcast_fusion
  212.0 1.9 pad_maximum_fusion.6
  (194 shorter events, 47.6 us)
Async XLA Ops:
  7.2 11.0 %copy-start.4 = (bf16[128,2048]{1,0:T(8,128)(2,1)S(1)}, bf16[128,2048]{1,0:T(8,128)(2,1)}, u32[]{:S(2)}) copy-start(bf16[128,2048]{1,0:T(8,128)(2,1)} %param.7) | copy-start | bytes 1572868
  7.2 37.8 %all-gather.11.cloned.1.call-start = ((), (), s32[]{:S(2)}) async-start(), calls=%async_computation.5 | async-start | bytes 1310720 | tf_op jit(solution)/shard_map/all_gather | solution.py:170
  9.2 59.5 %all-gather.9.cloned.1.call-start = ((), (), s32[]{:S(2)}) async-start(), calls=%async_computation.4 | async-start | bytes 1310720 | tf_op jit(solution)/shard_map/all_gather | solution.py:170
  10.0 94.9 %all-gather.13.cloned.1.call-start = ((), (), s32[]{:S(2)}) async-start(), calls=%async_computation.6 | async-start | bytes 1310720 | tf_op jit(solution)/shard_map/all_gather | solution.py:170
  10.0 32.3 %collective-permute-start.6 = (bf16[1024,768]{1,0:T(8,128)(2,1)}, bf16[1024,768]{1,0:T(8,128)(2,1)}, u32[]{:S(2)}, u32[]{:S(2)}) collective-permute-start(bf16[1024,768]{1,0:T(8,128)(2,1)} %bitcast.116), channel_id=1, source_target_pairs={{0,1},{1,0},{2,3},{3,2},{4,5},{5,4},{6,7},{7,6},{8,9},{9,8},{10,11... | collective-permute-start | bytes 4718600 | tf_op jit(solution)/shard_map/ppermute | solution.py:143
  11.6 154.9 %all-gather.15.cloned.1.call-start = ((), (), s32[]{:S(2)}) async-start(), calls=%async_computation.7 | async-start | bytes 1310720 | tf_op jit(solution)/shard_map/all_gather | solution.py:170
  11.8 3.2 %collective-permute-start.2 = (f32[2,16,128]{2,1,0:T(8,128)S(1)}, f32[2,16,128]{2,1,0:T(8,128)S(1)}, u32[]{:S(2)}, u32[]{:S(2)}) collective-permute-start(f32[2,16,128]{2,1,0:T(8,128)S(1)} %get-tuple-element.163), channel_id=1, source_target_pairs={{0,24},{2,26},{4,28},{6,30},{8,0},{10,2},{12,4},{14,6},{16,8},{18,... | collective-permute-start | bytes 49160 | tf_op jit(solution)/shard_map/ppermute | solution.py:137
  11.8 5.5 %collective-permute-start.1 = (f32[2,16,128]{2,1,0:T(8,128)S(1)}, f32[2,16,128]{2,1,0:T(8,128)S(1)}, u32[]{:S(2)}, u32[]{:S(2)}) collective-permute-start(f32[2,16,128]{2,1,0:T(8,128)S(1)} %get-tuple-element.163), channel_id=1, source_target_pairs={{0,16},{2,18},{4,20},{6,22},{8,24},{10,26},{12,28},{14,30},{16,0},... | collective-permute-start | bytes 49160 | tf_op jit(solution)/shard_map/ppermute | solution.py:137
  14.3 30.7 %collective-permute-start.7 = (bf16[1024,768]{1,0:T(8,128)(2,1)}, bf16[1024,768]{1,0:T(8,128)(2,1)}, u32[]{:S(2)}, u32[]{:S(2)}) collective-permute-start(bf16[1024,768]{1,0:T(8,128)(2,1)} %bitcast.17), channel_id=1, source_target_pairs={{0,1},{1,0},{2,3},{3,2},{4,5},{5,4},{6,7},{7,6},{8,9},{9,8},{10,11... | collective-permute-start | bytes 4718600 | tf_op jit(solution)/shard_map/ppermute | solution.py:143
  14.9 30.1 %collective-permute-start.8 = (bf16[1024,768]{1,0:T(8,128)(2,1)}, bf16[1024,768]{1,0:T(8,128)(2,1)}, u32[]{:S(2)}, u32[]{:S(2)}) collective-permute-start(bf16[1024,768]{1,0:T(8,128)(2,1)} %bitcast.18), channel_id=1, source_target_pairs={{0,1},{1,0},{2,3},{3,2},{4,5},{5,4},{6,7},{7,6},{8,9},{9,8},{10,11... | collective-permute-start | bytes 4718600 | tf_op jit(solution)/shard_map/ppermute | solution.py:143
  15.1 3.1 %collective-permute-start = (f32[2,16,128]{2,1,0:T(8,128)S(1)}, f32[2,16,128]{2,1,0:T(8,128)S(1)}, u32[]{:S(2)}, u32[]{:S(2)}) collective-permute-start(f32[2,16,128]{2,1,0:T(8,128)S(1)} %get-tuple-element.163), channel_id=1, source_target_pairs={{0,8},{2,10},{4,12},{6,14},{8,16},{10,18},{12,20},{14,22},{16,24},... | collective-permute-start | bytes 49160 | tf_op jit(solution)/shard_map/ppermute | solution.py:137
  19.3 7.2 %collective-permute-start.3 = (bf16[1,72,2048]{2,1,0:T(8,128)(2,1)S(1)}, bf16[1,72,2048]{2,1,0:T(8,128)(2,1)S(1)}, u32[]{:S(2)}, u32[]{:S(2)}) collective-permute-start(bf16[1,72,2048]{2,1,0:T(8,128)(2,1)S(1)} %get-tuple-element.68), channel_id=1, source_target_pairs={{0,2},{2,0},{4,6},{6,4},{8,10},{10,8},{12,14},{14,12},{16,18},{18,... | collective-permute-start | bytes 884744 | tf_op jit(solution)/shard_map/ppermute | solution.py:140
  21.3 190.6 %reduce-scatter.3.cloned.1.call-start = ((), (), s32[]{:S(2)}) async-start(), calls=%async_computation.2 | async-start | bytes 1310720 | tf_op jit(solution)/shard_map/reduce_scatter | solution.py:250
  21.4 19.7 %collective-permute-start.5 = (bf16[1,72,2048]{2,1,0:T(8,128)(2,1)S(1)}, bf16[1,72,2048]{2,1,0:T(8,128)(2,1)}, u32[]{:S(2)}, u32[]{:S(2)}) collective-permute-start(bf16[1,72,2048]{2,1,0:T(8,128)(2,1)S(1)} %get-tuple-element.70), channel_id=1, source_target_pairs={{0,6},{2,4},{4,2},{6,0},{8,14},{10,12},{12,10},{14,8},{16,22},{18,... | collective-permute-start | bytes 884744 | tf_op jit(solution)/shard_map/ppermute | solution.py:140
  26.6 13.4 %collective-permute-start.4 = (bf16[1,72,2048]{2,1,0:T(8,128)(2,1)S(1)}, bf16[1,72,2048]{2,1,0:T(8,128)(2,1)}, u32[]{:S(2)}, u32[]{:S(2)}) collective-permute-start(bf16[1,72,2048]{2,1,0:T(8,128)(2,1)S(1)} %get-tuple-element.69), channel_id=1, source_target_pairs={{0,4},{2,6},{4,0},{6,2},{8,12},{10,14},{12,8},{14,10},{16,20},{18,... | collective-permute-start | bytes 884744 | tf_op jit(solution)/shard_map/ppermute | solution.py:140
  40.0 7.9 %collective-permute-start.9 = (bf16[1,72,2048]{2,1,0:T(8,128)(2,1)S(1)}, bf16[1,72,2048]{2,1,0:T(8,128)(2,1)S(1)}, u32[]{:S(2)}, u32[]{:S(2)}) collective-permute-start(bf16[1,72,2048]{2,1,0:T(8,128)(2,1)S(1)} %get-tuple-element.74), channel_id=1, source_target_pairs={{0,2},{2,0},{4,6},{6,4},{8,10},{10,8},{12,14},{14,12},{16,18},{18,... | collective-permute-start | bytes 884744 | tf_op jit(solution)/shard_map/ppermute | solution.py:140
  41.1 8.6 %collective-permute-start.11 = (bf16[1,72,2048]{2,1,0:T(8,128)(2,1)S(1)}, bf16[1,72,2048]{2,1,0:T(8,128)(2,1)}, u32[]{:S(2)}, u32[]{:S(2)}) collective-permute-start(bf16[1,72,2048]{2,1,0:T(8,128)(2,1)S(1)} %get-tuple-element.78), channel_id=1, source_target_pairs={{0,4},{2,6},{4,0},{6,2},{8,12},{10,14},{12,8},{14,10},{16,20},{18,... | collective-permute-start | bytes 884744 | tf_op jit(solution)/shard_map/ppermute | solution.py:140
  42.4 12.5 %collective-permute-start.13 = (bf16[1,72,2048]{2,1,0:T(8,128)(2,1)S(1)}, bf16[1,72,2048]{2,1,0:T(8,128)(2,1)}, u32[]{:S(2)}, u32[]{:S(2)}) collective-permute-start(bf16[1,72,2048]{2,1,0:T(8,128)(2,1)S(1)} %get-tuple-element.82), channel_id=1, source_target_pairs={{0,6},{2,4},{4,2},{6,0},{8,14},{10,12},{12,10},{14,8},{16,22},{18,... | collective-permute-start | bytes 884744 | tf_op jit(solution)/shard_map/ppermute | solution.py:140
  46.3 9.2 %copy-start.20 = (bf16[1,1024,768]{2,1,0:T(8,128)(2,1)S(1)}, bf16[1,1024,768]{2,1,0:T(8,128)(2,1)}, u32[]{:S(2)}) copy-start(bf16[1,1024,768]{2,1,0:T(8,128)(2,1)} %param.11) | copy-start | bytes 4718596
  48.6 20.1 %collective-permute-start.10 = (bf16[3,72,1024]{2,1,0:T(8,128)(2,1)S(1)}, bf16[3,72,1024]{2,1,0:T(8,128)(2,1)S(1)}, u32[]{:S(2)}, u32[]{:S(2)}) collective-permute-start(bf16[3,72,1024]{2,1,0:T(8,128)(2,1)S(1)} %get-tuple-element.75), channel_id=1, source_target_pairs={{0,2},{2,0},{4,6},{6,4},{8,10},{10,8},{12,14},{14,12},{16,18},{18,... | collective-permute-start | bytes 1327112 | tf_op jit(solution)/shard_map/ppermute | solution.py:140
  49.7 18.9 %collective-permute-start.12 = (bf16[3,72,1024]{2,1,0:T(8,128)(2,1)S(1)}, bf16[3,72,1024]{2,1,0:T(8,128)(2,1)}, u32[]{:S(2)}, u32[]{:S(2)}) collective-permute-start(bf16[3,72,1024]{2,1,0:T(8,128)(2,1)S(1)} %get-tuple-element.79), channel_id=1, source_target_pairs={{0,4},{2,6},{4,0},{6,2},{8,12},{10,14},{12,8},{14,10},{16,20},{18,... | collective-permute-start | bytes 1327112 | tf_op jit(solution)/shard_map/ppermute | solution.py:140
  54.8 19.0 %collective-permute-start.14 = (bf16[3,72,1024]{2,1,0:T(8,128)(2,1)S(1)}, bf16[3,72,1024]{2,1,0:T(8,128)(2,1)}, u32[]{:S(2)}, u32[]{:S(2)}) collective-permute-start(bf16[3,72,1024]{2,1,0:T(8,128)(2,1)S(1)} %get-tuple-element.83), channel_id=1, source_target_pairs={{0,6},{2,4},{4,2},{6,0},{8,14},{10,12},{12,10},{14,8},{16,22},{18,... | collective-permute-start | bytes 1327112 | tf_op jit(solution)/shard_map/ppermute | solution.py:140
  76.8 9.7 %collective-permute-start.15 = (bf16[3,72,1024]{2,1,0:T(8,128)(2,1)S(1)}, bf16[3,72,1024]{2,1,0:T(8,128)(2,1)S(1)}, u32[]{:S(2)}, u32[]{:S(2)}) collective-permute-start(bf16[3,72,1024]{2,1,0:T(8,128)(2,1)S(1)} %get-tuple-element.86), channel_id=1, source_target_pairs={{0,2},{2,0},{4,6},{6,4},{8,10},{10,8},{12,14},{14,12},{16,18},{18,... | collective-permute-start | bytes 1327112 | tf_op jit(solution)/shard_map/ppermute | solution.py:140
  78.0 12.3 %collective-permute-start.17 = (bf16[3,72,1024]{2,1,0:T(8,128)(2,1)S(1)}, bf16[3,72,1024]{2,1,0:T(8,128)(2,1)S(1)}, u32[]{:S(2)}, u32[]{:S(2)}) collective-permute-start(bf16[3,72,1024]{2,1,0:T(8,128)(2,1)S(1)} %get-tuple-element.89), channel_id=1, source_target_pairs={{0,4},{2,6},{4,0},{6,2},{8,12},{10,14},{12,8},{14,10},{16,20},{18,... | collective-permute-start | bytes 1327112 | tf_op jit(solution)/shard_map/ppermute | solution.py:140
  78.0 16.9 %collective-permute-start.19 = (bf16[3,72,1024]{2,1,0:T(8,128)(2,1)S(1)}, bf16[3,72,1024]{2,1,0:T(8,128)(2,1)S(1)}, u32[]{:S(2)}, u32[]{:S(2)}) collective-permute-start(bf16[3,72,1024]{2,1,0:T(8,128)(2,1)S(1)} %get-tuple-element.92), channel_id=1, source_target_pairs={{0,6},{2,4},{4,2},{6,0},{8,14},{10,12},{12,10},{14,8},{16,22},{18,... | collective-permute-start | bytes 1327112 | tf_op jit(solution)/shard_map/ppermute | solution.py:140
  97.9 5.0 %copy-start.36 = (bf16[1,72,2048]{2,1,0:T(8,128)(2,1)S(1)}, bf16[1,72,2048]{2,1,0:T(8,128)(2,1)}, u32[]{:S(2)}) copy-start(bf16[1,72,2048]{2,1,0:T(8,128)(2,1)} %get-tuple-element.93) | copy-start | bytes 884740
  99.4 12.2 %collective-permute-start.16 = (bf16[1,72,2048]{2,1,0:T(8,128)(2,1)}, bf16[1,72,2048]{2,1,0:T(8,128)(2,1)S(1)}, u32[]{:S(2)}, u32[]{:S(2)}) collective-permute-start(bf16[1,72,2048]{2,1,0:T(8,128)(2,1)} %get-tuple-element.87), channel_id=1, source_target_pairs={{0,2},{2,0},{4,6},{6,4},{8,10},{10,8},{12,14},{14,12},{16,18},{18,... | collective-permute-start | bytes 884744 | tf_op jit(solution)/shard_map/ppermute | solution.py:140
  100.5 14.4 %collective-permute-start.18 = (bf16[1,72,2048]{2,1,0:T(8,128)(2,1)}, bf16[1,72,2048]{2,1,0:T(8,128)(2,1)S(1)}, u32[]{:S(2)}, u32[]{:S(2)}) collective-permute-start(bf16[1,72,2048]{2,1,0:T(8,128)(2,1)} %get-tuple-element.90), channel_id=1, source_target_pairs={{0,4},{2,6},{4,0},{6,2},{8,12},{10,14},{12,8},{14,10},{16,20},{18,... | collective-permute-start | bytes 884744 | tf_op jit(solution)/shard_map/ppermute | solution.py:140
  102.9 14.5 %collective-permute-start.20 = (bf16[1,72,2048]{2,1,0:T(8,128)(2,1)S(1)}, bf16[1,72,2048]{2,1,0:T(8,128)(2,1)S(1)}, u32[]{:S(2)}, u32[]{:S(2)}) collective-permute-start(bf16[1,72,2048]{2,1,0:T(8,128)(2,1)S(1)} %copy-done.36), channel_id=1, source_target_pairs={{0,6},{2,4},{4,2},{6,0},{8,14},{10,12},{12,10},{14,8},{16,22},{18,... | collective-permute-start | bytes 884744 | tf_op jit(solution)/shard_map/ppermute | solution.py:140
  111.5 5.9 %copy-start.22 = (bf16[1024,768]{1,0:T(8,128)(2,1)S(1)}, bf16[1024,768]{1,0:T(8,128)(2,1)}, u32[]{:S(2)}) copy-start(bf16[1024,768]{1,0:T(8,128)(2,1)} %copy-done.21) | copy-start | bytes 4718596
  111.5 5.9 %copy-start.41 = (bf16[864,768]{1,0:T(8,128)(2,1)S(1)}, bf16[864,768]{1,0:T(8,128)(2,1)}, u32[]{:S(2)}) copy-start(bf16[864,768]{1,0:T(8,128)(2,1)} %copy-done.40) | copy-start | bytes 3981316
  111.7 8.4 %collective-permute-start.21 = (bf16[3,72,1024]{2,1,0:T(8,128)(2,1)S(1)}, bf16[3,72,1024]{2,1,0:T(8,128)(2,1)S(1)}, u32[]{:S(2)}, u32[]{:S(2)}) collective-permute-start(bf16[3,72,1024]{2,1,0:T(8,128)(2,1)S(1)} %bitcast.122), channel_id=1, source_target_pairs={{0,2},{2,0},{4,6},{6,4},{8,10},{10,8},{12,14},{14,12},{16,18},{18,... | collective-permute-start | bytes 1327112 | tf_op jit(solution)/shard_map/ppermute | solution.py:140
  115.0 20.5 %collective-permute-start.22 = (bf16[3,72,1024]{2,1,0:T(8,128)(2,1)S(1)}, bf16[3,72,1024]{2,1,0:T(8,128)(2,1)S(1)}, u32[]{:S(2)}, u32[]{:S(2)}) collective-permute-start(bf16[3,72,1024]{2,1,0:T(8,128)(2,1)S(1)} %bitcast.121), channel_id=1, source_target_pairs={{0,4},{2,6},{4,0},{6,2},{8,12},{10,14},{12,8},{14,10},{16,20},{18,... | collective-permute-start | bytes 1327112 | tf_op jit(solution)/shard_map/ppermute | solution.py:140
  117.4 18.1 %collective-permute-start.23 = (bf16[3,72,1024]{2,1,0:T(8,128)(2,1)S(1)}, bf16[3,72,1024]{2,1,0:T(8,128)(2,1)S(1)}, u32[]{:S(2)}, u32[]{:S(2)}) collective-permute-start(bf16[3,72,1024]{2,1,0:T(8,128)(2,1)S(1)} %bitcast.120), channel_id=1, source_target_pairs={{0,6},{2,4},{4,2},{6,0},{8,14},{10,12},{12,10},{14,8},{16,22},{18,... | collective-permute-start | bytes 1327112 | tf_op jit(solution)/shard_map/ppermute | solution.py:140
  138.9 73.1 %reduce-scatter.5.cloned.1.call-start = ((), (), s32[]{:S(2)}) async-start(), calls=%async_computation.3 | async-start | bytes 1310720 | tf_op jit(solution)/shard_map/reduce_scatter | solution.py:250
  140.5 24.2 %copy-start.16 = (bf16[288,1024]{1,0:T(8,128)(2,1)}, bf16[288,1024]{1,0:T(8,128)(2,1)S(1)}, u32[]{:S(2)}) copy-start(bf16[288,1024]{1,0:T(8,128)(2,1)S(1)} %get-tuple-element.146) | copy-start | bytes 1769476
  140.5 23.1 %collective-permute-start.24 = (bf16[3,72,1024]{2,1,0:T(8,128)(2,1)}, bf16[3,72,1024]{2,1,0:T(8,128)(2,1)S(1)}, u32[]{:S(2)}, u32[]{:S(2)}) collective-permute-start(bf16[3,72,1024]{2,1,0:T(8,128)(2,1)} %bitcast.36), channel_id=1, source_target_pairs={{0,2},{2,0},{4,6},{6,4},{8,10},{10,8},{12,14},{14,12},{16,18},{18,... | collective-permute-start | bytes 1327112 | tf_op jit(solution)/shard_map/ppermute | solution.py:140
  140.6 21.5 %collective-permute-start.25 = (bf16[3,72,1024]{2,1,0:T(8,128)(2,1)}, bf16[3,72,1024]{2,1,0:T(8,128)(2,1)S(1)}, u32[]{:S(2)}, u32[]{:S(2)}) collective-permute-start(bf16[3,72,1024]{2,1,0:T(8,128)(2,1)} %bitcast.37), channel_id=1, source_target_pairs={{0,4},{2,6},{4,0},{6,2},{8,12},{10,14},{12,8},{14,10},{16,20},{18,... | collective-permute-start | bytes 1327112 | tf_op jit(solution)/shard_map/ppermute | solution.py:140
  142.9 19.2 %collective-permute-start.26 = (bf16[3,72,1024]{2,1,0:T(8,128)(2,1)S(1)}, bf16[3,72,1024]{2,1,0:T(8,128)(2,1)S(1)}, u32[]{:S(2)}, u32[]{:S(2)}) collective-permute-start(bf16[3,72,1024]{2,1,0:T(8,128)(2,1)S(1)} %bitcast.119), channel_id=1, source_target_pairs={{0,6},{2,4},{4,2},{6,0},{8,14},{10,12},{12,10},{14,8},{16,22},{18,... | collective-permute-start | bytes 1327112 | tf_op jit(solution)/shard_map/ppermute | solution.py:140
  162.1 14.1 %collective-permute-start.29 = (bf16[3,72,1024]{2,1,0:T(8,128)(2,1)}, bf16[3,72,1024]{2,1,0:T(8,128)(2,1)}, u32[]{:S(2)}, u32[]{:S(2)}) collective-permute-start(bf16[3,72,1024]{2,1,0:T(8,128)(2,1)} %get-tuple-element.122), channel_id=1, source_target_pairs={{0,6},{2,4},{4,2},{6,0},{8,14},{10,12},{12,10},{14,8},{16,22},{18,... | collective-permute-start | bytes 1327112 | tf_op jit(solution)/shard_map/ppermute | solution.py:140
  162.1 22.5 %collective-permute-start.28 = (bf16[3,72,1024]{2,1,0:T(8,128)(2,1)}, bf16[3,72,1024]{2,1,0:T(8,128)(2,1)}, u32[]{:S(2)}, u32[]{:S(2)}) collective-permute-start(bf16[3,72,1024]{2,1,0:T(8,128)(2,1)} %get-tuple-element.121), channel_id=1, source_target_pairs={{0,4},{2,6},{4,0},{6,2},{8,12},{10,14},{12,8},{14,10},{16,20},{18,... | collective-permute-start | bytes 1327112 | tf_op jit(solution)/shard_map/ppermute | solution.py:140
  163.6 23.7 %collective-permute-start.27 = (bf16[3,72,1024]{2,1,0:T(8,128)(2,1)}, bf16[3,72,1024]{2,1,0:T(8,128)(2,1)}, u32[]{:S(2)}, u32[]{:S(2)}) collective-permute-start(bf16[3,72,1024]{2,1,0:T(8,128)(2,1)} %get-tuple-element.120), channel_id=1, source_target_pairs={{0,2},{2,0},{4,6},{6,4},{8,10},{10,8},{12,14},{14,12},{16,18},{18,... | collective-permute-start | bytes 1327112 | tf_op jit(solution)/shard_map/ppermute | solution.py:140
  176.2 15.6 %collective-permute-start.33 = (bf16[3,72,1024]{2,1,0:T(8,128)(2,1)}, bf16[3,72,1024]{2,1,0:T(8,128)(2,1)S(1)}, u32[]{:S(2)}, u32[]{:S(2)}) collective-permute-start(bf16[3,72,1024]{2,1,0:T(8,128)(2,1)} %copy-done.10), channel_id=1, source_target_pairs={{0,6},{2,4},{4,2},{6,0},{8,14},{10,12},{12,10},{14,8},{16,22},{18,... | collective-permute-start | bytes 1327112 | tf_op jit(solution)/shard_map/ppermute | solution.py:140
  184.6 19.2 %collective-permute-start.32 = (bf16[3,72,1024]{2,1,0:T(8,128)(2,1)}, bf16[3,72,1024]{2,1,0:T(8,128)(2,1)S(1)}, u32[]{:S(2)}, u32[]{:S(2)}) collective-permute-start(bf16[3,72,1024]{2,1,0:T(8,128)(2,1)} %copy-done.9), channel_id=1, source_target_pairs={{0,4},{2,6},{4,0},{6,2},{8,12},{10,14},{12,8},{14,10},{16,20},{18,... | collective-permute-start | bytes 1327112 | tf_op jit(solution)/shard_map/ppermute | solution.py:140
  187.3 16.5 %collective-permute-start.31 = (bf16[3,72,1024]{2,1,0:T(8,128)(2,1)}, bf16[3,72,1024]{2,1,0:T(8,128)(2,1)S(1)}, u32[]{:S(2)}, u32[]{:S(2)}) collective-permute-start(bf16[3,72,1024]{2,1,0:T(8,128)(2,1)} %copy-done.8), channel_id=1, source_target_pairs={{0,2},{2,0},{4,6},{6,4},{8,10},{10,8},{12,14},{14,12},{16,18},{18,... | collective-permute-start | bytes 1327112 | tf_op jit(solution)/shard_map/ppermute | solution.py:140
  189.7 14.1 %copy-start.7 = (bf16[3,72,1024]{2,1,0:T(8,128)(2,1)S(1)}, bf16[3,72,1024]{2,1,0:T(8,128)(2,1)}, u32[]{:S(2)}) copy-start(bf16[3,72,1024]{2,1,0:T(8,128)(2,1)} %copy-done.6) | copy-start | bytes 1327108
  190.8 18.2 %collective-permute-start.30 = (bf16[512,768]{1,0:T(8,128)(2,1)S(1)}, bf16[512,768]{1,0:T(8,128)(2,1)S(1)}, u32[]{:S(2)}, u32[]{:S(2)}) collective-permute-start(bf16[512,768]{1,0:T(8,128)(2,1)S(1)} %add_convert_fusion.3), channel_id=1, source_target_pairs={{0,1},{1,0},{2,3},{3,2},{4,5},{5,4},{6,7},{7,6},{8,9},{9,8},{10,11... | collective-permute-start | bytes 2359304 | tf_op jit(solution)/shard_map/ppermute | solution.py:143
  206.2 3.4 %collective-permute-start.34 = (bf16[512,768]{1,0:T(8,128)(2,1)S(1)}, bf16[512,768]{1,0:T(8,128)(2,1)S(1)}, u32[]{:S(2)}, u32[]{:S(2)}) collective-permute-start(bf16[512,768]{1,0:T(8,128)(2,1)S(1)} %add_convert_fusion.1), channel_id=1, source_target_pairs={{0,1},{1,0},{2,3},{3,2},{4,5},{5,4},{6,7},{7,6},{8,9},{9,8},{10,11... | collective-permute-start | bytes 2359304 | tf_op jit(solution)/shard_map/ppermute | solution.py:143
  (36 other events, 77.9 us)
Sparse Core Ops, SparseCore 0:
  9.6 28.8 all-gather.10
  40.0 27.5 all-gather.8
  69.2 27.4 all-gather.12
  98.1 27.4 all-gather.14
  139.0 25.5 reduce-scatter.2
  176.4 25.5 reduce-scatter.4

commit v4 on v3

--- a/solution.py
+++ b/solution.py
@@ -122,6 +122,144 @@
     )(which, pos, weight, *own, *rest)
 
 
+def place_kernel(a_ref, b_ref, *refs):
+    refs[-1][...] = (a_ref[...] + b_ref[...].astype(F32)).astype(BF16)
+
+
+def place_sum(a, b, at, count, base):
+    rows, cols = a.shape
+    block = pl.BlockSpec((rows, cols), lambda i: (0, 0))
+    given = [a, b] if base is None else [a, b, base]
+    return pl.pallas_call(
+        place_kernel,
+        grid=(1,),
+        in_specs=[block, block, pl.BlockSpec(memory_space=pl.ANY)][: len(given)],
+        out_specs=pl.BlockSpec((rows, cols), lambda i: (at, 0)),
+        out_shape=jax.ShapeDtypeStruct((count * rows, cols), BF16),
+        input_output_aliases={} if base is None else {2: 0},
+        compiler_params=pltpu.CompilerParams(vmem_limit_bytes=VMEM_LIMIT),
+        cost_estimate=pl.CostEstimate(
+            flops=rows * cols, bytes_accessed=8 * rows * cols, transcendentals=0
+        ),
+    )(*given)
+
+
+def expert_kernel(peers, parts, held, mats, halves, joined_out, *refs):
+    take = iter(refs)
+    rows = [[next(take) for _ in range(peers)] for _ in range(parts)]
+    gates, ups = ([next(take) for _ in range(mats)] for _ in range(2))
+    before = [next(take) for _ in range(2)] if held else None
+    downs = [next(take) for _ in range(halves)]
+    outs = list(take)
+    count, slots = rows[0][0].shape[:2]
+    pieces = []
+    for part in rows:
+        stacked = jnp.concatenate([x[g] for x in part for g in range(count)], axis=0)
+        deep = gates[0].shape[0]
+        pieces += [stacked[:, at : at + deep] for at in range(0, stacked.shape[1], deep)]
+    sums = []
+    for i, mats in enumerate((gates, ups)):
+        total = before[i][...] if before else None
+        for x, w in zip(pieces, mats):
+            part = jnp.dot(x, w[...], preferred_element_type=F32)
+            total = part if total is None else total + part
+        sums.append(total)
+    if not halves:
+        outs[0][...], outs[1][...] = sums
+        return
+    wider = sums[0] / (1.0 + jnp.exp(-sums[0])) * sums[1]
+    for i in range(peers * count):
+        outs[0][i] = wider[i * slots : (i + 1) * slots].astype(BF16)
+    project(peers, count, slots, wider.astype(BF16), downs, outs[1:], joined_out)
+
+
+def project(peers, count, slots, hidden, downs, outs, joined_out):
+    for h, w in enumerate(downs):
+        wide = w.shape[0]
+        out = lax.dot_general(
+            hidden, w[...], (((1,), (1,)), ((), ())), preferred_element_type=F32
+        )
+        for k in range(peers):
+            for g in range(count):
+                at = (k * count + g) * slots
+                block = out[at : at + slots].astype(BF16)
+                if joined_out:
+                    outs[k][g, :, h * wide : (h + 1) * wide] = block
+                else:
+                    outs[k][g] = block
+
+
+def project_kernel(peers, count, hidden_ref, down_ref, *outs):
+    slots = hidden_ref.shape[1]
+    hidden = jnp.concatenate([hidden_ref[i] for i in range(peers * count)], axis=0)
+    project(peers, count, slots, hidden, [down_ref], outs, False)
+
+
+def in_vmem(kernel, shapes, flops, *args):
+    vmem = pl.BlockSpec(memory_space=pltpu.VMEM)
+    return pl.pallas_call(
+        kernel,
+        in_specs=[vmem] * len(args),
+        out_specs=[vmem] * len(shapes),
+        out_shape=shapes,
+        compiler_params=pltpu.CompilerParams(vmem_limit_bytes=VMEM_LIMIT),
+        cost_estimate=pl.CostEstimate(
+            flops=flops,
+            bytes_accessed=sum(x.size * x.dtype.itemsize for x in (*args, *shapes)),
+            transcendentals=0,
+        ),
+    )(*args)
+
+
+def expert(rows, gates, ups, held, downs):
+    peers = len(rows[0])
+    count, slots, _ = rows[0][0].shape
+    units = gates[0].shape[1]
+    total = peers * count * slots
+    flops = 4 * total * units * sum(w.shape[0] for w in gates)
+    if not downs:
+        shapes = [jax.ShapeDtypeStruct((total, units), F32)] * 2
+    else:
+        wide = sum(w.shape[0] for w in downs)
+        flops += 2 * total * units * wide
+        shapes = [jax.ShapeDtypeStruct((peers * count, slots, units), BF16)]
+        shapes += [jax.ShapeDtypeStruct((count, slots, wide), BF16)] * peers
+    kernel = functools.partial(
+        expert_kernel, peers, len(rows), bool(held), len(gates), len(downs), len(downs) > 1
+    )
+    return in_vmem(kernel, shapes, flops, *sum(rows, []), *gates, *ups, *held, *downs)
+
+
+def own_grad_kernel(peers, _, hidden_ref, *refs):
+    rows = jnp.concatenate([x[0] for x in refs[:peers]], axis=0)
+    hidden = jnp.concatenate([hidden_ref[k] for k in range(peers)], axis=0)
+    refs[peers][0] = lax.dot_general(
+        rows, hidden, (((0,), (0,)), ((), ())), preferred_element_type=F32
+    )
+
+
+def own_grads(blocks, hidden, rows, piece):
+    peers, slots, units = hidden.shape
+    count = blocks.shape[0]
+    return pl.pallas_call(
+        functools.partial(own_grad_kernel, peers),
+        grid_spec=pltpu.PrefetchScalarGridSpec(
+            num_scalar_prefetch=1,
+            grid=(count,),
+            in_specs=[pl.BlockSpec(hidden.shape, lambda i, ref: (0, 0, 0))]
+            + [pl.BlockSpec((1, slots, piece), lambda i, ref: (0, 0, ref[i]))] * peers,
+            out_specs=pl.BlockSpec((1, piece, units), lambda i, ref: (i, 0, 0)),
+        ),
+        out_shape=jax.ShapeDtypeStruct((count, piece, units), F32),
+        compiler_params=pltpu.CompilerParams(vmem_limit_bytes=VMEM_LIMIT),
+        cost_estimate=pl.CostEstimate(
+            flops=2 * peers * slots * count * piece * units,
+            bytes_accessed=4 * count * piece * units,
+            transcendentals=0,
+        ),
+    )(blocks, hidden, *rows)
+
+
 def shards(tokens, routes, route_logits, cotangent, gate_weight, up_weight, down_weight):
     toks, top = routes.shape
     experts = lax.axis_size("expert")
@@ -198,50 +336,35 @@
             queue[k] = [back[k]]
         return back
 
-    def joined(parts):
-        return jnp.concatenate(parts, axis=0).reshape(-1, parts[0].shape[-1])
-
     def pick_rest(x, scaled):
         tile = column_tile(x.shape[2])
         tiles = list(range(x.shape[2] // tile))
         return select([x] * (major - 1), sender[1:], rest_table, slots, scaled, tiles, tile)
 
-    def hidden_of(pieces):
-        def against(w):
-            total, at = None, 0
-            for x in pieces:
-                part = jnp.dot(x, w[at : at + x.shape[1]], preferred_element_type=F32)
-                total, at = part if total is None else total + part, at + x.shape[1]
-            return total
-
-        return (jax.nn.silu(against(gate_mat)) * against(up_mat)).astype(BF16)
-
-    def out_of(hidden, w):
-        out = lax.dot_general(hidden, w, (((1,), (1,)), ((), ())), preferred_element_type=F32)
-        out = out.astype(BF16).reshape(minor, -1, slots, w.shape[0])
-        return [out[k] for k in range(minor)]
-
     tile = column_tile(model_width)
     got = [other_core(w[0]) for w in (gate_weight, up_weight, down_weight)]
-    gate_mat, up_mat, down_mat = (
-        jnp.concatenate([jnp.where(core == 0, w[0], g), jnp.where(core == 0, g, w[0])], axis=0)
+    gate_mats, up_mats, down_mats = (
+        [jnp.where(core == 0, w[0], g), jnp.where(core == 0, g, w[0])]
         for w, g in zip((gate_weight, up_weight, down_weight), got)
     )
     every = list(range(model_width // tile))
     own_tokens = after(tokens, metas[1:])[None]
     own_rows = exchange(select([own_tokens], zero, own_table, slots, False, every, tile))
-    own_cots = joined(
-        exchange(select([cotangent[None]], zero, own_table, slots, True, [0, 2, 1, 3], piece))
-    )
-    own_hidden = hidden_of([joined(own_rows)])
-    own_out = out_of(own_hidden, down_mat)
+    own_cots = exchange(
+        select([cotangent[None]], zero, own_table, slots, True, [0, 2, 1, 3], piece)
+    )
     first = exchange(pick_rest(after(token_all[0], got), False))
-    second = exchange(pick_rest(after(token_all[1], [*first[1:], *own_out]), False))
-    own_back = exchange(own_out)
-    rest_hidden = hidden_of([joined(first), joined(second)])
-
-    outs = [out_of(rest_hidden, down_mat[h * wide : (h + 1) * wide]) for h in range(2)]
-    cots = [pick_rest(after(cot_all[0], second[1:]), True), None]
+    second = exchange(pick_rest(after(token_all[1], first[1:]), False))
+    own_hidden, *own_out = expert([own_rows], gate_mats, up_mats, [], down_mats)
+    held = expert([first], gate_mats[:1], up_mats[:1], [], [])
+    own_back = exchange(after_all(own_out, held))
+    rest_hidden, *out = expert([second], gate_mats[1:], up_mats[1:], held, down_mats[:1])
+
+    shapes = [jax.ShapeDtypeStruct(x.shape, x.dtype) for x in out]
+    flops = 2 * rest_hidden.size * wide
+    kernel = functools.partial(project_kernel, minor, major - 1)
+    outs = [out, in_vmem(kernel, shapes, flops, rest_hidden, down_mats[1])]
+    cots = [pick_rest(after(cot_all[0], out[1:]), True), None]
     mixed = []
     for h in range(2):
         back = exchange(outs[h] if h else after_all(outs[h], cots[0]))
@@ -251,23 +374,28 @@
         )
     mixed = jnp.concatenate(mixed, axis=1)
     cots[1] = pick_rest(cot_all[1], True)
-    rest_cots = [joined(exchange(x)) for x in cots]
-
-    over_rows = (((0,), (0,)), ((), ()))
-    done = []
+    rest_cots = [exchange(x) for x in cots]
+
+    whose = (1 - core, core)
+    blocks = jnp.stack([2 * h + c for h in range(2) for c in whose]).astype(jnp.int32)
+    own_parts = own_grads(blocks, own_hidden, own_cots, piece)
+    rest_hidden = rest_hidden.reshape(-1, rest_hidden.shape[2])
+    grad = None
     for h in range(2):
-        own_half = own_cots[:, h * 2 * piece : (h + 1) * 2 * piece]
-
-        def grad_of(which):
-            def part(rows, hidden):
-                side = lax.dynamic_slice_in_dim(rows, which * piece, piece, axis=1)
-                return lax.dot_general(side, hidden, over_rows, preferred_element_type=F32)
-
-            return part(own_half, own_hidden) + part(rest_cots[h], rest_hidden)
-
-        theirs = other_core(grad_of(1 - core).astype(BF16))
-        done.append((grad_of(core) + theirs.astype(F32)).astype(BF16))
-    return mixed, jnp.concatenate(done, axis=0)[None]
+        rows = jnp.concatenate(rest_cots[h], axis=0).reshape(-1, wide)
+        theirs, ours = (
+            own_parts[2 * h + i]
+            + lax.dot_general(
+                lax.dynamic_slice_in_dim(rows, c * piece, piece, axis=1),
+                rest_hidden,
+                (((0,), (0,)), ((), ())),
+                preferred_element_type=F32,
+            )
+            for i, c in enumerate(whose)
+        )
+        theirs = other_core(theirs.astype(BF16))
+        grad = place_sum(ours, after(theirs, [mixed] if h else []), h, 2, grad)
+    return mixed, grad[None]
 
 
 def solution(mesh):

time: 222 us -> 201 us (0.905)
  waiting for transfers between devices: 89.7 us -> 55.2 us
  Pallas kernels: 16.6 us -> 48 us
  matrix products: 26 us -> 6.13 us
  starting transfers between devices: 37 us -> 45.3 us
  other arithmetic: 18.7 us -> 13.9 us
  local copies, waits for them, and re-layouts: 18 us -> 15.2 us
    ppermute x27, waiting for transfers between devices: 88 us -> 44.5 us  [to_peer(): return lax.ppermute(x, 'expert', [(i, i ^ k) for i in range(experts)])]
    pallas_call x0 -> x7, Pallas kernels: none -> 31.4 us  [the longest x4 24.5 us: in_vmem(): pl.pallas_call(kernel, in_specs=[vmem] * len(args), out_specs=[vmem] * le...]
    dot_general x17 -> x4, matrix products: 25.8 us -> 6 us  [shards(): lax.dot_general(lax.dynamic_slice_in_dim(rows, c * piece, piece, axis=1),...]
    ppermute x5, starting transfers between devices: 2.96 us -> 12.4 us  [other_core(): return lax.ppermute(x, 'dp', [(0, 1), (1, 0)])]
    all_gather x4, waiting for transfers between devices: 0.04 us -> 9.07 us  [spread(): return lax.all_gather(x, 'expert', axis=0, axis_index_groups=same_place)]
    concatenate x6 -> x2, other arithmetic: 7.11 us -> 0.44 us  [shards(): rows = jnp.concatenate(rest_cots[h], axis=0).reshape(-1, wide)]
    select_n x3, other arithmetic: 5.98 us -> 9.71 us  [shards(): jnp.where(core == 0, g, w[0])]
    unnamed x86 -> x82, local copies, waits for them, and re-layouts: 13.6 us -> 13.2 us
  transfers between devices with their start and end apart: 41 -> 41, of which waited for: 13 -> 13; matrix products, arithmetic and copies ran while one was open for 20% -> 10% of each run, Pallas kernels for 8% -> 24%
where the time goes in v4:
time: 201 us; the launch traced here: 198 us
  waiting for transfers between devices  55.2 us (27%)
  Pallas kernels  48 us (24%)
  starting transfers between devices  45.3 us (23%)
  local copies, waits for them, and re-layouts  15.2 us (8%)
  between operations  14.6 us (7%)
  other arithmetic  13.9 us (7%)
  matrix products  6.13 us (3%)
    ppermute x27, waiting for transfers between devices, to_peer(): return lax.ppermute(x, 'expert', [(i, i ^ k) for i in range(experts)])  44.5 us
    ppermute x27, starting transfers between devices, to_peer(): return lax.ppermute(x, 'expert', [(i, i ^ k) for i in range(experts)])  27.9 us
    pallas_call x4, Pallas kernels, in_vmem(): pl.pallas_call(kernel, in_specs=[vmem] * len(args), out_specs=[vmem] * le...  24.5 us
    unnamed x82, local copies, waits for them, and re-layouts  13.2 us
    ppermute x5, starting transfers between devices, other_core(): return lax.ppermute(x, 'dp', [(0, 1), (1, 0)])  12.4 us
    select_n x3, other arithmetic, shards(): jnp.where(core == 0, g, w[0])  9.71 us
    pallas_call x6, Pallas kernels, select(): pl.pallas_call(functools.partial(select_kernel, peers, count, slots, scal...  9.56 us
    all_gather x4, waiting for transfers between devices, spread(): return lax.all_gather(x, 'expert', axis=0, axis_index_groups=same_place)  9.07 us
  transfers between devices with their start and end apart: 41, of which 13 were waited for; matrix products, arithmetic and copies ran while one was open for 10% of the time, Pallas kernels for 24%

profile of v4, /device:TPU:9, one launch (start us, length us, event | category | flops | bytes accessed | tf_op | source)
XLA Modules:
  0.0 198.4 jit_solution(7857350643778947611)
XLA Ops:
  7.3 1.9 fusion.32
  11.8 2.5 %collective-permute-start.1 = (f32[2,16,128]{2,1,0:T(8,128)S(1)}, f32[2,16,128]{2,1,0:T(8,128)S(1)}, u32[]{:S(2)}, u32[]{:S(2)}) collective-permute-start(f32[2,16,128]{2,1,0:T(8,128)S(1)} %get-tuple-element.191), channel_id=1, source_target_pairs={{0,16},{2,18},{4,20},{6,22},{8,24},{10,26},{12,28},{14,30},{16,0},... | collective-permute-start | bytes 49160 | tf_op jit(solution)/shard_map/ppermute | solution.py:275
  15.1 2.2 %collective-permute-start = (f32[2,16,128]{2,1,0:T(8,128)S(1)}, f32[2,16,128]{2,1,0:T(8,128)S(1)}, u32[]{:S(2)}, u32[]{:S(2)}) collective-permute-start(f32[2,16,128]{2,1,0:T(8,128)S(1)} %get-tuple-element.191), channel_id=1, source_target_pairs={{0,8},{2,10},{4,12},{6,14},{8,16},{10,18},{12,20},{14,22},{16,24},... | collective-permute-start | bytes 49160 | tf_op jit(solution)/shard_map/ppermute | solution.py:275
  20.0 1.2 collective-permute-start.3
  21.2 1.2 collective-permute-start.4
  22.5 4.8 %collective-permute-done.3.refs_1_ = bf16[1,72,2048]{2,1,0:T(8,128)(2,1)S(1)} collective-permute-done((bf16[1,72,2048]{2,1,0:T(8,128)(2,1)S(1)}, bf16[1,72,2048]{2,1,0:T(8,128)(2,1)S(1)}, u32[]{:S(2)}, u32[]{:S(2)}) %collective-permute-start.3) | collective-permute-done | bytes 294944 | tf_op jit(solution)/shard_map/ppermute | solution.py:278
  28.0 2.0 %collective-permute-start.5 = (bf16[1,72,2048]{2,1,0:T(8,128)(2,1)S(1)}, bf16[1,72,2048]{2,1,0:T(8,128)(2,1)S(1)}, u32[]{:S(2)}, u32[]{:S(2)}) collective-permute-start(bf16[1,72,2048]{2,1,0:T(8,128)(2,1)S(1)} %get-tuple-element.91), channel_id=1, source_target_pairs={{0,6},{2,4},{4,2},{6,0},{8,14},{10,12},{12,10},{14,8},{16,22},{18,... | collective-permute-start | bytes 884744 | tf_op jit(solution)/shard_map/ppermute | solution.py:278
  33.7 1.5 collective-permute-done.5.refs_3_
  36.3 1.2 collective-permute-start.13
  37.7 1.4 all-gather.9.cloned.1.call-done
  39.1 1.2 copy-done.3
  40.3 2.3 %shard_map.88 = (bf16[3,72,1024]{2,1,0:T(8,128)(2,1)S(1)}, bf16[3,72,1024]{2,1,0:T(8,128)(2,1)}, bf16[3,72,1024]{2,1,0:T(8,128)(2,1)}, bf16[3,72,1024]{2,1,0:T(8,128)(2,1)}) custom-call(s32[3]{0:T(128)S(1)} %slice.62._, f32[12,128]{1,0:T(8,128)S(1)} %reshape.61.pos_ref, f32[12,128]{1,0:T(8,128)S(1)} %reshape.62.weight_ref, ...), custom_call_target="tpu_custom_call" | custom-call | flops 226492416 | bytes 2555904 | tf_op jit(solution)/shard_map/pallas_call | solution.py:59
  46.0 1.2 collective-permute-start.12
  47.2 1.7 collective-permute-done.13.refs_3_
  50.8 1.6 broadcast_select_fusion.4
  52.4 4.3 %broadcast_select_fusion.2 = (bf16[1024,768]{1,0:T(8,128)(2,1)}, bf16[1024,768]{1,0:T(8,128)(2,1)}) fusion(bf16[1024,768]{1,0:T(8,128)(2,1)} %collective-permute-done.7, pred[]{:T(512)S(6)} %eq.46, bf16[1,1024,768]{2,1,0:T(8,128)(2,1)} %param.12), kind=kLoop, calls=%fused_computation.14 | loop fusion | flops 1572864 | bytes 6291457 | tf_op jit(solution)/shard_map/jit(_where)/select_n | solution.py:347
  56.7 3.8 %broadcast_select_fusion = (bf16[1024,768]{1,0:T(8,128)(2,1)}, bf16[1024,768]{1,0:T(8,128)(2,1)}) fusion(bf16[1024,768]{1,0:T(8,128)(2,1)} %collective-permute-done.8, pred[]{:T(512)S(6)} %eq.46, bf16[1,1024,768]{2,1,0:T(8,128)(2,1)} %param.13), kind=kLoop, calls=%fused_computation.12 | loop fusion | flops 1572864 | bytes 6291457 | tf_op jit(solution)/shard_map/jit(_where)/select_n | solution.py:347
  60.5 7.6 %all-gather.11.cloned.1.call-done = bf16[512,1024]{1,0:T(8,128)(2,1)} async-done(((bf16[128,1024]{1,0:T(8,128)(2,1)}), bf16[512,1024]{1,0:T(8,128)(2,1)}) %all-gather.11.cloned.1.call-update) | async-done | bytes 1048592 | tf_op jit(solution)/shard_map/all_gather | solution.py:308
  68.1 1.2 copy-done.2
  69.4 1.6 shard_map.91
  71.0 1.3 collective-permute-start.15
  73.7 6.8 %shard_map.87 = (bf16[4,72,768]{2,1,0:T(8,128)(2,1)S(1)}, bf16[1,72,2048]{2,1,0:T(8,128)(2,1)S(1)}, bf16[1,72,2048]{2,1,0:T(8,128)(2,1)}, bf16[1,72,2048]{2,1,0:T(8,128)(2,1)}, bf16[1,72,2048]{2,1,0:T(8,128)(2,1)}) custom-call(bf16[1,72,2048]{2,1,0:T(8,128)(2,1)S(1)} %copy-done.20, bf16[1,72,2048]{2,1,0:T(8,128)(2,1)S(1)} %copy-done.22, ...), custom_call_target="tpu_custom_call" | custom-call | flops 2717908992 | bytes 12238848 | tf_op jit(solution)/shard_map/pallas_call | solution.py:200
  81.3 6.0 %shard_map.90 = (f32[864,768]{1,0:T(8,128)}, f32[864,768]{1,0:T(8,128)}) custom-call(bf16[3,72,1024]{2,1,0:T(8,128)(2,1)S(1)} %copy-done.31, bf16[3,72,1024]{2,1,0:T(8,128)(2,1)} %collective-permute-done.10.refs_1_, bf16[3,72,1024]{2,1,0:T(8,128)(2,1)} %collective-permute-done.12.refs_2_, bf16[3,72,1024]{2,1,0:T(8,128)(2,1)} %collective-permute-done.14.refs_3_, ...), custom_call_target="tpu_custom_call" | custom-call | flops 2717908992 | bytes 10223616 | tf_op jit(solution)/shard_map/pallas_call | solution.py:200
  87.3 1.2 collective-permute-start.16
  90.0 9.2 %shard_map.92 = (bf16[12,72,768]{2,1,0:T(8,128)(2,1)S(1)}, bf16[3,72,1024]{2,1,0:T(8,128)(2,1)S(1)}, bf16[3,72,1024]{2,1,0:T(8,128)(2,1)}, bf16[3,72,1024]{2,1,0:T(8,128)(2,1)}, bf16[3,72,1024]{2,1,0:T(8,128)(2,1)S(1)}) custom-call(bf16[3,72,1024]{2,1,0:T(8,128)(2,1)S(1)} %get-tuple-element.126.refs_0_, ...), custom_call_target="tpu_custom_call" | custom-call | flops 4076863488 | bytes 14893056 | tf_op jit(solution)/shard_map/pallas_call | solution.py:200
  100.3 1.2 copy-done.1
  101.5 1.8 shard_map.93
  103.4 1.3 collective-permute-start.21
  106.5 2.5 %shard_map.94 = (bf16[3,72,1024]{2,1,0:T(8,128)(2,1)S(1)}, bf16[3,72,1024]{2,1,0:T(8,128)(2,1)}, bf16[3,72,1024]{2,1,0:T(8,128)(2,1)}, bf16[3,72,1024]{2,1,0:T(8,128)(2,1)S(1)}) custom-call(bf16[12,72,768]{2,1,0:T(8,128)(2,1)S(1)} %copy-done.34, bf16[1024,768]{1,0:T(8,128)(2,1)S(1)} %copy-done.4), custom_call_target="tpu_custom_call" | custom-call | flops 1358954496 | bytes 4669440 | tf_op jit(solution)/shard_map/pallas_call | solution.py:200
  109.0 1.9 collective-permute-done.21.refs_5_
  110.9 6.0 %collective-permute-done.22.refs_6_ = bf16[3,72,1024]{2,1,0:T(8,128)(2,1)S(1)} collective-permute-done((bf16[3,72,1024]{2,1,0:T(8,128)(2,1)}, bf16[3,72,1024]{2,1,0:T(8,128)(2,1)S(1)}, u32[]{:S(2)}, u32[]{:S(2)}) %collective-permute-start.22) | collective-permute-done | bytes 442400 | tf_op jit(solution)/shard_map/ppermute | solution.py:278
  117.9 3.5 %shard_map.95 = bf16[4,128,1024]{2,1,0:T(8,128)(2,1)} custom-call(s32[4]{0:T(128)S(1)} %and_select_fusion._, f32[16,128]{1,0:T(8,128)S(1)} %bitcast.86, f32[16,128]{1,0:T(8,128)S(1)} %bitcast.88, bf16[1,72,2048]{2,1,0:T(8,128)(2,1)S(1)} %get-tuple-element.112.refs_0_, bf16[1,72,2048]{2,1,0:T(8,128)(2,1)S(1)} %collective-permute-done.16.refs_1_, ...), custom_call_target="tpu_custom_call" | custom-call | flops 603979776 | bytes 3407872 | tf_op jit(solution)/shard_map/pallas_call | solution.py:105
  121.5 2.1 %collective-permute-start.24 = (bf16[3,72,1024]{2,1,0:T(8,128)(2,1)}, bf16[3,72,1024]{2,1,0:T(8,128)(2,1)S(1)}, u32[]{:S(2)}, u32[]{:S(2)}) collective-permute-start(bf16[3,72,1024]{2,1,0:T(8,128)(2,1)} %get-tuple-element.152), channel_id=1, source_target_pairs={{0,2},{2,0},{4,6},{6,4},{8,10},{10,8},{12,14},{14,12},{16,18},{18,... | collective-permute-start | bytes 1327112 | tf_op jit(solution)/shard_map/ppermute | solution.py:278
  124.8 5.0 %collective-permute-done.24.refs_5_ = bf16[3,72,1024]{2,1,0:T(8,128)(2,1)S(1)} collective-permute-done((bf16[3,72,1024]{2,1,0:T(8,128)(2,1)}, bf16[3,72,1024]{2,1,0:T(8,128)(2,1)S(1)}, u32[]{:S(2)}, u32[]{:S(2)}) %collective-permute-start.24) | collective-permute-done | bytes 442400 | tf_op jit(solution)/shard_map/ppermute | solution.py:278
  129.8 6.7 %collective-permute-done.25.refs_6_ = bf16[3,72,1024]{2,1,0:T(8,128)(2,1)S(1)} collective-permute-done((bf16[3,72,1024]{2,1,0:T(8,128)(2,1)}, bf16[3,72,1024]{2,1,0:T(8,128)(2,1)S(1)}, u32[]{:S(2)}, u32[]{:S(2)}) %collective-permute-start.25) | collective-permute-done | bytes 442400 | tf_op jit(solution)/shard_map/ppermute | solution.py:278
  136.6 3.5 %shard_map.96 = bf16[4,128,1024]{2,1,0:T(8,128)(2,1)} custom-call(s32[4]{0:T(128)S(1)} %and_select_fusion._, f32[16,128]{1,0:T(8,128)S(1)} %bitcast.87, f32[16,128]{1,0:T(8,128)S(1)} %bitcast.89, bf16[1,72,2048]{2,1,0:T(8,128)(2,1)S(1)} %get-tuple-element.112.refs_0_, bf16[1,72,2048]{2,1,0:T(8,128)(2,1)S(1)} %collective-permute-done.16.refs_1_, ...), custom_call_target="tpu_custom_call" | custom-call | flops 603979776 | bytes 3407872 | tf_op jit(solution)/shard_map/pallas_call | solution.py:105
  140.1 1.3 collective-permute-start.31
  142.9 1.2 copy-done
  144.1 1.6 shard_map.98
  145.8 4.9 %shard_map.97 = f32[4,512,768]{2,1,0:T(8,128)} custom-call(s32[4]{0:T(128)S(1)} %pad_add_fusion._, bf16[4,72,768]{2,1,0:T(8,128)(2,1)S(1)} %copy-done.10, bf16[1,72,2048]{2,1,0:T(8,128)(2,1)S(1)} %copy-done.12, bf16[1,72,2048]{2,1,0:T(8,128)(2,1)S(1)} %copy-done.14, bf16[1,72,2048]{2,1,0:T(8,128)(2,1)S(1)} %copy-done.16, bf16[1,72,2048]{2,1,0:T(8,128)(2,1)S(1)} %copy-done.18), custom_call_target="tpu_custom_call" | custom-call | flops 905969664 | bytes 6291456 | tf_op jit(solution)/shard_map/pallas_call | solution.py:244
  150.7 1.3 collective-permute-start.32
  152.0 13.0 %collective-permute-done.29 = bf16[3,72,1024]{2,1,0:T(8,128)(2,1)S(1)} collective-permute-done((bf16[3,72,1024]{2,1,0:T(8,128)(2,1)}, bf16[3,72,1024]{2,1,0:T(8,128)(2,1)S(1)}, u32[]{:S(2)}, u32[]{:S(2)}) %collective-permute-start.29) | collective-permute-done | bytes 442400 | tf_op jit(solution)/shard_map/ppermute | solution.py:278
  165.0 1.2 collective-permute-start.30
  167.6 2.8 %fusion.1 = bf16[512,768]{1,0:T(8,128)(2,1)S(1)} fusion(f32[4,512,768]{2,1,0:T(8,128)} %shard_map.97, bf16[864,768]{1,0:T(8,128)(2,1)S(1)} %bitcast.90, bf16[864,1024]{1,0:T(8,128)(2,1)S(1)} %bitcast.97, s32[]{:T(128)S(6)} %select_n.74), kind=kOutput, calls=%fused_computation.4 | convolution fusion | flops 680263680 | bytes 4571140 | tf_op jit(solution)/shard_map/dot_general | solution.py:388
  170.4 7.1 %collective-permute-start.34 = (bf16[512,768]{1,0:T(8,128)(2,1)S(1)}, bf16[512,768]{1,0:T(8,128)(2,1)S(1)}, u32[]{:S(2)}, u32[]{:S(2)}) collective-permute-start(bf16[512,768]{1,0:T(8,128)(2,1)S(1)} %fusion.1), channel_id=1, source_target_pairs={{0,1},{1,0},{2,3},{3,2},{4,5},{5,4},{6,7},{7,6},{8,9},{9,8},{10,11... | collective-permute-start | bytes 2359304 | tf_op jit(solution)/shard_map/ppermute | solution.py:281
  177.5 2.7 %collective-permute-done.30 = bf16[3,72,1024]{2,1,0:T(8,128)(2,1)S(1)} collective-permute-done((bf16[3,72,1024]{2,1,0:T(8,128)(2,1)S(1)}, bf16[3,72,1024]{2,1,0:T(8,128)(2,1)S(1)}, u32[]{:S(2)}, u32[]{:S(2)}) %collective-permute-start.30) | collective-permute-done | bytes 442400 | tf_op jit(solution)/shard_map/ppermute | solution.py:278
  181.6 3.9 %collective-permute-start.33 = (bf16[512,768]{1,0:T(8,128)(2,1)S(1)}, bf16[512,768]{1,0:T(8,128)(2,1)S(1)}, u32[]{:S(2)}, u32[]{:S(2)}) collective-permute-start(bf16[512,768]{1,0:T(8,128)(2,1)S(1)} %fusion.4), channel_id=1, source_target_pairs={{0,1},{1,0},{2,3},{3,2},{4,5},{5,4},{6,7},{7,6},{8,9},{9,8},{10,11... | collective-permute-start | bytes 2359304 | tf_op jit(solution)/shard_map/ppermute | solution.py:281
  188.7 1.9 pad_maximum_fusion.2
  (175 shorter events, 34.1 us)
Async XLA Ops:
  7.2 11.0 %copy-start.7 = (bf16[128,2048]{1,0:T(8,128)(2,1)S(1)}, bf16[128,2048]{1,0:T(8,128)(2,1)}, u32[]{:S(2)}) copy-start(bf16[128,2048]{1,0:T(8,128)(2,1)} %param.7) | copy-start | bytes 1572868
  7.2 31.9 %all-gather.9.cloned.1.call-start = ((), (), s32[]{:S(2)}) async-start(), calls=%async_computation.4 | async-start | bytes 1310720 | tf_op jit(solution)/shard_map/all_gather | solution.py:308
  9.2 58.9 %all-gather.11.cloned.1.call-start = ((), (), s32[]{:S(2)}) async-start(), calls=%async_computation.5 | async-start | bytes 1310720 | tf_op jit(solution)/shard_map/all_gather | solution.py:308
  10.0 90.3 %all-gather.13.cloned.1.call-start = ((), (), s32[]{:S(2)}) async-start(), calls=%async_computation.6 | async-start | bytes 1310720 | tf_op jit(solution)/shard_map/all_gather | solution.py:308
  10.0 26.3 %collective-permute-start.6 = (bf16[1024,768]{1,0:T(8,128)(2,1)}, bf16[1024,768]{1,0:T(8,128)(2,1)}, u32[]{:S(2)}, u32[]{:S(2)}) collective-permute-start(bf16[1024,768]{1,0:T(8,128)(2,1)} %bitcast.101), channel_id=1, source_target_pairs={{0,1},{1,0},{2,3},{3,2},{4,5},{5,4},{6,7},{7,6},{8,9},{9,8},{10,11... | collective-permute-start | bytes 4718600 | tf_op jit(solution)/shard_map/ppermute | solution.py:281
  11.5 131.3 %all-gather.15.cloned.1.call-start = ((), (), s32[]{:S(2)}) async-start(), calls=%async_computation.7 | async-start | bytes 1310720 | tf_op jit(solution)/shard_map/all_gather | solution.py:308
  11.8 3.2 %collective-permute-start.2 = (f32[2,16,128]{2,1,0:T(8,128)S(1)}, f32[2,16,128]{2,1,0:T(8,128)S(1)}, u32[]{:S(2)}, u32[]{:S(2)}) collective-permute-start(f32[2,16,128]{2,1,0:T(8,128)S(1)} %get-tuple-element.191), channel_id=1, source_target_pairs={{0,24},{2,26},{4,28},{6,30},{8,0},{10,2},{12,4},{14,6},{16,8},{18,... | collective-permute-start | bytes 49160 | tf_op jit(solution)/shard_map/ppermute | solution.py:275
  11.8 5.5 %collective-permute-start.1 = (f32[2,16,128]{2,1,0:T(8,128)S(1)}, f32[2,16,128]{2,1,0:T(8,128)S(1)}, u32[]{:S(2)}, u32[]{:S(2)}) collective-permute-start(f32[2,16,128]{2,1,0:T(8,128)S(1)} %get-tuple-element.191), channel_id=1, source_target_pairs={{0,16},{2,18},{4,20},{6,22},{8,24},{10,26},{12,28},{14,30},{16,0},... | collective-permute-start | bytes 49160 | tf_op jit(solution)/shard_map/ppermute | solution.py:275
  14.3 23.4 %collective-permute-start.7 = (bf16[1024,768]{1,0:T(8,128)(2,1)}, bf16[1024,768]{1,0:T(8,128)(2,1)}, u32[]{:S(2)}, u32[]{:S(2)}) collective-permute-start(bf16[1024,768]{1,0:T(8,128)(2,1)} %bitcast.16), channel_id=1, source_target_pairs={{0,1},{1,0},{2,3},{3,2},{4,5},{5,4},{6,7},{7,6},{8,9},{9,8},{10,11... | collective-permute-start | bytes 4718600 | tf_op jit(solution)/shard_map/ppermute | solution.py:281
  14.9 22.8 %collective-permute-start.8 = (bf16[1024,768]{1,0:T(8,128)(2,1)}, bf16[1024,768]{1,0:T(8,128)(2,1)}, u32[]{:S(2)}, u32[]{:S(2)}) collective-permute-start(bf16[1024,768]{1,0:T(8,128)(2,1)} %bitcast.17), channel_id=1, source_target_pairs={{0,1},{1,0},{2,3},{3,2},{4,5},{5,4},{6,7},{7,6},{8,9},{9,8},{10,11... | collective-permute-start | bytes 4718600 | tf_op jit(solution)/shard_map/ppermute | solution.py:281
  15.1 3.1 %collective-permute-start = (f32[2,16,128]{2,1,0:T(8,128)S(1)}, f32[2,16,128]{2,1,0:T(8,128)S(1)}, u32[]{:S(2)}, u32[]{:S(2)}) collective-permute-start(f32[2,16,128]{2,1,0:T(8,128)S(1)} %get-tuple-element.191), channel_id=1, source_target_pairs={{0,8},{2,10},{4,12},{6,14},{8,16},{10,18},{12,20},{14,22},{16,24},... | collective-permute-start | bytes 49160 | tf_op jit(solution)/shard_map/ppermute | solution.py:275
  20.0 7.3 %collective-permute-start.3 = (bf16[1,72,2048]{2,1,0:T(8,128)(2,1)S(1)}, bf16[1,72,2048]{2,1,0:T(8,128)(2,1)S(1)}, u32[]{:S(2)}, u32[]{:S(2)}) collective-permute-start(bf16[1,72,2048]{2,1,0:T(8,128)(2,1)S(1)} %get-tuple-element.89), channel_id=1, source_target_pairs={{0,2},{2,0},{4,6},{6,4},{8,10},{10,8},{12,14},{14,12},{16,18},{18,... | collective-permute-start | bytes 884744 | tf_op jit(solution)/shard_map/ppermute | solution.py:278
  21.2 11.5 %collective-permute-start.4 = (bf16[1,72,2048]{2,1,0:T(8,128)(2,1)S(1)}, bf16[1,72,2048]{2,1,0:T(8,128)(2,1)S(1)}, u32[]{:S(2)}, u32[]{:S(2)}) collective-permute-start(bf16[1,72,2048]{2,1,0:T(8,128)(2,1)S(1)} %get-tuple-element.90), channel_id=1, source_target_pairs={{0,4},{2,6},{4,0},{6,2},{8,12},{10,14},{12,8},{14,10},{16,20},{18,... | collective-permute-start | bytes 884744 | tf_op jit(solution)/shard_map/ppermute | solution.py:278
  28.0 7.2 %collective-permute-start.5 = (bf16[1,72,2048]{2,1,0:T(8,128)(2,1)S(1)}, bf16[1,72,2048]{2,1,0:T(8,128)(2,1)S(1)}, u32[]{:S(2)}, u32[]{:S(2)}) collective-permute-start(bf16[1,72,2048]{2,1,0:T(8,128)(2,1)S(1)} %get-tuple-element.91), channel_id=1, source_target_pairs={{0,6},{2,4},{4,2},{6,0},{8,14},{10,12},{12,10},{14,8},{16,22},{18,... | collective-permute-start | bytes 884744 | tf_op jit(solution)/shard_map/ppermute | solution.py:278
  30.7 157.9 %reduce-scatter.3.cloned.1.call-start = ((), (), s32[]{:S(2)}) async-start(), calls=%async_computation.2 | async-start | bytes 1310720 | tf_op jit(solution)/shard_map/reduce_scatter | solution.py:373
  33.5 9.9 %collective-permute-start.9 = (bf16[1,72,2048]{2,1,0:T(8,128)(2,1)S(1)}, bf16[1,72,2048]{2,1,0:T(8,128)(2,1)S(1)}, u32[]{:S(2)}, u32[]{:S(2)}) collective-permute-start(bf16[1,72,2048]{2,1,0:T(8,128)(2,1)S(1)} %get-tuple-element.100), channel_id=1, source_target_pairs={{0,2},{2,0},{4,6},{6,4},{8,10},{10,8},{12,14},{14,12},{16,18},{18,... | collective-permute-start | bytes 884744 | tf_op jit(solution)/shard_map/ppermute | solution.py:278
  35.2 10.1 %collective-permute-start.11 = (bf16[1,72,2048]{2,1,0:T(8,128)(2,1)S(1)}, bf16[1,72,2048]{2,1,0:T(8,128)(2,1)S(1)}, u32[]{:S(2)}, u32[]{:S(2)}) collective-permute-start(bf16[1,72,2048]{2,1,0:T(8,128)(2,1)S(1)} %get-tuple-element.104), channel_id=1, source_target_pairs={{0,4},{2,6},{4,0},{6,2},{8,12},{10,14},{12,8},{14,10},{16,20},{18,... | collective-permute-start | bytes 884744 | tf_op jit(solution)/shard_map/ppermute | solution.py:278
  36.3 12.6 %collective-permute-start.13 = (bf16[1,72,2048]{2,1,0:T(8,128)(2,1)S(1)}, bf16[1,72,2048]{2,1,0:T(8,128)(2,1)S(1)}, u32[]{:S(2)}, u32[]{:S(2)}) collective-permute-start(bf16[1,72,2048]{2,1,0:T(8,128)(2,1)S(1)} %get-tuple-element.108), channel_id=1, source_target_pairs={{0,6},{2,4},{4,2},{6,0},{8,14},{10,12},{12,10},{14,8},{16,22},{18,... | collective-permute-start | bytes 884744 | tf_op jit(solution)/shard_map/ppermute | solution.py:278
  40.3 10.4 %copy-start.36 = (bf16[1,1024,768]{2,1,0:T(8,128)(2,1)S(1)}, bf16[1,1024,768]{2,1,0:T(8,128)(2,1)}, u32[]{:S(2)}) copy-start(bf16[1,1024,768]{2,1,0:T(8,128)(2,1)} %param.11) | copy-start | bytes 4718596
  44.1 24.0 %collective-permute-start.10 = (bf16[3,72,1024]{2,1,0:T(8,128)(2,1)}, bf16[3,72,1024]{2,1,0:T(8,128)(2,1)}, u32[]{:S(2)}, u32[]{:S(2)}) collective-permute-start(bf16[3,72,1024]{2,1,0:T(8,128)(2,1)} %get-tuple-element.101), channel_id=1, source_target_pairs={{0,2},{2,0},{4,6},{6,4},{8,10},{10,8},{12,14},{14,12},{16,18},{18,... | collective-permute-start | bytes 1327112 | tf_op jit(solution)/shard_map/ppermute | solution.py:278
  46.0 22.1 %collective-permute-start.12 = (bf16[3,72,1024]{2,1,0:T(8,128)(2,1)}, bf16[3,72,1024]{2,1,0:T(8,128)(2,1)}, u32[]{:S(2)}, u32[]{:S(2)}) collective-permute-start(bf16[3,72,1024]{2,1,0:T(8,128)(2,1)} %get-tuple-element.105), channel_id=1, source_target_pairs={{0,4},{2,6},{4,0},{6,2},{8,12},{10,14},{12,8},{14,10},{16,20},{18,... | collective-permute-start | bytes 1327112 | tf_op jit(solution)/shard_map/ppermute | solution.py:278
  49.6 18.5 %collective-permute-start.14 = (bf16[3,72,1024]{2,1,0:T(8,128)(2,1)}, bf16[3,72,1024]{2,1,0:T(8,128)(2,1)}, u32[]{:S(2)}, u32[]{:S(2)}) collective-permute-start(bf16[3,72,1024]{2,1,0:T(8,128)(2,1)} %get-tuple-element.109), channel_id=1, source_target_pairs={{0,6},{2,4},{4,2},{6,0},{8,14},{10,12},{12,10},{14,8},{16,22},{18,... | collective-permute-start | bytes 1327112 | tf_op jit(solution)/shard_map/ppermute | solution.py:278
  52.4 21.3 %copy-start.5 = (bf16[1024,768]{1,0:T(8,128)(2,1)}, bf16[1024,768]{1,0:T(8,128)(2,1)S(1)}, u32[]{:S(2)}) copy-start(bf16[1024,768]{1,0:T(8,128)(2,1)S(1)} %get-tuple-element.178.refs_5_.refs_4_) | copy-start | bytes 4718596
  71.0 16.4 %collective-permute-start.15 = (bf16[3,72,1024]{2,1,0:T(8,128)(2,1)S(1)}, bf16[3,72,1024]{2,1,0:T(8,128)(2,1)S(1)}, u32[]{:S(2)}, u32[]{:S(2)}) collective-permute-start(bf16[3,72,1024]{2,1,0:T(8,128)(2,1)S(1)} %get-tuple-element.116), channel_id=1, source_target_pairs={{0,2},{2,0},{4,6},{6,4},{8,10},{10,8},{12,14},{14,12},{16,18},{18,... | collective-permute-start | bytes 1327112 | tf_op jit(solution)/shard_map/ppermute | solution.py:278
  72.2 16.3 %collective-permute-start.17 = (bf16[3,72,1024]{2,1,0:T(8,128)(2,1)S(1)}, bf16[3,72,1024]{2,1,0:T(8,128)(2,1)S(1)}, u32[]{:S(2)}, u32[]{:S(2)}) collective-permute-start(bf16[3,72,1024]{2,1,0:T(8,128)(2,1)S(1)} %get-tuple-element.120), channel_id=1, source_target_pairs={{0,4},{2,6},{4,0},{6,2},{8,12},{10,14},{12,8},{14,10},{16,20},{18,... | collective-permute-start | bytes 1327112 | tf_op jit(solution)/shard_map/ppermute | solution.py:278
  73.4 16.3 %collective-permute-start.19 = (bf16[3,72,1024]{2,1,0:T(8,128)(2,1)S(1)}, bf16[3,72,1024]{2,1,0:T(8,128)(2,1)S(1)}, u32[]{:S(2)}, u32[]{:S(2)}) collective-permute-start(bf16[3,72,1024]{2,1,0:T(8,128)(2,1)S(1)} %get-tuple-element.124), channel_id=1, source_target_pairs={{0,6},{2,4},{4,2},{6,0},{8,14},{10,12},{12,10},{14,8},{16,22},{18,... | collective-permute-start | bytes 1327112 | tf_op jit(solution)/shard_map/ppermute | solution.py:278
  73.7 7.6 %copy-start.6 = (bf16[1024,768]{1,0:T(8,128)(2,1)S(1)}, bf16[1024,768]{1,0:T(8,128)(2,1)}, u32[]{:S(2)}) copy-start(bf16[1024,768]{1,0:T(8,128)(2,1)} %get-tuple-element.177.refs_6_.refs_5_) | copy-start | bytes 4718596
  87.3 16.0 %collective-permute-start.16 = (bf16[1,72,2048]{2,1,0:T(8,128)(2,1)}, bf16[1,72,2048]{2,1,0:T(8,128)(2,1)S(1)}, u32[]{:S(2)}, u32[]{:S(2)}) collective-permute-start(bf16[1,72,2048]{2,1,0:T(8,128)(2,1)} %get-tuple-element.117), channel_id=1, source_target_pairs={{0,2},{2,0},{4,6},{6,4},{8,10},{10,8},{12,14},{14,12},{16,18},{18,... | collective-permute-start | bytes 884744 | tf_op jit(solution)/shard_map/ppermute | solution.py:278
  88.5 16.1 %collective-permute-start.18 = (bf16[1,72,2048]{2,1,0:T(8,128)(2,1)}, bf16[1,72,2048]{2,1,0:T(8,128)(2,1)S(1)}, u32[]{:S(2)}, u32[]{:S(2)}) collective-permute-start(bf16[1,72,2048]{2,1,0:T(8,128)(2,1)} %get-tuple-element.121), channel_id=1, source_target_pairs={{0,4},{2,6},{4,0},{6,2},{8,12},{10,14},{12,8},{14,10},{16,20},{18,... | collective-permute-start | bytes 884744 | tf_op jit(solution)/shard_map/ppermute | solution.py:278
  89.7 16.1 %collective-permute-start.20 = (bf16[1,72,2048]{2,1,0:T(8,128)(2,1)}, bf16[1,72,2048]{2,1,0:T(8,128)(2,1)S(1)}, u32[]{:S(2)}, u32[]{:S(2)}) collective-permute-start(bf16[1,72,2048]{2,1,0:T(8,128)(2,1)} %get-tuple-element.125), channel_id=1, source_target_pairs={{0,6},{2,4},{4,2},{6,0},{8,14},{10,12},{12,10},{14,8},{16,22},{18,... | collective-permute-start | bytes 884744 | tf_op jit(solution)/shard_map/ppermute | solution.py:278
  103.4 7.5 %collective-permute-start.21 = (bf16[3,72,1024]{2,1,0:T(8,128)(2,1)}, bf16[3,72,1024]{2,1,0:T(8,128)(2,1)S(1)}, u32[]{:S(2)}, u32[]{:S(2)}) collective-permute-start(bf16[3,72,1024]{2,1,0:T(8,128)(2,1)} %get-tuple-element.138), channel_id=1, source_target_pairs={{0,2},{2,0},{4,6},{6,4},{8,10},{10,8},{12,14},{14,12},{16,18},{18,... | collective-permute-start | bytes 1327112 | tf_op jit(solution)/shard_map/ppermute | solution.py:278
  104.6 12.3 %collective-permute-start.22 = (bf16[3,72,1024]{2,1,0:T(8,128)(2,1)}, bf16[3,72,1024]{2,1,0:T(8,128)(2,1)S(1)}, u32[]{:S(2)}, u32[]{:S(2)}) collective-permute-start(bf16[3,72,1024]{2,1,0:T(8,128)(2,1)} %get-tuple-element.140), channel_id=1, source_target_pairs={{0,4},{2,6},{4,0},{6,2},{8,12},{10,14},{12,8},{14,10},{16,20},{18,... | collective-permute-start | bytes 1327112 | tf_op jit(solution)/shard_map/ppermute | solution.py:278
  105.8 12.1 %collective-permute-start.23 = (bf16[3,72,1024]{2,1,0:T(8,128)(2,1)S(1)}, bf16[3,72,1024]{2,1,0:T(8,128)(2,1)S(1)}, u32[]{:S(2)}, u32[]{:S(2)}) collective-permute-start(bf16[3,72,1024]{2,1,0:T(8,128)(2,1)S(1)} %get-tuple-element.142), channel_id=1, source_target_pairs={{0,6},{2,4},{4,2},{6,0},{8,14},{10,12},{12,10},{14,8},{16,22},{18,... | collective-permute-start | bytes 1327112 | tf_op jit(solution)/shard_map/ppermute | solution.py:278
  109.0 8.9 %copy-start.32 = (bf16[3,72,1024]{2,1,0:T(8,128)(2,1)}, bf16[3,72,1024]{2,1,0:T(8,128)(2,1)S(1)}, u32[]{:S(2)}) copy-start(bf16[3,72,1024]{2,1,0:T(8,128)(2,1)S(1)} %get-tuple-element.154) | copy-start | bytes 1327108
  121.4 67.2 %reduce-scatter.5.cloned.1.call-start = ((), (), s32[]{:S(2)}) async-start(), calls=%async_computation.3 | async-start | bytes 1310720 | tf_op jit(solution)/shard_map/reduce_scatter | solution.py:373
  121.5 8.3 %collective-permute-start.24 = (bf16[3,72,1024]{2,1,0:T(8,128)(2,1)}, bf16[3,72,1024]{2,1,0:T(8,128)(2,1)S(1)}, u32[]{:S(2)}, u32[]{:S(2)}) collective-permute-start(bf16[3,72,1024]{2,1,0:T(8,128)(2,1)} %get-tuple-element.152), channel_id=1, source_target_pairs={{0,2},{2,0},{4,6},{6,4},{8,10},{10,8},{12,14},{14,12},{16,18},{18,... | collective-permute-start | bytes 1327112 | tf_op jit(solution)/shard_map/ppermute | solution.py:278
  123.6 13.0 %collective-permute-start.25 = (bf16[3,72,1024]{2,1,0:T(8,128)(2,1)}, bf16[3,72,1024]{2,1,0:T(8,128)(2,1)S(1)}, u32[]{:S(2)}, u32[]{:S(2)}) collective-permute-start(bf16[3,72,1024]{2,1,0:T(8,128)(2,1)} %get-tuple-element.153), channel_id=1, source_target_pairs={{0,4},{2,6},{4,0},{6,2},{8,12},{10,14},{12,8},{14,10},{16,20},{18,... | collective-permute-start | bytes 1327112 | tf_op jit(solution)/shard_map/ppermute | solution.py:278
  123.9 12.6 %collective-permute-start.26 = (bf16[3,72,1024]{2,1,0:T(8,128)(2,1)}, bf16[3,72,1024]{2,1,0:T(8,128)(2,1)S(1)}, u32[]{:S(2)}, u32[]{:S(2)}) collective-permute-start(bf16[3,72,1024]{2,1,0:T(8,128)(2,1)} %copy-done.32), channel_id=1, source_target_pairs={{0,6},{2,4},{4,2},{6,0},{8,14},{10,12},{12,10},{14,8},{16,22},{18,... | collective-permute-start | bytes 1327112 | tf_op jit(solution)/shard_map/ppermute | solution.py:278
  140.1 10.6 %collective-permute-start.31 = (bf16[3,72,1024]{2,1,0:T(8,128)(2,1)}, bf16[3,72,1024]{2,1,0:T(8,128)(2,1)S(1)}, u32[]{:S(2)}, u32[]{:S(2)}) collective-permute-start(bf16[3,72,1024]{2,1,0:T(8,128)(2,1)} %copy-done.29), channel_id=1, source_target_pairs={{0,6},{2,4},{4,2},{6,0},{8,14},{10,12},{12,10},{14,8},{16,22},{18,... | collective-permute-start | bytes 1327112 | tf_op jit(solution)/shard_map/ppermute | solution.py:278
  141.4 23.6 %collective-permute-start.29 = (bf16[3,72,1024]{2,1,0:T(8,128)(2,1)}, bf16[3,72,1024]{2,1,0:T(8,128)(2,1)S(1)}, u32[]{:S(2)}, u32[]{:S(2)}) collective-permute-start(bf16[3,72,1024]{2,1,0:T(8,128)(2,1)} %copy-done.28), channel_id=1, source_target_pairs={{0,4},{2,6},{4,0},{6,2},{8,12},{10,14},{12,8},{14,10},{16,20},{18,... | collective-permute-start | bytes 1327112 | tf_op jit(solution)/shard_map/ppermute | solution.py:278
  142.3 24.0 %collective-permute-start.27 = (bf16[3,72,1024]{2,1,0:T(8,128)(2,1)}, bf16[3,72,1024]{2,1,0:T(8,128)(2,1)S(1)}, u32[]{:S(2)}, u32[]{:S(2)}) collective-permute-start(bf16[3,72,1024]{2,1,0:T(8,128)(2,1)} %copy-done.27), channel_id=1, source_target_pairs={{0,2},{2,0},{4,6},{6,4},{8,10},{10,8},{12,14},{14,12},{16,18},{18,... | collective-permute-start | bytes 1327112 | tf_op jit(solution)/shard_map/ppermute | solution.py:278
  150.7 26.8 %collective-permute-start.32 = (bf16[3,72,1024]{2,1,0:T(8,128)(2,1)S(1)}, bf16[3,72,1024]{2,1,0:T(8,128)(2,1)S(1)}, u32[]{:S(2)}, u32[]{:S(2)}) collective-permute-start(bf16[3,72,1024]{2,1,0:T(8,128)(2,1)S(1)} %get-tuple-element.170), channel_id=1, source_target_pairs={{0,6},{2,4},{4,2},{6,0},{8,14},{10,12},{12,10},{14,8},{16,22},{18,... | collective-permute-start | bytes 1327112 | tf_op jit(solution)/shard_map/ppermute | solution.py:278
  165.0 15.3 %collective-permute-start.30 = (bf16[3,72,1024]{2,1,0:T(8,128)(2,1)S(1)}, bf16[3,72,1024]{2,1,0:T(8,128)(2,1)S(1)}, u32[]{:S(2)}, u32[]{:S(2)}) collective-permute-start(bf16[3,72,1024]{2,1,0:T(8,128)(2,1)S(1)} %get-tuple-element.167), channel_id=1, source_target_pairs={{0,4},{2,6},{4,0},{6,2},{8,12},{10,14},{12,8},{14,10},{16,20},{18,... | collective-permute-start | bytes 1327112 | tf_op jit(solution)/shard_map/ppermute | solution.py:278
  166.2 14.0 %collective-permute-start.28 = (bf16[3,72,1024]{2,1,0:T(8,128)(2,1)S(1)}, bf16[3,72,1024]{2,1,0:T(8,128)(2,1)S(1)}, u32[]{:S(2)}, u32[]{:S(2)}) collective-permute-start(bf16[3,72,1024]{2,1,0:T(8,128)(2,1)S(1)} %get-tuple-element.164), channel_id=1, source_target_pairs={{0,2},{2,0},{4,6},{6,4},{8,10},{10,8},{12,14},{14,12},{16,18},{18,... | collective-permute-start | bytes 1327112 | tf_op jit(solution)/shard_map/ppermute | solution.py:278
  166.8 13.7 %slice-start = ((s8[6291456]{0:T(1024)(128)(4,1)}), s8[4194304]{0:T(1024)(128)(4,1)S(1)}, s32[]{:S(2)}) async-start(s8[6291456]{0:T(1024)(128)(4,1)} %bitcast.94), calls=%async_computation.8 | async-start | bytes 8388608
  167.6 12.9 %slice-start.1 = ((s8[6291456]{0:T(1024)(128)(4,1)}), s8[2097152]{0:T(1024)(128)(4,1)S(1)}, s32[]{:S(2)}) async-start(s8[6291456]{0:T(1024)(128)(4,1)} %bitcast.94), calls=%async_computation.9 | async-start | bytes 4194304
  170.4 17.2 %collective-permute-start.34 = (bf16[512,768]{1,0:T(8,128)(2,1)S(1)}, bf16[512,768]{1,0:T(8,128)(2,1)S(1)}, u32[]{:S(2)}, u32[]{:S(2)}) collective-permute-start(bf16[512,768]{1,0:T(8,128)(2,1)S(1)} %fusion.1), channel_id=1, source_target_pairs={{0,1},{1,0},{2,3},{3,2},{4,5},{5,4},{6,7},{7,6},{8,9},{9,8},{10,11... | collective-permute-start | bytes 2359304 | tf_op jit(solution)/shard_map/ppermute | solution.py:281
  181.6 9.0 %collective-permute-start.33 = (bf16[512,768]{1,0:T(8,128)(2,1)S(1)}, bf16[512,768]{1,0:T(8,128)(2,1)S(1)}, u32[]{:S(2)}, u32[]{:S(2)}) collective-permute-start(bf16[512,768]{1,0:T(8,128)(2,1)S(1)} %fusion.4), channel_id=1, source_target_pairs={{0,1},{1,0},{2,3},{3,2},{4,5},{5,4},{6,7},{7,6},{8,9},{9,8},{10,11... | collective-permute-start | bytes 2359304 | tf_op jit(solution)/shard_map/ppermute | solution.py:281
  (34 other events, 84.5 us)
Sparse Core Ops, SparseCore 0:
  10.2 28.8 all-gather.8
  40.7 27.4 all-gather.10
  69.7 27.4 all-gather.12
  98.6 27.4 all-gather.14
  128.2 26.9 reduce-scatter.2
  157.4 25.7 reduce-scatter.4

commit v5 on v4

--- a/solution.py
+++ b/solution.py
@@ -9,7 +9,8 @@
 
 F32 = jnp.float32
 BF16 = jnp.bfloat16
-VMEM_LIMIT = 48 * 1024 * 1024
+VMEM_LIMIT = 32 * 1024 * 1024
+LONG = pl.CostEstimate(flops=10**11, bytes_accessed=1, transcendentals=0)
 
 
 def two_levels(experts):
@@ -20,7 +21,7 @@
 
 
 def column_tile(columns):
-    return 512 if columns % 512 == 0 else columns
+    return next((t for t in (512, 640, 384) if columns % t == 0), columns)
 
 
 def select_kernel(peers, count, slots, scaled, _, pos_ref, weight_ref, *refs):
@@ -114,11 +115,7 @@
         ),
         out_shape=jax.ShapeDtypeStruct((count, toks, cols), BF16),
         compiler_params=pltpu.CompilerParams(vmem_limit_bytes=VMEM_LIMIT),
-        cost_estimate=pl.CostEstimate(
-            flops=4 * peers * count * slots * toks * cols,
-            bytes_accessed=2 * cols * count * (toks + peers * slots),
-            transcendentals=0,
-        ),
+        cost_estimate=LONG,
     )(which, pos, weight, *own, *rest)
 
 
@@ -144,25 +141,22 @@
     )(*given)
 
 
-def expert_kernel(peers, parts, held, mats, halves, joined_out, *refs):
+def expert_kernel(peers, spans, held, mats, halves, joined_out, *refs):
     take = iter(refs)
-    rows = [[next(take) for _ in range(peers)] for _ in range(parts)]
+    rows = [next(take) for _ in range(peers)]
     gates, ups = ([next(take) for _ in range(mats)] for _ in range(2))
     before = [next(take) for _ in range(2)] if held else None
     downs = [next(take) for _ in range(halves)]
     outs = list(take)
-    count, slots = rows[0][0].shape[:2]
-    pieces = []
-    for part in rows:
-        stacked = jnp.concatenate([x[g] for x in part for g in range(count)], axis=0)
-        deep = gates[0].shape[0]
-        pieces += [stacked[:, at : at + deep] for at in range(0, stacked.shape[1], deep)]
+    count, slots = rows[0].shape[:2]
+    stacked = jnp.concatenate([x[g] for x in rows for g in range(count)], axis=0)
     sums = []
-    for i, mats in enumerate((gates, ups)):
-        total = before[i][...] if before else None
-        for x, w in zip(pieces, mats):
-            part = jnp.dot(x, w[...], preferred_element_type=F32)
-            total = part if total is None else total + part
+    for i, weights in enumerate((gates, ups)):
+        total, at = before[i][...] if before else None, 0
+        for which, low, high in spans:
+            piece = stacked[:, at : at + high - low]
+            part = jnp.dot(piece, weights[which][low:high], preferred_element_type=F32)
+            total, at = part if total is None else total + part, at + high - low
         sums.append(total)
     if not halves:
         outs[0][...], outs[1][...] = sums
@@ -211,12 +205,12 @@
     )(*args)
 
 
-def expert(rows, gates, ups, held, downs):
-    peers = len(rows[0])
-    count, slots, _ = rows[0][0].shape
+def expert(rows, spans, gates, ups, held, downs):
+    peers = len(rows)
+    count, slots, deep = rows[0].shape
     units = gates[0].shape[1]
     total = peers * count * slots
-    flops = 4 * total * units * sum(w.shape[0] for w in gates)
+    flops = 4 * total * units * deep
     if not downs:
         shapes = [jax.ShapeDtypeStruct((total, units), F32)] * 2
     else:
@@ -225,9 +219,9 @@
         shapes = [jax.ShapeDtypeStruct((peers * count, slots, units), BF16)]
         shapes += [jax.ShapeDtypeStruct((count, slots, wide), BF16)] * peers
     kernel = functools.partial(
-        expert_kernel, peers, len(rows), bool(held), len(gates), len(downs), len(downs) > 1
-    )
-    return in_vmem(kernel, shapes, flops, *sum(rows, []), *gates, *ups, *held, *downs)
+        expert_kernel, peers, spans, bool(held), len(gates), len(downs), len(downs) > 1
+    )
+    return in_vmem(kernel, shapes, flops, *rows, *gates, *ups, *held, *downs)
 
 
 def own_grad_kernel(peers, _, hidden_ref, *refs):
@@ -252,11 +246,7 @@
         ),
         out_shape=jax.ShapeDtypeStruct((count, piece, units), F32),
         compiler_params=pltpu.CompilerParams(vmem_limit_bytes=VMEM_LIMIT),
-        cost_estimate=pl.CostEstimate(
-            flops=2 * peers * slots * count * piece * units,
-            bytes_accessed=4 * count * piece * units,
-            transcendentals=0,
-        ),
+        cost_estimate=LONG,
     )(blocks, hidden, *rows)
 
 
@@ -307,15 +297,9 @@
     def spread(x):
         return lax.all_gather(x, "expert", axis=0, axis_index_groups=same_place)
 
-    token_all = [spread(tokens[:, h * deep : (h + 1) * deep]) for h in range(2)]
-    cot_all = [
-        spread(
-            jnp.concatenate(
-                [cotangent[:, i * piece : (i + 1) * piece] for i in (h, 2 + h)], axis=1
-            )
-        )
-        for h in range(2)
-    ]
+    cut = model_width // 2
+    token_all = [spread(tokens[:, :cut]), spread(tokens[:, cut:])]
+    cot_all = spread(cotangent)
     metas = [meta] + [to_plane(meta, s) for s in range(1, major)]
 
     def table_of(shifts):
@@ -336,10 +320,12 @@
             queue[k] = [back[k]]
         return back
 
-    def pick_rest(x, scaled):
+    def pick_rest(x, scaled, tiles, tile):
+        return select([x] * (major - 1), sender[1:], rest_table, slots, scaled, tiles, tile)
+
+    def pick_tokens(x):
         tile = column_tile(x.shape[2])
-        tiles = list(range(x.shape[2] // tile))
-        return select([x] * (major - 1), sender[1:], rest_table, slots, scaled, tiles, tile)
+        return pick_rest(x, False, list(range(x.shape[2] // tile)), tile)
 
     tile = column_tile(model_width)
     got = [other_core(w[0]) for w in (gate_weight, up_weight, down_weight)]
@@ -353,31 +339,35 @@
     own_cots = exchange(
         select([cotangent[None]], zero, own_table, slots, True, [0, 2, 1, 3], piece)
     )
-    first = exchange(pick_rest(after(token_all[0], got), False))
-    second = exchange(pick_rest(after(token_all[1], first[1:]), False))
-    own_hidden, *own_out = expert([own_rows], gate_mats, up_mats, [], down_mats)
-    held = expert([first], gate_mats[:1], up_mats[:1], [], [])
+    first = exchange(pick_tokens(after(token_all[0], got)))
+    second = exchange(pick_tokens(after(token_all[1], first[1:])))
+    both = [(0, 0, deep), (1, 0, deep)]
+    own_hidden, *own_out = expert(own_rows, both, gate_mats, up_mats, [], down_mats)
+    early = [(0, 0, deep)]
+    held = expert(first, early, gate_mats[:1], up_mats[:1], [], [])
     own_back = exchange(after_all(own_out, held))
-    rest_hidden, *out = expert([second], gate_mats[1:], up_mats[1:], held, down_mats[:1])
+    late = [(0, 0, deep)]
+    rest_hidden, *out = expert(second, late, gate_mats[1:], up_mats[1:], held, down_mats[:1])
 
     shapes = [jax.ShapeDtypeStruct(x.shape, x.dtype) for x in out]
     flops = 2 * rest_hidden.size * wide
     kernel = functools.partial(project_kernel, minor, major - 1)
     outs = [out, in_vmem(kernel, shapes, flops, rest_hidden, down_mats[1])]
-    cots = [pick_rest(after(cot_all[0], out[1:]), True), None]
+    cots = [None, None]
     mixed = []
     for h in range(2):
-        back = exchange(outs[h] if h else after_all(outs[h], cots[0]))
-        sums = combine(sender, all_table, own_back, after_all(back, outs[1]), h)
+        back = exchange(outs[h])
+        cots[h] = pick_rest(after(cot_all, back[1:] if h else out[1:]), True, [h, 2 + h], piece)
+        sums = combine(sender, all_table, own_back, after_all(back, [] if h else [*outs[1], *cots[0]]), h)
         mixed.append(
             lax.psum_scatter(sums, "expert", scatter_dimension=0, axis_index_groups=same_place)
         )
     mixed = jnp.concatenate(mixed, axis=1)
-    cots[1] = pick_rest(cot_all[1], True)
     rest_cots = [exchange(x) for x in cots]
 
     whose = (1 - core, core)
     blocks = jnp.stack([2 * h + c for h in range(2) for c in whose]).astype(jnp.int32)
+    own_cots = after_all(own_cots, rest_cots[0][1:])
     own_parts = own_grads(blocks, own_hidden, own_cots, piece)
     rest_hidden = rest_hidden.reshape(-1, rest_hidden.shape[2])
     grad = None

time: 201 us -> 201 us (level)
  local copies, waits for them, and re-layouts: 15.2 us -> 27.1 us
  waiting for transfers between devices: 55.2 us -> 45.4 us
  starting transfers between devices: 45.3 us -> 53.3 us
  Pallas kernels: 48 us -> 40.6 us
    ppermute x27, waiting for transfers between devices: 44.5 us -> 27.5 us  [to_peer(): return lax.ppermute(x, 'expert', [(i, i ^ k) for i in range(experts)])]
    unnamed x82 -> x114, local copies, waits for them, and re-layouts: 13.2 us -> 25.1 us
    pallas_call x4, Pallas kernels: 24.5 us -> 15.3 us  [in_vmem(): pl.pallas_call(kernel, in_specs=[vmem] * len(args), out_specs=[vmem] * le...]
    all_gather x4 -> x3, waiting for transfers between devices: 9.07 us -> 16.9 us  [spread(): return lax.all_gather(x, 'expert', axis=0, axis_index_groups=same_place)]
    ppermute x5, starting transfers between devices: 12.4 us -> 17.3 us  [other_core(): return lax.ppermute(x, 'dp', [(0, 1), (1, 0)])]
    ppermute x27, starting transfers between devices: 27.9 us -> 31.1 us  [to_peer(): return lax.ppermute(x, 'expert', [(i, i ^ k) for i in range(experts)])]
    pallas_call x2, Pallas kernels: 7 us -> 9.71 us  [combine(): pl.pallas_call(functools.partial(combine_kernel, peers), grid_spec=pltpu....]
  transfers between devices with their start and end apart: 41 -> 40, of which waited for: 13 -> 14; matrix products, arithmetic and copies ran while one was open for 10% -> 9% of each run, Pallas kernels for 24% -> 20%
where the time goes in v5:
time: 201 us; the launch traced here: 198 us
  starting transfers between devices  53.3 us (27%)
  waiting for transfers between devices  45.4 us (23%)
  Pallas kernels  40.6 us (20%)
  local copies, waits for them, and re-layouts  27.1 us (13%)
  between operations  14.3 us (7%)
  other arithmetic  13.1 us (7%)
  matrix products  4.47 us (2%)
    ppermute x27, starting transfers between devices, to_peer(): return lax.ppermute(x, 'expert', [(i, i ^ k) for i in range(experts)])  31.1 us
    ppermute x27, waiting for transfers between devices, to_peer(): return lax.ppermute(x, 'expert', [(i, i ^ k) for i in range(experts)])  27.5 us
    unnamed x114, local copies, waits for them, and re-layouts  25.1 us
    ppermute x5, starting transfers between devices, other_core(): return lax.ppermute(x, 'dp', [(0, 1), (1, 0)])  17.3 us
    all_gather x3, waiting for transfers between devices, spread(): return lax.all_gather(x, 'expert', axis=0, axis_index_groups=same_place)  16.9 us
    pallas_call x4, Pallas kernels, in_vmem(): pl.pallas_call(kernel, in_specs=[vmem] * len(args), out_specs=[vmem] * le...  15.3 us
    pallas_call x6, Pallas kernels, select(): pl.pallas_call(functools.partial(select_kernel, peers, count, slots, scal...  10.3 us
    pallas_call x2, Pallas kernels, combine(): pl.pallas_call(functools.partial(combine_kernel, peers), grid_spec=pltpu....  9.71 us
  transfers between devices with their start and end apart: 40, of which 14 were waited for; matrix products, arithmetic and copies ran while one was open for 9% of the time, Pallas kernels for 20%

profile of v5, /device:TPU:9, one launch (start us, length us, event | category | flops | bytes accessed | tf_op | source)
XLA Modules:
  0.0 198.3 jit_solution(13730773092668772705)
XLA Ops:
  7.2 1.9 fusion.31
  10.3 2.5 %collective-permute-start.1 = (f32[2,16,128]{2,1,0:T(8,128)S(1)}, f32[2,16,128]{2,1,0:T(8,128)S(1)}, u32[]{:S(2)}, u32[]{:S(2)}) collective-permute-start(f32[2,16,128]{2,1,0:T(8,128)S(1)} %get-tuple-element.189), channel_id=1, source_target_pairs={{0,16},{2,18},{4,20},{6,22},{8,24},{10,26},{12,28},{14,30},{16,0},... | collective-permute-start | bytes 49160 | tf_op jit(solution)/shard_map/ppermute | solution.py:265
  14.1 2.2 %collective-permute-start = (f32[2,16,128]{2,1,0:T(8,128)S(1)}, f32[2,16,128]{2,1,0:T(8,128)S(1)}, u32[]{:S(2)}, u32[]{:S(2)}) collective-permute-start(f32[2,16,128]{2,1,0:T(8,128)S(1)} %get-tuple-element.189), channel_id=1, source_target_pairs={{0,8},{2,10},{4,12},{6,14},{8,16},{10,18},{12,20},{14,22},{16,24},... | collective-permute-start | bytes 49160 | tf_op jit(solution)/shard_map/ppermute | solution.py:265
  18.4 1.3 collective-permute-start.3
  20.9 4.7 %collective-permute-done.3.refs_1_ = bf16[1,72,2048]{2,1,0:T(8,128)(2,1)S(1)} collective-permute-done((bf16[1,72,2048]{2,1,0:T(8,128)(2,1)S(1)}, bf16[1,72,2048]{2,1,0:T(8,128)(2,1)S(1)}, u32[]{:S(2)}, u32[]{:S(2)}) %collective-permute-start.3) | collective-permute-done | bytes 294944 | tf_op jit(solution)/shard_map/ppermute | solution.py:268
  25.6 2.1 %collective-permute-start.5 = (bf16[1,72,2048]{2,1,0:T(8,128)(2,1)S(1)}, bf16[1,72,2048]{2,1,0:T(8,128)(2,1)S(1)}, u32[]{:S(2)}, u32[]{:S(2)}) collective-permute-start(bf16[1,72,2048]{2,1,0:T(8,128)(2,1)S(1)} %get-tuple-element.92), channel_id=1, source_target_pairs={{0,6},{2,4},{4,2},{6,0},{8,14},{10,12},{12,10},{14,8},{16,22},{18,... | collective-permute-start | bytes 884744 | tf_op jit(solution)/shard_map/ppermute | solution.py:268
  30.1 2.6 %collective-permute-done.5.refs_3_ = bf16[1,72,2048]{2,1,0:T(8,128)(2,1)S(1)} collective-permute-done((bf16[1,72,2048]{2,1,0:T(8,128)(2,1)S(1)}, bf16[1,72,2048]{2,1,0:T(8,128)(2,1)S(1)}, u32[]{:S(2)}, u32[]{:S(2)}) %collective-permute-start.5) | collective-permute-done | bytes 294944 | tf_op jit(solution)/shard_map/ppermute | solution.py:268
  33.9 1.2 collective-permute-start.13
  35.4 3.7 %all-gather.7.cloned.1.call-done = bf16[512,1024]{1,0:T(8,128)(2,1)} async-done(((bf16[128,1024]{1,0:T(8,128)(2,1)}), bf16[512,1024]{1,0:T(8,128)(2,1)}) %all-gather.7.cloned.1.call-update) | async-done | bytes 1048592 | tf_op jit(solution)/shard_map/all_gather | solution.py:298
  40.3 2.3 %shard_map.88 = (bf16[3,72,1024]{2,1,0:T(8,128)(2,1)S(1)}, bf16[3,72,1024]{2,1,0:T(8,128)(2,1)}, bf16[3,72,1024]{2,1,0:T(8,128)(2,1)}, bf16[3,72,1024]{2,1,0:T(8,128)(2,1)}) custom-call(s32[3]{0:T(128)S(1)} %slice.50._, f32[12,128]{1,0:T(8,128)S(1)} %reshape.61.pos_ref, f32[12,128]{1,0:T(8,128)S(1)} %reshape.62.weight_ref, ...), custom_call_target="tpu_custom_call" | custom-call | flops 226492416 | bytes 2555904 | tf_op jit(solution)/shard_map/pallas_call | solution.py:60
  42.6 1.3 collective-permute-start.10
  46.1 2.1 %collective-permute-start.14 = (bf16[3,72,1024]{2,1,0:T(8,128)(2,1)}, bf16[3,72,1024]{2,1,0:T(8,128)(2,1)}, u32[]{:S(2)}, u32[]{:S(2)}) collective-permute-start(bf16[3,72,1024]{2,1,0:T(8,128)(2,1)} %get-tuple-element.110), channel_id=1, source_target_pairs={{0,6},{2,4},{4,2},{6,0},{8,14},{10,12},{12,10},{14,8},{16,22},{18,... | collective-permute-start | bytes 1327112 | tf_op jit(solution)/shard_map/ppermute | solution.py:268
  48.2 2.8 %broadcast_select_fusion.4 = (bf16[1024,768]{1,0:T(8,128)(2,1)S(1)}, bf16[1024,768]{1,0:T(8,128)(2,1)}) fusion(bf16[1024,768]{1,0:T(8,128)(2,1)} %collective-permute-done.6, pred[]{:T(512)S(6)} %eq.46, bf16[1,1024,768]{2,1,0:T(8,128)(2,1)S(1)} %copy-done.52), kind=kLoop, calls=%fused_computation.16 | loop fusion | flops 1572864 | bytes 6291457 | tf_op jit(solution)/shard_map/jit(_where)/select_n | solution.py:333
  51.0 3.4 %broadcast_select_fusion.2 = (bf16[1024,768]{1,0:T(8,128)(2,1)}, bf16[1024,768]{1,0:T(8,128)(2,1)}) fusion(bf16[1024,768]{1,0:T(8,128)(2,1)} %collective-permute-done.7, pred[]{:T(512)S(6)} %eq.46, bf16[1,1024,768]{2,1,0:T(8,128)(2,1)S(1)} %copy-done.53), kind=kLoop, calls=%fused_computation.14 | loop fusion | flops 1572864 | bytes 6291457 | tf_op jit(solution)/shard_map/jit(_where)/select_n | solution.py:333
  54.4 2.8 %broadcast_select_fusion = (bf16[1024,768]{1,0:T(8,128)(2,1)S(1)}, bf16[1024,768]{1,0:T(8,128)(2,1)}) fusion(bf16[1024,768]{1,0:T(8,128)(2,1)} %collective-permute-done.8, pred[]{:T(512)S(6)} %eq.46, bf16[1,1024,768]{2,1,0:T(8,128)(2,1)S(1)} %copy-done.54), kind=kLoop, calls=%fused_computation.12 | loop fusion | flops 1572864 | bytes 6291457 | tf_op jit(solution)/shard_map/jit(_where)/select_n | solution.py:333
  57.2 10.8 %all-gather.9.cloned.1.call-done = bf16[512,1024]{1,0:T(8,128)(2,1)} async-done(((bf16[128,1024]{1,0:T(8,128)(2,1)}), bf16[512,1024]{1,0:T(8,128)(2,1)}) %all-gather.9.cloned.1.call-update) | async-done | bytes 1048592 | tf_op jit(solution)/shard_map/all_gather | solution.py:298
  69.3 1.6 shard_map.91
  70.9 1.3 collective-permute-start.15
  73.6 1.4 copy-done.6
  75.0 1.4 copy-done.7
  79.4 2.9 %shard_map.87 = (bf16[4,72,768]{2,1,0:T(8,128)(2,1)S(1)}, bf16[1,72,2048]{2,1,0:T(8,128)(2,1)S(1)}, bf16[1,72,2048]{2,1,0:T(8,128)(2,1)S(1)}, bf16[1,72,2048]{2,1,0:T(8,128)(2,1)S(1)}, bf16[1,72,2048]{2,1,0:T(8,128)(2,1)S(1)}) custom-call(bf16[1,72,2048]{2,1,0:T(8,128)(2,1)S(1)} %get-tuple-element.89.refs_0_, bf16[1,72,2048]{2,1,0:T(8,128)(2,1)S(1)} %copy-done.11, ...), custom_call_target="tpu_custom_call" | custom-call | flops 2717908992 | bytes 12238848 | tf_op jit(solution)/shard_map/pallas_call | solution.py:194
  82.3 4.5 %shard_map.90 = (f32[864,768]{1,0:T(8,128)S(1)}, f32[864,768]{1,0:T(8,128)S(1)}) custom-call(bf16[3,72,1024]{2,1,0:T(8,128)(2,1)S(1)} %copy-done.19, bf16[3,72,1024]{2,1,0:T(8,128)(2,1)} %collective-permute-done.10.refs_1_, bf16[3,72,1024]{2,1,0:T(8,128)(2,1)} %collective-permute-done.12.refs_2_, bf16[3,72,1024]{2,1,0:T(8,128)(2,1)} %collective-permute-done.14.refs_3_, ...), custom_call_target="tpu_custom_call" | custom-call | flops 2717908992 | bytes 10223616 | tf_op jit(solution)/shard_map/pallas_call | solution.py:194
  86.8 1.3 collective-permute-start.16
  89.3 2.3 %collective-permute-done.19.refs_3_ = bf16[3,72,1024]{2,1,0:T(8,128)(2,1)S(1)} collective-permute-done((bf16[3,72,1024]{2,1,0:T(8,128)(2,1)S(1)}, bf16[3,72,1024]{2,1,0:T(8,128)(2,1)S(1)}, u32[]{:S(2)}, u32[]{:S(2)}) %collective-permute-start.19) | collective-permute-done | bytes 442400 | tf_op jit(solution)/shard_map/ppermute | solution.py:268
  92.4 5.5 %shard_map.92 = (bf16[12,72,768]{2,1,0:T(8,128)(2,1)S(1)}, bf16[3,72,1024]{2,1,0:T(8,128)(2,1)S(1)}, bf16[3,72,1024]{2,1,0:T(8,128)(2,1)}, bf16[3,72,1024]{2,1,0:T(8,128)(2,1)}, bf16[3,72,1024]{2,1,0:T(8,128)(2,1)}) custom-call(bf16[3,72,1024]{2,1,0:T(8,128)(2,1)S(1)} %get-tuple-element.127.refs_0_, ...), custom_call_target="tpu_custom_call" | custom-call | flops 4076863488 | bytes 14893056 | tf_op jit(solution)/shard_map/pallas_call | solution.py:194
  100.7 1.5 collective-permute-start.22
  102.3 2.1 %collective-permute-done.20.refs_3_ = bf16[1,72,2048]{2,1,0:T(8,128)(2,1)S(1)} collective-permute-done((bf16[1,72,2048]{2,1,0:T(8,128)(2,1)S(1)}, bf16[1,72,2048]{2,1,0:T(8,128)(2,1)S(1)}, u32[]{:S(2)}, u32[]{:S(2)}) %collective-permute-start.20) | collective-permute-done | bytes 294944 | tf_op jit(solution)/shard_map/ppermute | solution.py:268
  105.8 1.3 copy-done.44
  107.1 2.4 %shard_map.93 = (bf16[3,72,1024]{2,1,0:T(8,128)(2,1)S(1)}, bf16[3,72,1024]{2,1,0:T(8,128)(2,1)}, bf16[3,72,1024]{2,1,0:T(8,128)(2,1)}, bf16[3,72,1024]{2,1,0:T(8,128)(2,1)S(1)}) custom-call(bf16[12,72,768]{2,1,0:T(8,128)(2,1)S(1)} %copy-done.44, bf16[1024,768]{1,0:T(8,128)(2,1)S(1)} %get-tuple-element.176.refs_9_.down_ref), custom_call_target="tpu_custom_call" | custom-call | flops 1358954496 | bytes 4669440 | tf_op jit(solution)/shard_map/pallas_call | solution.py:194
  111.1 2.4 %all-gather.11.cloned.1.call-done = bf16[512,2048]{1,0:T(8,128)(2,1)} async-done(((bf16[128,2048]{1,0:T(8,128)(2,1)}), bf16[512,2048]{1,0:T(8,128)(2,1)}) %all-gather.11.cloned.1.call-update) | async-done | bytes 2097168 | tf_op jit(solution)/shard_map/all_gather | solution.py:298
  113.5 1.6 copy-done
  115.1 2.5 %shard_map.94 = (bf16[3,72,1024]{2,1,0:T(8,128)(2,1)S(1)}, bf16[3,72,1024]{2,1,0:T(8,128)(2,1)}, bf16[3,72,1024]{2,1,0:T(8,128)(2,1)}, bf16[3,72,1024]{2,1,0:T(8,128)(2,1)S(1)}) custom-call(s32[3]{0:T(128)S(1)} %slice.50._, f32[12,128]{1,0:T(8,128)S(1)} %reshape.61.pos_ref, f32[12,128]{1,0:T(8,128)S(1)} %reshape.62.weight_ref, ...), custom_call_target="tpu_custom_call" | custom-call | flops 226492416 | bytes 2555904 | tf_op jit(solution)/shard_map/pallas_call | solution.py:60
  120.0 2.2 %collective-permute-done.23.refs_7_ = bf16[3,72,1024]{2,1,0:T(8,128)(2,1)} collective-permute-done((bf16[3,72,1024]{2,1,0:T(8,128)(2,1)}, bf16[3,72,1024]{2,1,0:T(8,128)(2,1)}, u32[]{:S(2)}, u32[]{:S(2)}) %collective-permute-start.23) | collective-permute-done | bytes 442400 | tf_op jit(solution)/shard_map/ppermute | solution.py:268
  122.2 1.9 collective-permute-start.26
  124.1 4.9 %shard_map.95 = bf16[4,128,1024]{2,1,0:T(8,128)(2,1)} custom-call(s32[4]{0:T(128)S(1)} %and_select_fusion._, f32[16,128]{1,0:T(8,128)S(1)} %bitcast.85, f32[16,128]{1,0:T(8,128)S(1)} %bitcast.87, bf16[1,72,2048]{2,1,0:T(8,128)(2,1)S(1)} %copy-done.33, bf16[1,72,2048]{2,1,0:T(8,128)(2,1)S(1)} %copy-done.35, bf16[1,72,2048]{2,1,0:T(8,128)(2,1)S(1)} %copy-done.38, ...), custom_call_target="tpu_custom_call" | custom-call | flops 99999997952 | bytes 1 | tf_op jit(solution)/shard_map/pallas_call | solution.py:106
  129.0 1.5 collective-permute-done.24.refs_5_
  131.3 1.7 collective-permute-done.25.refs_6_
  133.8 7.4 %collective-permute-done.26.refs_7_ = bf16[3,72,1024]{2,1,0:T(8,128)(2,1)} collective-permute-done((bf16[3,72,1024]{2,1,0:T(8,128)(2,1)S(1)}, bf16[3,72,1024]{2,1,0:T(8,128)(2,1)}, u32[]{:S(2)}, u32[]{:S(2)}) %collective-permute-start.26) | collective-permute-done | bytes 442400 | tf_op jit(solution)/shard_map/ppermute | solution.py:268
  141.2 1.8 collective-permute-start.27
  150.2 4.8 %shard_map.96 = bf16[4,128,1024]{2,1,0:T(8,128)(2,1)} custom-call(s32[4]{0:T(128)S(1)} %and_select_fusion._, f32[16,128]{1,0:T(8,128)S(1)} %bitcast.86, f32[16,128]{1,0:T(8,128)S(1)} %bitcast.88, bf16[1,72,2048]{2,1,0:T(8,128)(2,1)S(1)} %copy-done.33, bf16[1,72,2048]{2,1,0:T(8,128)(2,1)S(1)} %copy-done.36, bf16[1,72,2048]{2,1,0:T(8,128)(2,1)S(1)} %copy-done.39, ...), custom_call_target="tpu_custom_call" | custom-call | flops 99999997952 | bytes 1 | tf_op jit(solution)/shard_map/pallas_call | solution.py:106
  155.1 1.6 shard_map.98
  156.7 2.7 %collective-permute-done.29 = bf16[3,72,1024]{2,1,0:T(8,128)(2,1)} collective-permute-done((bf16[3,72,1024]{2,1,0:T(8,128)(2,1)S(1)}, bf16[3,72,1024]{2,1,0:T(8,128)(2,1)}, u32[]{:S(2)}, u32[]{:S(2)}) %collective-permute-start.29) | collective-permute-done | bytes 442400 | tf_op jit(solution)/shard_map/ppermute | solution.py:268
  159.4 3.2 %collective-permute-start.32 = (bf16[3,72,1024]{2,1,0:T(8,128)(2,1)S(1)}, bf16[3,72,1024]{2,1,0:T(8,128)(2,1)S(1)}, u32[]{:S(2)}, u32[]{:S(2)}) collective-permute-start(bf16[3,72,1024]{2,1,0:T(8,128)(2,1)S(1)} %get-tuple-element.172), channel_id=1, source_target_pairs={{0,6},{2,4},{4,2},{6,0},{8,14},{10,12},{12,10},{14,8},{16,22},{18,... | collective-permute-start | bytes 1327112 | tf_op jit(solution)/shard_map/ppermute | solution.py:268
  162.9 3.3 %shard_map.97 = f32[4,512,768]{2,1,0:T(8,128)S(1)} custom-call(s32[4]{0:T(128)S(1)} %pad_add_fusion._, bf16[4,72,768]{2,1,0:T(8,128)(2,1)S(1)} %copy-done.17, bf16[1,72,2048]{2,1,0:T(8,128)(2,1)S(1)} %copy-done.47, bf16[1,72,2048]{2,1,0:T(8,128)(2,1)S(1)} %copy-done.27, bf16[1,72,2048]{2,1,0:T(8,128)(2,1)S(1)} %copy-done.29, bf16[1,72,2048]{2,1,0:T(8,128)(2,1)S(1)} %copy-done.31), custom_call_target="tpu_custom_call" | custom-call | flops 99999997952 | bytes 1 | tf_op jit(solution)/shard_map/pallas_call | solution.py:238
  166.2 1.6 pad_maximum_fusion.1
  169.0 11.8 %collective-permute-start.34 = (bf16[512,768]{1,0:T(8,128)(2,1)S(1)}, bf16[512,768]{1,0:T(8,128)(2,1)S(1)}, u32[]{:S(2)}, u32[]{:S(2)}) collective-permute-start(bf16[512,768]{1,0:T(8,128)(2,1)S(1)} %fusion.1), channel_id=1, source_target_pairs={{0,1},{1,0},{2,3},{3,2},{4,5},{5,4},{6,7},{7,6},{8,9},{9,8},{10,11... | collective-permute-start | bytes 2359304 | tf_op jit(solution)/shard_map/ppermute | solution.py:271
  182.1 3.6 %collective-permute-start.33 = (bf16[512,768]{1,0:T(8,128)(2,1)S(1)}, bf16[512,768]{1,0:T(8,128)(2,1)S(1)}, u32[]{:S(2)}, u32[]{:S(2)}) collective-permute-start(bf16[512,768]{1,0:T(8,128)(2,1)S(1)} %fusion.4), channel_id=1, source_target_pairs={{0,1},{1,0},{2,3},{3,2},{4,5},{5,4},{6,7},{7,6},{8,9},{9,8},{10,11... | collective-permute-start | bytes 2359304 | tf_op jit(solution)/shard_map/ppermute | solution.py:271
  188.9 1.9 pad_maximum_fusion.2
  (200 shorter events, 44.4 us)
Async XLA Ops:
  7.2 10.1 %copy-start.8 = (bf16[128,2048]{1,0:T(8,128)(2,1)S(1)}, bf16[128,2048]{1,0:T(8,128)(2,1)}, u32[]{:S(2)}) copy-start(bf16[128,2048]{1,0:T(8,128)(2,1)} %param.7) | copy-start | bytes 1572868
  7.2 20.7 %copy-start.9 = (bf16[128,2048]{1,0:T(8,128)(2,1)S(1)}, bf16[128,2048]{1,0:T(8,128)(2,1)}, u32[]{:S(2)}) copy-start(bf16[128,2048]{1,0:T(8,128)(2,1)} %param.10) | copy-start | bytes 1572868
  7.2 31.8 %all-gather.7.cloned.1.call-start = ((), (), s32[]{:S(2)}) async-start(), calls=%async_computation.4 | async-start | bytes 1310720 | tf_op jit(solution)/shard_map/all_gather | solution.py:298
  9.2 58.9 %all-gather.9.cloned.1.call-start = ((), (), s32[]{:S(2)}) async-start(), calls=%async_computation.5 | async-start | bytes 1310720 | tf_op jit(solution)/shard_map/all_gather | solution.py:298
  9.3 24.7 %collective-permute-start.6 = (bf16[1024,768]{1,0:T(8,128)(2,1)}, bf16[1024,768]{1,0:T(8,128)(2,1)}, u32[]{:S(2)}, u32[]{:S(2)}) collective-permute-start(bf16[1024,768]{1,0:T(8,128)(2,1)} %bitcast.98), channel_id=1, source_target_pairs={{0,1},{1,0},{2,3},{3,2},{4,5},{5,4},{6,7},{7,6},{8,9},{9,8},{10,11... | collective-permute-start | bytes 4718600 | tf_op jit(solution)/shard_map/ppermute | solution.py:271
  10.0 103.5 %all-gather.11.cloned.1.call-start = ((), (), s32[]{:S(2)}) async-start(), calls=%async_computation.6 | async-start | bytes 2621440 | tf_op jit(solution)/shard_map/all_gather | solution.py:298
  10.3 3.8 %collective-permute-start.2 = (f32[2,16,128]{2,1,0:T(8,128)S(1)}, f32[2,16,128]{2,1,0:T(8,128)S(1)}, u32[]{:S(2)}, u32[]{:S(2)}) collective-permute-start(f32[2,16,128]{2,1,0:T(8,128)S(1)} %get-tuple-element.189), channel_id=1, source_target_pairs={{0,24},{2,26},{4,28},{6,30},{8,0},{10,2},{12,4},{14,6},{16,8},{18,... | collective-permute-start | bytes 49160 | tf_op jit(solution)/shard_map/ppermute | solution.py:265
  10.3 6.1 %collective-permute-start.1 = (f32[2,16,128]{2,1,0:T(8,128)S(1)}, f32[2,16,128]{2,1,0:T(8,128)S(1)}, u32[]{:S(2)}, u32[]{:S(2)}) collective-permute-start(f32[2,16,128]{2,1,0:T(8,128)S(1)} %get-tuple-element.189), channel_id=1, source_target_pairs={{0,16},{2,18},{4,20},{6,22},{8,24},{10,26},{12,28},{14,30},{16,0},... | collective-permute-start | bytes 49160 | tf_op jit(solution)/shard_map/ppermute | solution.py:265
  12.8 22.6 %collective-permute-start.7 = (bf16[1024,768]{1,0:T(8,128)(2,1)}, bf16[1024,768]{1,0:T(8,128)(2,1)}, u32[]{:S(2)}, u32[]{:S(2)}) collective-permute-start(bf16[1024,768]{1,0:T(8,128)(2,1)} %bitcast.99), channel_id=1, source_target_pairs={{0,1},{1,0},{2,3},{3,2},{4,5},{5,4},{6,7},{7,6},{8,9},{9,8},{10,11... | collective-permute-start | bytes 4718600 | tf_op jit(solution)/shard_map/ppermute | solution.py:271
  13.9 21.4 %collective-permute-start.8 = (bf16[1024,768]{1,0:T(8,128)(2,1)}, bf16[1024,768]{1,0:T(8,128)(2,1)}, u32[]{:S(2)}, u32[]{:S(2)}) collective-permute-start(bf16[1024,768]{1,0:T(8,128)(2,1)} %bitcast.100), channel_id=1, source_target_pairs={{0,1},{1,0},{2,3},{3,2},{4,5},{5,4},{6,7},{7,6},{8,9},{9,8},{10,11... | collective-permute-start | bytes 4718600 | tf_op jit(solution)/shard_map/ppermute | solution.py:271
  14.1 3.1 %collective-permute-start = (f32[2,16,128]{2,1,0:T(8,128)S(1)}, f32[2,16,128]{2,1,0:T(8,128)S(1)}, u32[]{:S(2)}, u32[]{:S(2)}) collective-permute-start(f32[2,16,128]{2,1,0:T(8,128)S(1)} %get-tuple-element.189), channel_id=1, source_target_pairs={{0,8},{2,10},{4,12},{6,14},{8,16},{10,18},{12,20},{14,22},{16,24},... | collective-permute-start | bytes 49160 | tf_op jit(solution)/shard_map/ppermute | solution.py:265
  18.4 7.2 %collective-permute-start.3 = (bf16[1,72,2048]{2,1,0:T(8,128)(2,1)S(1)}, bf16[1,72,2048]{2,1,0:T(8,128)(2,1)S(1)}, u32[]{:S(2)}, u32[]{:S(2)}) collective-permute-start(bf16[1,72,2048]{2,1,0:T(8,128)(2,1)S(1)} %get-tuple-element.90), channel_id=1, source_target_pairs={{0,2},{2,0},{4,6},{6,4},{8,10},{10,8},{12,14},{14,12},{16,18},{18,... | collective-permute-start | bytes 884744 | tf_op jit(solution)/shard_map/ppermute | solution.py:268
  19.6 10.1 %collective-permute-start.4 = (bf16[1,72,2048]{2,1,0:T(8,128)(2,1)S(1)}, bf16[1,72,2048]{2,1,0:T(8,128)(2,1)S(1)}, u32[]{:S(2)}, u32[]{:S(2)}) collective-permute-start(bf16[1,72,2048]{2,1,0:T(8,128)(2,1)S(1)} %get-tuple-element.91), channel_id=1, source_target_pairs={{0,4},{2,6},{4,0},{6,2},{8,12},{10,14},{12,8},{14,10},{16,20},{18,... | collective-permute-start | bytes 884744 | tf_op jit(solution)/shard_map/ppermute | solution.py:268
  25.6 17.0 %copy-start.10 = (bf16[1,72,2048]{2,1,0:T(8,128)(2,1)}, bf16[1,72,2048]{2,1,0:T(8,128)(2,1)S(1)}, u32[]{:S(2)}) copy-start(bf16[1,72,2048]{2,1,0:T(8,128)(2,1)S(1)} %collective-permute-done.3.refs_1_) | copy-start | bytes 884740
  25.6 7.1 %collective-permute-start.5 = (bf16[1,72,2048]{2,1,0:T(8,128)(2,1)S(1)}, bf16[1,72,2048]{2,1,0:T(8,128)(2,1)S(1)}, u32[]{:S(2)}, u32[]{:S(2)}) collective-permute-start(bf16[1,72,2048]{2,1,0:T(8,128)(2,1)S(1)} %get-tuple-element.92), channel_id=1, source_target_pairs={{0,6},{2,4},{4,2},{6,0},{8,14},{10,12},{12,10},{14,8},{16,22},{18,... | collective-permute-start | bytes 884744 | tf_op jit(solution)/shard_map/ppermute | solution.py:268
  27.7 161.2 %reduce-scatter.3.cloned.1.call-start = ((), (), s32[]{:S(2)}) async-start(), calls=%async_computation.2 | async-start | bytes 1310720 | tf_op jit(solution)/shard_map/reduce_scatter | solution.py:363
  29.8 12.9 %copy-start.12 = (bf16[1,72,2048]{2,1,0:T(8,128)(2,1)}, bf16[1,72,2048]{2,1,0:T(8,128)(2,1)S(1)}, u32[]{:S(2)}) copy-start(bf16[1,72,2048]{2,1,0:T(8,128)(2,1)S(1)} %collective-permute-done.4.refs_2_) | copy-start | bytes 884740
  29.8 12.9 %collective-permute-start.9 = (bf16[1,72,2048]{2,1,0:T(8,128)(2,1)S(1)}, bf16[1,72,2048]{2,1,0:T(8,128)(2,1)S(1)}, u32[]{:S(2)}, u32[]{:S(2)}) collective-permute-start(bf16[1,72,2048]{2,1,0:T(8,128)(2,1)S(1)} %get-tuple-element.101), channel_id=1, source_target_pairs={{0,2},{2,0},{4,6},{6,4},{8,10},{10,8},{12,14},{14,12},{16,18},{18,... | collective-permute-start | bytes 884744 | tf_op jit(solution)/shard_map/ppermute | solution.py:268
  32.7 9.9 %copy-start.14 = (bf16[1,72,2048]{2,1,0:T(8,128)(2,1)}, bf16[1,72,2048]{2,1,0:T(8,128)(2,1)S(1)}, u32[]{:S(2)}) copy-start(bf16[1,72,2048]{2,1,0:T(8,128)(2,1)S(1)} %collective-permute-done.5.refs_3_) | copy-start | bytes 884740
  32.7 11.2 %collective-permute-start.11 = (bf16[1,72,2048]{2,1,0:T(8,128)(2,1)S(1)}, bf16[1,72,2048]{2,1,0:T(8,128)(2,1)S(1)}, u32[]{:S(2)}, u32[]{:S(2)}) collective-permute-start(bf16[1,72,2048]{2,1,0:T(8,128)(2,1)S(1)} %get-tuple-element.105), channel_id=1, source_target_pairs={{0,4},{2,6},{4,0},{6,2},{8,12},{10,14},{12,8},{14,10},{16,20},{18,... | collective-permute-start | bytes 884744 | tf_op jit(solution)/shard_map/ppermute | solution.py:268
  33.9 11.4 %collective-permute-start.13 = (bf16[1,72,2048]{2,1,0:T(8,128)(2,1)S(1)}, bf16[1,72,2048]{2,1,0:T(8,128)(2,1)S(1)}, u32[]{:S(2)}, u32[]{:S(2)}) collective-permute-start(bf16[1,72,2048]{2,1,0:T(8,128)(2,1)S(1)} %get-tuple-element.109), channel_id=1, source_target_pairs={{0,6},{2,4},{4,2},{6,0},{8,14},{10,12},{12,10},{14,8},{16,22},{18,... | collective-permute-start | bytes 884744 | tf_op jit(solution)/shard_map/ppermute | solution.py:268
  42.6 25.4 %collective-permute-start.10 = (bf16[3,72,1024]{2,1,0:T(8,128)(2,1)}, bf16[3,72,1024]{2,1,0:T(8,128)(2,1)}, u32[]{:S(2)}, u32[]{:S(2)}) collective-permute-start(bf16[3,72,1024]{2,1,0:T(8,128)(2,1)} %get-tuple-element.102), channel_id=1, source_target_pairs={{0,2},{2,0},{4,6},{6,4},{8,10},{10,8},{12,14},{14,12},{16,18},{18,... | collective-permute-start | bytes 1327112 | tf_op jit(solution)/shard_map/ppermute | solution.py:268
  43.9 24.2 %collective-permute-start.12 = (bf16[3,72,1024]{2,1,0:T(8,128)(2,1)}, bf16[3,72,1024]{2,1,0:T(8,128)(2,1)}, u32[]{:S(2)}, u32[]{:S(2)}) collective-permute-start(bf16[3,72,1024]{2,1,0:T(8,128)(2,1)} %get-tuple-element.106), channel_id=1, source_target_pairs={{0,4},{2,6},{4,0},{6,2},{8,12},{10,14},{12,8},{14,10},{16,20},{18,... | collective-permute-start | bytes 1327112 | tf_op jit(solution)/shard_map/ppermute | solution.py:268
  46.1 22.0 %collective-permute-start.14 = (bf16[3,72,1024]{2,1,0:T(8,128)(2,1)}, bf16[3,72,1024]{2,1,0:T(8,128)(2,1)}, u32[]{:S(2)}, u32[]{:S(2)}) collective-permute-start(bf16[3,72,1024]{2,1,0:T(8,128)(2,1)} %get-tuple-element.110), channel_id=1, source_target_pairs={{0,6},{2,4},{4,2},{6,0},{8,14},{10,12},{12,10},{14,8},{16,22},{18,... | collective-permute-start | bytes 1327112 | tf_op jit(solution)/shard_map/ppermute | solution.py:268
  70.9 15.9 %collective-permute-start.15 = (bf16[3,72,1024]{2,1,0:T(8,128)(2,1)S(1)}, bf16[3,72,1024]{2,1,0:T(8,128)(2,1)S(1)}, u32[]{:S(2)}, u32[]{:S(2)}) collective-permute-start(bf16[3,72,1024]{2,1,0:T(8,128)(2,1)S(1)} %get-tuple-element.117), channel_id=1, source_target_pairs={{0,2},{2,0},{4,6},{6,4},{8,10},{10,8},{12,14},{14,12},{16,18},{18,... | collective-permute-start | bytes 1327112 | tf_op jit(solution)/shard_map/ppermute | solution.py:268
  72.2 15.9 %collective-permute-start.17 = (bf16[3,72,1024]{2,1,0:T(8,128)(2,1)S(1)}, bf16[3,72,1024]{2,1,0:T(8,128)(2,1)S(1)}, u32[]{:S(2)}, u32[]{:S(2)}) collective-permute-start(bf16[3,72,1024]{2,1,0:T(8,128)(2,1)S(1)} %get-tuple-element.121), channel_id=1, source_target_pairs={{0,4},{2,6},{4,0},{6,2},{8,12},{10,14},{12,8},{14,10},{16,20},{18,... | collective-permute-start | bytes 1327112 | tf_op jit(solution)/shard_map/ppermute | solution.py:268
  73.4 18.2 %collective-permute-start.19 = (bf16[3,72,1024]{2,1,0:T(8,128)(2,1)S(1)}, bf16[3,72,1024]{2,1,0:T(8,128)(2,1)S(1)}, u32[]{:S(2)}, u32[]{:S(2)}) collective-permute-start(bf16[3,72,1024]{2,1,0:T(8,128)(2,1)S(1)} %get-tuple-element.125), channel_id=1, source_target_pairs={{0,6},{2,4},{4,2},{6,0},{8,14},{10,12},{12,10},{14,8},{16,22},{18,... | collective-permute-start | bytes 1327112 | tf_op jit(solution)/shard_map/ppermute | solution.py:268
  86.8 12.8 %collective-permute-start.16 = (bf16[1,72,2048]{2,1,0:T(8,128)(2,1)S(1)}, bf16[1,72,2048]{2,1,0:T(8,128)(2,1)S(1)}, u32[]{:S(2)}, u32[]{:S(2)}) collective-permute-start(bf16[1,72,2048]{2,1,0:T(8,128)(2,1)S(1)} %get-tuple-element.118), channel_id=1, source_target_pairs={{0,2},{2,0},{4,6},{6,4},{8,10},{10,8},{12,14},{14,12},{16,18},{18,... | collective-permute-start | bytes 884744 | tf_op jit(solution)/shard_map/ppermute | solution.py:268
  88.1 11.9 %collective-permute-start.18 = (bf16[1,72,2048]{2,1,0:T(8,128)(2,1)S(1)}, bf16[1,72,2048]{2,1,0:T(8,128)(2,1)S(1)}, u32[]{:S(2)}, u32[]{:S(2)}) collective-permute-start(bf16[1,72,2048]{2,1,0:T(8,128)(2,1)S(1)} %get-tuple-element.122), channel_id=1, source_target_pairs={{0,4},{2,6},{4,0},{6,2},{8,12},{10,14},{12,8},{14,10},{16,20},{18,... | collective-permute-start | bytes 884744 | tf_op jit(solution)/shard_map/ppermute | solution.py:268
  91.6 12.8 %collective-permute-start.20 = (bf16[1,72,2048]{2,1,0:T(8,128)(2,1)S(1)}, bf16[1,72,2048]{2,1,0:T(8,128)(2,1)S(1)}, u32[]{:S(2)}, u32[]{:S(2)}) collective-permute-start(bf16[1,72,2048]{2,1,0:T(8,128)(2,1)S(1)} %get-tuple-element.126), channel_id=1, source_target_pairs={{0,6},{2,4},{4,2},{6,0},{8,14},{10,12},{12,10},{14,8},{16,22},{18,... | collective-permute-start | bytes 884744 | tf_op jit(solution)/shard_map/ppermute | solution.py:268
  99.7 9.9 %copy-start.34 = (bf16[1,72,2048]{2,1,0:T(8,128)(2,1)}, bf16[1,72,2048]{2,1,0:T(8,128)(2,1)S(1)}, u32[]{:S(2)}) copy-start(bf16[1,72,2048]{2,1,0:T(8,128)(2,1)S(1)} %collective-permute-done.16.refs_1_) | copy-start | bytes 884740
  99.7 18.0 %collective-permute-start.21 = (bf16[3,72,1024]{2,1,0:T(8,128)(2,1)}, bf16[3,72,1024]{2,1,0:T(8,128)(2,1)S(1)}, u32[]{:S(2)}, u32[]{:S(2)}) collective-permute-start(bf16[3,72,1024]{2,1,0:T(8,128)(2,1)} %get-tuple-element.130), channel_id=1, source_target_pairs={{0,2},{2,0},{4,6},{6,4},{8,10},{10,8},{12,14},{14,12},{16,18},{18,... | collective-permute-start | bytes 1327112 | tf_op jit(solution)/shard_map/ppermute | solution.py:268
  100.7 18.1 %collective-permute-start.22 = (bf16[3,72,1024]{2,1,0:T(8,128)(2,1)}, bf16[3,72,1024]{2,1,0:T(8,128)(2,1)}, u32[]{:S(2)}, u32[]{:S(2)}) collective-permute-start(bf16[3,72,1024]{2,1,0:T(8,128)(2,1)} %get-tuple-element.132), channel_id=1, source_target_pairs={{0,4},{2,6},{4,0},{6,2},{8,12},{10,14},{12,8},{14,10},{16,20},{18,... | collective-permute-start | bytes 1327112 | tf_op jit(solution)/shard_map/ppermute | solution.py:268
  105.1 17.1 %collective-permute-start.23 = (bf16[3,72,1024]{2,1,0:T(8,128)(2,1)}, bf16[3,72,1024]{2,1,0:T(8,128)(2,1)}, u32[]{:S(2)}, u32[]{:S(2)}) collective-permute-start(bf16[3,72,1024]{2,1,0:T(8,128)(2,1)} %get-tuple-element.134), channel_id=1, source_target_pairs={{0,6},{2,4},{4,2},{6,0},{8,14},{10,12},{12,10},{14,8},{16,22},{18,... | collective-permute-start | bytes 1327112 | tf_op jit(solution)/shard_map/ppermute | solution.py:268
  115.1 9.0 %copy-start.35 = (bf16[1,72,2048]{2,1,0:T(8,128)(2,1)S(1)}, bf16[1,72,2048]{2,1,0:T(8,128)(2,1)}, u32[]{:S(2)}) copy-start(bf16[1,72,2048]{2,1,0:T(8,128)(2,1)} %copy-done.34) | copy-start | bytes 884740
  115.1 9.0 %copy-start.38 = (bf16[1,72,2048]{2,1,0:T(8,128)(2,1)S(1)}, bf16[1,72,2048]{2,1,0:T(8,128)(2,1)}, u32[]{:S(2)}) copy-start(bf16[1,72,2048]{2,1,0:T(8,128)(2,1)} %copy-done.37) | copy-start | bytes 884740
  117.6 12.9 %collective-permute-start.24 = (bf16[3,72,1024]{2,1,0:T(8,128)(2,1)}, bf16[3,72,1024]{2,1,0:T(8,128)(2,1)S(1)}, u32[]{:S(2)}, u32[]{:S(2)}) collective-permute-start(bf16[3,72,1024]{2,1,0:T(8,128)(2,1)} %get-tuple-element.149), channel_id=1, source_target_pairs={{0,2},{2,0},{4,6},{6,4},{8,10},{10,8},{12,14},{14,12},{16,18},{18,... | collective-permute-start | bytes 1327112 | tf_op jit(solution)/shard_map/ppermute | solution.py:268
  118.8 14.1 %collective-permute-start.25 = (bf16[3,72,1024]{2,1,0:T(8,128)(2,1)}, bf16[3,72,1024]{2,1,0:T(8,128)(2,1)S(1)}, u32[]{:S(2)}, u32[]{:S(2)}) collective-permute-start(bf16[3,72,1024]{2,1,0:T(8,128)(2,1)} %get-tuple-element.150), channel_id=1, source_target_pairs={{0,4},{2,6},{4,0},{6,2},{8,12},{10,14},{12,8},{14,10},{16,20},{18,... | collective-permute-start | bytes 1327112 | tf_op jit(solution)/shard_map/ppermute | solution.py:268
  122.2 19.0 %collective-permute-start.26 = (bf16[3,72,1024]{2,1,0:T(8,128)(2,1)S(1)}, bf16[3,72,1024]{2,1,0:T(8,128)(2,1)}, u32[]{:S(2)}, u32[]{:S(2)}) collective-permute-start(bf16[3,72,1024]{2,1,0:T(8,128)(2,1)S(1)} %copy-done.23), channel_id=1, source_target_pairs={{0,6},{2,4},{4,2},{6,0},{8,14},{10,12},{12,10},{14,8},{16,22},{18,... | collective-permute-start | bytes 1327112 | tf_op jit(solution)/shard_map/ppermute | solution.py:268
  129.0 59.9 %reduce-scatter.5.cloned.1.call-start = ((), (), s32[]{:S(2)}) async-start(), calls=%async_computation.3 | async-start | bytes 1310720 | tf_op jit(solution)/shard_map/reduce_scatter | solution.py:363
  141.2 15.5 %collective-permute-start.27 = (bf16[3,72,1024]{2,1,0:T(8,128)(2,1)}, bf16[3,72,1024]{2,1,0:T(8,128)(2,1)}, u32[]{:S(2)}, u32[]{:S(2)}) collective-permute-start(bf16[3,72,1024]{2,1,0:T(8,128)(2,1)} %get-tuple-element.158), channel_id=1, source_target_pairs={{0,2},{2,0},{4,6},{6,4},{8,10},{10,8},{12,14},{14,12},{16,18},{18,... | collective-permute-start | bytes 1327112 | tf_op jit(solution)/shard_map/ppermute | solution.py:268
  143.0 13.7 %collective-permute-start.28 = (bf16[3,72,1024]{2,1,0:T(8,128)(2,1)}, bf16[3,72,1024]{2,1,0:T(8,128)(2,1)}, u32[]{:S(2)}, u32[]{:S(2)}) collective-permute-start(bf16[3,72,1024]{2,1,0:T(8,128)(2,1)} %get-tuple-element.159), channel_id=1, source_target_pairs={{0,4},{2,6},{4,0},{6,2},{8,12},{10,14},{12,8},{14,10},{16,20},{18,... | collective-permute-start | bytes 1327112 | tf_op jit(solution)/shard_map/ppermute | solution.py:268
  143.3 16.1 %collective-permute-start.29 = (bf16[3,72,1024]{2,1,0:T(8,128)(2,1)S(1)}, bf16[3,72,1024]{2,1,0:T(8,128)(2,1)}, u32[]{:S(2)}, u32[]{:S(2)}) collective-permute-start(bf16[3,72,1024]{2,1,0:T(8,128)(2,1)S(1)} %get-tuple-element.160), channel_id=1, source_target_pairs={{0,6},{2,4},{4,2},{6,0},{8,14},{10,12},{12,10},{14,8},{16,22},{18,... | collective-permute-start | bytes 1327112 | tf_op jit(solution)/shard_map/ppermute | solution.py:268
  159.4 21.4 %collective-permute-start.32 = (bf16[3,72,1024]{2,1,0:T(8,128)(2,1)S(1)}, bf16[3,72,1024]{2,1,0:T(8,128)(2,1)S(1)}, u32[]{:S(2)}, u32[]{:S(2)}) collective-permute-start(bf16[3,72,1024]{2,1,0:T(8,128)(2,1)S(1)} %get-tuple-element.172), channel_id=1, source_target_pairs={{0,6},{2,4},{4,2},{6,0},{8,14},{10,12},{12,10},{14,8},{16,22},{18,... | collective-permute-start | bytes 1327112 | tf_op jit(solution)/shard_map/ppermute | solution.py:268
  162.6 18.2 %collective-permute-start.31 = (bf16[3,72,1024]{2,1,0:T(8,128)(2,1)S(1)}, bf16[3,72,1024]{2,1,0:T(8,128)(2,1)S(1)}, u32[]{:S(2)}, u32[]{:S(2)}) collective-permute-start(bf16[3,72,1024]{2,1,0:T(8,128)(2,1)S(1)} %get-tuple-element.170), channel_id=1, source_target_pairs={{0,4},{2,6},{4,0},{6,2},{8,12},{10,14},{12,8},{14,10},{16,20},{18,... | collective-permute-start | bytes 1327112 | tf_op jit(solution)/shard_map/ppermute | solution.py:268
  162.6 18.2 %collective-permute-start.30 = (bf16[3,72,1024]{2,1,0:T(8,128)(2,1)S(1)}, bf16[3,72,1024]{2,1,0:T(8,128)(2,1)S(1)}, u32[]{:S(2)}, u32[]{:S(2)}) collective-permute-start(bf16[3,72,1024]{2,1,0:T(8,128)(2,1)S(1)} %get-tuple-element.168), channel_id=1, source_target_pairs={{0,2},{2,0},{4,6},{6,4},{8,10},{10,8},{12,14},{14,12},{16,18},{18,... | collective-permute-start | bytes 1327112 | tf_op jit(solution)/shard_map/ppermute | solution.py:268
  169.0 18.9 %collective-permute-start.34 = (bf16[512,768]{1,0:T(8,128)(2,1)S(1)}, bf16[512,768]{1,0:T(8,128)(2,1)S(1)}, u32[]{:S(2)}, u32[]{:S(2)}) collective-permute-start(bf16[512,768]{1,0:T(8,128)(2,1)S(1)} %fusion.1), channel_id=1, source_target_pairs={{0,1},{1,0},{2,3},{3,2},{4,5},{5,4},{6,7},{7,6},{8,9},{9,8},{10,11... | collective-permute-start | bytes 2359304 | tf_op jit(solution)/shard_map/ppermute | solution.py:271
  182.1 8.7 %collective-permute-start.33 = (bf16[512,768]{1,0:T(8,128)(2,1)S(1)}, bf16[512,768]{1,0:T(8,128)(2,1)S(1)}, u32[]{:S(2)}, u32[]{:S(2)}) collective-permute-start(bf16[512,768]{1,0:T(8,128)(2,1)S(1)} %fusion.4), channel_id=1, source_target_pairs={{0,1},{1,0},{2,3},{3,2},{4,5},{5,4},{6,7},{7,6},{8,9},{9,8},{10,11... | collective-permute-start | bytes 2359304 | tf_op jit(solution)/shard_map/ppermute | solution.py:271
  (49 other events, 171.2 us)
Sparse Core Ops, SparseCore 0:
  10.2 28.8 all-gather.6
  40.6 27.4 all-gather.8
  69.6 43.8 all-gather.10
  129.1 29.5 reduce-scatter.2
  160.9 25.7 reduce-scatter.4
